TPU v7x, 128 devices: a whole 4x4x4 slice. The times are simulated.
128 devices in a mesh: seq: 32 (over y, x, core), row: 4 (over z).
Axes of the slice: x: 4, y: 4, z: 4, core: 2. Of those that a mesh axis runs over, the one named last changes fastest.
Arguments:
- events: bfloat16 [8, 4096, 512], P('row', 'seq'), may hold values from -6 to 6
- grad_out: bfloat16 [8, 4096, 512], P('row', 'seq'), may hold values from -6 to 6
- w_inner: bfloat16 [512, 2048], replicated, may hold values from -0.25 to 0.25
- w_outer: bfloat16 [512, 512], replicated, may hold values from -0.25 to 0.25
- valid_lengths: int32 [8], P('row'), may hold values from 1024 to 4096, as said below
- item_ids: int32 [8, 4096], P('row', 'seq'), may hold values from 0 to 131071, as said below
Outputs:
- table_grad: float32 [131072, 512], P(('seq', 'row'))
Inputs may be any that keep to these rules, and one draw needn't show every extreme that they name: `valid_lengths`: each sequence's valid events are its first ones; some sequence is full. `item_ids`: table row r lies in block r // 1024; block o belongs to device o of seq and row taken together, seq slowest. Of the events of one device, at most 4 have items in one block, and on every device some block gets exactly 4.
All inputs are finite; a program needn't handle non-finite values.
Results may differ from a plain program's by a relative error of at most 0.0047.
Values may be sent and summed in bfloat16 or wider, within the bound.
No kernel may reach another device: no remote copies, remote signals or barrier semaphores. Data moves between devices by JAX's collectives and lax.ppermute only.
A program may use at most 192 MiB of HBM per device.

v0:
```python
import jax
import jax.numpy as jnp
from jax import lax
from jax.sharding import PartitionSpec as P

HEADS = 4
ROWS_DEV = 1024


def normalize(values):
    center = values - jnp.mean(values, axis=-1, keepdims=True)
    inverse = lax.rsqrt(jnp.mean(center * center, axis=-1, keepdims=True) + 1e-05)
    return (center * inverse, inverse)


def norm_back(upstream, normed, inverse):
    return inverse * (
        upstream
        - jnp.mean(upstream, axis=-1, keepdims=True)
        - normed * jnp.mean(upstream * normed, axis=-1, keepdims=True)
    )


def silu_slope(values):
    sigma = jax.nn.sigmoid(values)
    return sigma * (1.0 + values * (1.0 - sigma))


def local(events, grad_out, w_inner, w_outer, valid_lengths, item_ids):
    groups, local_len, model_width = events.shape
    seq_count = lax.axis_size("seq")
    row_count = lax.axis_size("row")
    owner_count = seq_count * row_count
    slot_cap = max(2, 2 * groups * local_len // owner_count)
    total_len = local_len * seq_count
    head_dim = model_width // HEADS
    score_scale = head_dim ** (-0.5)
    first_pos = lax.axis_index("seq") * local_len
    normed, norm_inv = normalize(events.astype(jnp.float32))
    pre_act = jnp.einsum(
        "gtd,de->gte", normed.astype(jnp.bfloat16), w_inner, preferred_element_type=jnp.float32
    )
    activated = jax.nn.silu(pre_act).astype(jnp.bfloat16)
    u_part = activated[..., :model_width]
    v_part = activated[..., model_width : 2 * model_width]
    q_part = activated[..., 2 * model_width : 3 * model_width]
    k_part = activated[..., 3 * model_width :]
    keys_all, values_all = (
        lax.all_gather(k_part, "seq", axis=1, tiled=True),
        lax.all_gather(v_part, "seq", axis=1, tiled=True),
    )
    query_pos = first_pos + jnp.arange(local_len, dtype=jnp.int32)
    key_pos = jnp.arange(total_len, dtype=jnp.int32)
    inv_len = 1.0 / valid_lengths.astype(jnp.float32)
    causal_mask = (key_pos[None, None, :] <= query_pos[None, :, None]) & (
        query_pos[None, :, None] < valid_lengths[:, None, None]
    )
    pair_weight = jnp.where(causal_mask, inv_len[:, None, None], 0.0)

    def head_scores(head_cols):
        return score_scale * jnp.einsum(
            "gid,gjd->gij",
            q_part[..., head_cols],
            keys_all[..., head_cols],
            preferred_element_type=jnp.float32,
        )

    outputs = []
    for head_index in range(HEADS):
        head_cols = slice(head_index * head_dim, (head_index + 1) * head_dim)
        attn_weights = (jax.nn.silu(head_scores(head_cols)) * pair_weight).astype(jnp.bfloat16)
        outputs.append(
            jnp.einsum(
                "gij,gjd->gid",
                attn_weights,
                values_all[..., head_cols],
                preferred_element_type=jnp.float32,
            )
        )
    normed_out, out_inv = normalize(jnp.concatenate(outputs, axis=-1))
    grad_gated = jnp.einsum("gte,de->gtd", grad_out, w_outer, preferred_element_type=jnp.float32)
    grad_upart = grad_gated * normed_out
    grad_attn = norm_back(grad_gated * u_part.astype(jnp.float32), normed_out, out_inv).astype(
        jnp.bfloat16
    )
    grad_query = []
    for head_index in range(HEADS):
        head_cols = slice(head_index * head_dim, (head_index + 1) * head_dim)
        score_block = head_scores(head_cols)
        attn_weights = (jax.nn.silu(score_block) * pair_weight).astype(jnp.bfloat16)
        grad_weights = jnp.einsum(
            "gid,gjd->gij",
            grad_attn[..., head_cols],
            values_all[..., head_cols],
            preferred_element_type=jnp.float32,
        )
        grad_score = (grad_weights * pair_weight * silu_slope(score_block)).astype(jnp.bfloat16)
        grad_query.append(
            score_scale
            * jnp.einsum(
                "gij,gjd->gid",
                grad_score,
                keys_all[..., head_cols],
                preferred_element_type=jnp.float32,
            )
        )
    queries_all, grads_all = (
        lax.all_gather(q_part, "seq", axis=1, tiled=True),
        lax.all_gather(grad_attn, "seq", axis=1, tiled=True),
    )
    own_mask = (query_pos[None, None, :] <= key_pos[None, :, None]) & (
        key_pos[None, :, None] < valid_lengths[:, None, None]
    )
    own_weight = jnp.where(own_mask, inv_len[:, None, None], 0.0)
    key_list = []
    value_list = []
    for head_index in range(HEADS):
        head_cols = slice(head_index * head_dim, (head_index + 1) * head_dim)
        score_block = score_scale * jnp.einsum(
            "gid,gjd->gij",
            queries_all[..., head_cols],
            k_part[..., head_cols],
            preferred_element_type=jnp.float32,
        )
        attn_weights = (jax.nn.silu(score_block) * own_weight).astype(jnp.bfloat16)
        grad_weights = jnp.einsum(
            "gid,gjd->gij",
            grads_all[..., head_cols],
            v_part[..., head_cols],
            preferred_element_type=jnp.float32,
        )
        grad_score = (grad_weights * own_weight * silu_slope(score_block)).astype(jnp.bfloat16)
        key_list.append(
            score_scale
            * jnp.einsum(
                "gij,gid->gjd",
                grad_score,
                queries_all[..., head_cols],
                preferred_element_type=jnp.float32,
            )
        )
        value_list.append(
            jnp.einsum(
                "gij,gid->gjd",
                attn_weights,
                grads_all[..., head_cols],
                preferred_element_type=jnp.float32,
            )
        )
    grad_key = jnp.concatenate(key_list, axis=-1)
    grad_value = jnp.concatenate(value_list, axis=-1)
    grad_joined = jnp.concatenate([grad_upart, grad_value] + grad_query + [grad_key], axis=-1)
    grad_pre = (grad_joined * silu_slope(pre_act)).astype(jnp.bfloat16)
    grad_normed = jnp.einsum("gte,de->gtd", grad_pre, w_inner, preferred_element_type=jnp.float32)
    grad_events = grad_out.astype(jnp.float32) + norm_back(grad_normed, normed, norm_inv)
    flat_grads = grad_events.reshape(groups * local_len, model_width)
    flat_ids = item_ids.reshape(-1)
    is_valid = (query_pos[None, :] < valid_lengths[:, None]).reshape(-1)
    owner_block = flat_ids // ROWS_DEV
    row_within = flat_ids - owner_block * ROWS_DEV
    owner_hits = (
        (owner_block[:, None] == jnp.arange(owner_count, dtype=jnp.int32)[None, :])
        & is_valid[:, None]
    ).astype(jnp.int32)
    slot_rank = jnp.sum(jnp.cumsum(owner_hits, axis=0) * owner_hits, axis=1) - 1
    slot_index = jnp.where(is_valid, owner_block * slot_cap + slot_rank, owner_count * slot_cap)
    send_rows = (
        jnp.zeros((owner_count * slot_cap, model_width), jnp.float32)
        .at[slot_index]
        .set(flat_grads, mode="drop")
    )
    send_ids = (
        jnp.full((owner_count * slot_cap,), ROWS_DEV, jnp.int32)
        .at[slot_index]
        .set(row_within, mode="drop")
    )
    got_rows, got_ids = (
        lax.all_to_all(
            send_rows.reshape(owner_count, slot_cap, model_width),
            ("seq", "row"),
            split_axis=0,
            concat_axis=0,
            tiled=True,
        ),
        lax.all_to_all(
            send_ids.reshape(owner_count, slot_cap),
            ("seq", "row"),
            split_axis=0,
            concat_axis=0,
            tiled=True,
        ),
    )
    table_grad = jnp.zeros((ROWS_DEV, model_width), jnp.float32)
    return table_grad.at[got_ids.reshape(-1)].add(got_rows.reshape(-1, model_width), mode="drop")


def solution(mesh):
    return jax.shard_map(
        local,
        mesh=mesh,
        in_specs=(
            P("row", "seq", None),
            P("row", "seq", None),
            P(),
            P(),
            P("row"),
            P("row", "seq"),
        ),
        out_specs=P(("seq", "row"), None),
        check_vma=False,
    )
```

profile of v0, /device:TPU:1, one launch (start us, length us, event | category | flops | bytes accessed | tf_op | source)
XLA Modules:
  0.0 356.9 jit_solution(10724598347083516744)
XLA Ops:
  6.5 1.2 convert_reduce_fusion
  7.8 1.2 fusion.179
  9.0 3.1 multiply_convert_fusion.1
  14.7 1.2 iota_compare_fusion.1
  15.8 53.8 %all-gather.5.cloned.1.call-done = bf16[2,4096,512]{2,1,0:T(8,128)(2,1)} async-done(((bf16[2,128,512]{2,1,0:T(8,128)(2,1)}), bf16[2,4096,512]{2,1,0:T(8,128)(2,1)}) %all-gather.5.cloned.1.call-update) | async-done | bytes 8388624 | tf_op jit(solution)/shard_map/all_gather | solution.py:49
  69.6 4.3 %convolution_multiply_fusion.7 = f32[2,128,4096]{2,1,0:T(8,128)} fusion(bf16[2,4096,512]{2,1,0:T(8,128)(2,1)} %all-gather.5.cloned.1.call-done, bf16[2,128,2048]{2,1,0:T(8,128)(2,1)S(1)} %get-tuple-element.16), kind=kOutput, calls=%fused_computation.26 | convolution fusion | flops 269484032 | bytes 6356992 | tf_op jit(solution)/shard_map/gid,gjd->gij/dot_general | solution.py:61
  74.0 50.5 %all-gather.7.cloned.1.call-done = bf16[2,4096,512]{2,1,0:T(8,128)(2,1)} async-done(((bf16[2,128,512]{2,1,0:T(8,128)(2,1)}), bf16[2,4096,512]{2,1,0:T(8,128)(2,1)}) %all-gather.7.cloned.1.call-update) | async-done | bytes 8388624 | tf_op jit(solution)/shard_map/all_gather | solution.py:50
  124.4 5.0 %fusion.257 = (f32[2,128]{1,0:T(2,128)S(1)}, f32[2,128,128]{1,2,0:T(8,128)S(1)}) fusion(bf16[2,4096,512]{2,1,0:T(8,128)(2,1)} %all-gather.7.cloned.1.call-done, f32[2,128,4096]{2,1,0:T(8,128)} %convolution_multiply_fusion.7, f32[2]{0:T(128)S(1)} %convert_divide_fusion, pred[2,128]{1,0:T(4,128)(4,1)S(1)} %broadcast_compare_fusion, ...), kind=kOutput, calls=%fused_computation.259 | convolution fusion | flops 276856576 | bytes 6948104 | tf_op jit(solution)/shard_map/gij,gjd->gid/dot_general | solution.py:73
  129.6 2.4 convolution_multiply_fusion.6
  132.0 4.5 %fusion.258 = (f32[2,128]{1,0:T(2,128)S(1)}, f32[2,128,128]{1,2,0:T(8,128)S(1)}) fusion(bf16[2,4096,512]{2,1,0:T(8,128)(2,1)} %all-gather.7.cloned.1.call-done, f32[2,128,4096]{2,1,0:T(8,128)S(1)} %convolution_multiply_fusion.6, f32[2]{0:T(128)S(1)} %copy-done.25, pred[2,128]{1,0:T(4,128)(4,1)S(1)} %broadcast_compare_fusion, ...), kind=kOutput, calls=%fused_computation.260 | convolution fusion | flops 276856576 | bytes 6948104 | tf_op jit(solution)/shard_map/gij,gjd->gid/dot_general | solution.py:73
  136.6 2.4 convolution_multiply_fusion.5
  139.0 6.4 %fusion.256 = (f32[2,128]{1,0:T(2,128)}, f32[2,128,128]{1,2,0:T(8,128)}) fusion(bf16[2,4096,512]{2,1,0:T(8,128)(2,1)} %all-gather.7.cloned.1.call-done, f32[2,128,4096]{2,1,0:T(8,128)S(1)} %convolution_multiply_fusion.5, f32[2]{0:T(128)} %copy-done.24, pred[2,128]{1,0:T(4,128)(4,1)S(1)} %broadcast_compare_fusion, pred[128,4096]{1,0:T(8,128)(4,1)S(1)} %copy-done.11), kind=kOutput, calls=%fused_computation.258 | convolution fusion | flops 276856576 | bytes 6948608 | tf_op jit(solution)/shard_map/gij,gjd->gid/dot_general | solution.py:73
  145.5 1.0 copy.38
  146.5 2.4 convolution_multiply_fusion.4
  148.9 6.4 %fusion.255 = (f32[2,128]{1,0:T(2,128)}, f32[2,128,128]{1,2,0:T(8,128)}) fusion(bf16[2,4096,512]{2,1,0:T(8,128)(2,1)} %all-gather.7.cloned.1.call-done, f32[2,128,4096]{2,1,0:T(8,128)S(1)} %convolution_multiply_fusion.4, f32[2]{0:T(128)} %copy-done.24, pred[2,128]{1,0:T(4,128)(4,1)S(1)} %broadcast_compare_fusion, pred[128,4096]{1,0:T(8,128)(4,1)S(1)} %copy-done.12), kind=kOutput, calls=%fused_computation.257 | convolution fusion | flops 276856576 | bytes 6948608 | tf_op jit(solution)/shard_map/gij,gjd->gid/dot_general | solution.py:73
  155.3 1.7 copy.39
  157.7 1.1 multiply_reduce_fusion.1
  158.8 1.6 fusion.187
  160.4 2.0 multiply_convert_fusion.3
  164.9 1.4 scatter_custom_fusion
  167.1 7.8 %all-to-all-start = ((s32[128,1,4]{2,1,0:T(1,128)}), s32[128,1,4]{2,1,0:T(1,128)S(1)}, u32[]{:S(2)}, u32[]{:S(2)}) async-start(s32[128,1,4]{2,1,0:T(1,128)} %bitcast.8), calls=%async_computation | async-start | bytes 131072 | tf_op jit(solution)/shard_map/all_to_all | solution.py:185
  175.6 1.1 iota_compare_fusion
  176.8 2.5 all-gather.9.cloned.1.call-done
  179.2 4.5 %convolution_multiply_fusion.3 = f32[2,4096,128]{2,1,0:T(8,128)} fusion(bf16[2,4096,512]{2,1,0:T(8,128)(2,1)} %all-gather.9.cloned.1.call-done, bf16[2,128,2048]{2,1,0:T(8,128)(2,1)S(1)} %get-tuple-element.16), kind=kOutput, calls=%fused_computation.22 | convolution fusion | flops 269484032 | bytes 6356992 | tf_op jit(solution)/shard_map/gid,gjd->gij/dot_general | solution.py:119
  183.8 4.2 %convolution_multiply_fusion.2 = f32[2,4096,128]{2,1,0:T(8,128)} fusion(bf16[2,4096,512]{2,1,0:T(8,128)(2,1)} %all-gather.9.cloned.1.call-done, bf16[2,128,2048]{2,1,0:T(8,128)(2,1)S(1)} %get-tuple-element.16), kind=kOutput, calls=%fused_computation.21 | convolution fusion | flops 269484032 | bytes 6356992 | tf_op jit(solution)/shard_map/gid,gjd->gij/dot_general | solution.py:119
  188.0 2.7 convolution_multiply_fusion.1
  190.7 2.6 convolution_multiply_fusion
  193.3 40.6 %all-gather.11.cloned.1.call-done = bf16[2,4096,512]{2,1,0:T(8,128)(2,1)} async-done(((bf16[2,128,512]{2,1,0:T(8,128)(2,1)}), bf16[2,4096,512]{2,1,0:T(8,128)(2,1)}) %all-gather.11.cloned.1.call-update) | async-done | bytes 8388624 | tf_op jit(solution)/shard_map/all_gather | solution.py:109
  233.9 8.0 %fusion.84 = f32[2,128,2048]{2,1,0:T(8,128)} fusion(f32[2,128,2048]{2,1,0:T(8,128)} %get-tuple-element.12, bf16[2,4096,512]{2,1,0:T(8,128)(2,1)} %all-gather.11.cloned.1.call-done, f32[2,4096,128]{2,1,0:T(8,128)} %convolution_multiply_fusion.3, f32[2]{0:T(128)S(1)} %copy-done.26, pred[2,4096]{1,0:T(4,128)(4,1)S(1)} %iota_compare_fusion.3, ...), kind=kOutput, calls=%fused_computation.116 | convolution fusion | flops 276824064 | bytes 6955016 | tf_op jit(solution)/shard_map/gij,gid->gjd/dot_general | solution.py:143
  242.0 3.3 fusion.89
  245.3 3.2 fusion.94
  248.5 3.3 fusion.99
  251.8 7.1 %fusion.107 = f32[2,128,2048]{2,1,0:T(8,128)} fusion(f32[2,128,2048]{2,1,0:T(8,128)} %fusion.99, bf16[2,4096,512]{2,1,0:T(8,128)(2,1)} %all-gather.5.cloned.1.call-done, f32[2,128,4096]{2,1,0:T(8,128)} %convolution_multiply_fusion.7, f32[2]{0:T(128)S(1)} %copy-done.26, pred[2,128]{1,0:T(4,128)(4,1)S(1)} %copy-done.22, ...), kind=kOutput, calls=%fused_computation.121 | convolution fusion | flops 549486592 | bytes 9110528 | tf_op jit(solution)/shard_map/gij,gjd->gid/dot_general | solution.py:100
  258.8 7.2 %fusion.113 = f32[2,128,2048]{2,1,0:T(8,128)} fusion(f32[2,128,2048]{2,1,0:T(8,128)} %fusion.107, bf16[2,4096,512]{2,1,0:T(8,128)(2,1)} %all-gather.5.cloned.1.call-done, f32[2,128,4096]{2,1,0:T(8,128)} %copy-done.2, f32[2]{0:T(128)S(1)} %copy-done.26, pred[2,128]{1,0:T(4,128)(4,1)S(1)} %copy-done.22, pred[128,4096]{1,0:T(8,128)(4,1)} %iota_compare_fusion.1, ...), kind=kOutput, calls=%fused_computation.123 | convolution fusion | flops 549486592 | bytes 9110528 | tf_op jit(solution)/shard_map/gij,gjd->gid/dot_general | solution.py:100
  266.1 7.1 %fusion.119 = f32[2,128,2048]{2,1,0:T(8,128)} fusion(f32[2,128,2048]{2,1,0:T(8,128)} %fusion.113, bf16[2,4096,512]{2,1,0:T(8,128)(2,1)} %all-gather.5.cloned.1.call-done, f32[2,128,4096]{2,1,0:T(8,128)} %copy-done.4, f32[2]{0:T(128)S(1)} %copy-done.26, pred[2,128]{1,0:T(4,128)(4,1)S(1)} %copy-done.22, pred[128,4096]{1,0:T(8,128)(4,1)} %iota_compare_fusion.1, ...), kind=kOutput, calls=%fused_computation.125 | convolution fusion | flops 549486592 | bytes 9110528 | tf_op jit(solution)/shard_map/gij,gjd->gid/dot_general | solution.py:100
  273.1 7.0 %fusion.125 = f32[2,128,2048]{2,1,0:T(8,128)} fusion(f32[2,128,2048]{2,1,0:T(8,128)} %fusion.119, bf16[2,4096,512]{2,1,0:T(8,128)(2,1)} %all-gather.5.cloned.1.call-done, f32[2,128,4096]{2,1,0:T(8,128)} %copy-done.3, f32[2]{0:T(128)S(1)} %copy-done.26, pred[2,128]{1,0:T(4,128)(4,1)S(1)} %copy-done.22, pred[128,4096]{1,0:T(8,128)(4,1)} %iota_compare_fusion.1, ...), kind=kOutput, calls=%fused_computation.127 | convolution fusion | flops 549486592 | bytes 9110528 | tf_op jit(solution)/shard_map/gij,gjd->gid/dot_general | solution.py:100
  280.2 7.0 %fusion.131 = f32[2,128,2048]{2,1,0:T(8,128)} fusion(f32[2,128,2048]{2,1,0:T(8,128)} %fusion.125, bf16[2,4096,512]{2,1,0:T(8,128)(2,1)} %all-gather.9.cloned.1.call-done, f32[2,4096,128]{2,1,0:T(8,128)} %convolution_multiply_fusion.3, f32[2]{0:T(128)S(1)} %copy-done.26, pred[2,4096]{1,0:T(4,128)(4,1)S(1)} %iota_compare_fusion.3, ...), kind=kOutput, calls=%fused_computation.129 | convolution fusion | flops 549486592 | bytes 9126400 | tf_op jit(solution)/shard_map/gij,gid->gjd/dot_general | solution.py:135
  287.2 6.9 %fusion.137 = f32[2,128,2048]{2,1,0:T(8,128)} fusion(f32[2,128,2048]{2,1,0:T(8,128)} %fusion.131, bf16[2,4096,512]{2,1,0:T(8,128)(2,1)} %all-gather.9.cloned.1.call-done, f32[2,4096,128]{2,1,0:T(8,128)} %convolution_multiply_fusion.2, f32[2]{0:T(128)S(1)} %copy-done.26, pred[2,4096]{1,0:T(4,128)(4,1)S(1)} %iota_compare_fusion.3, ...), kind=kOutput, calls=%fused_computation.131 | convolution fusion | flops 549486592 | bytes 9126400 | tf_op jit(solution)/shard_map/gij,gid->gjd/dot_general | solution.py:135
  294.1 7.2 %fusion.143 = f32[2,128,2048]{2,1,0:T(8,128)} fusion(f32[2,128,2048]{2,1,0:T(8,128)} %fusion.137, bf16[2,4096,512]{2,1,0:T(8,128)(2,1)} %all-gather.9.cloned.1.call-done, f32[2,4096,128]{2,1,0:T(8,128)} %convolution_multiply_fusion.1, f32[2]{0:T(128)S(1)} %copy-done.26, pred[2,4096]{1,0:T(4,128)(4,1)S(1)} %iota_compare_fusion.3, ...), kind=kOutput, calls=%fused_computation.133 | convolution fusion | flops 549486592 | bytes 9126400 | tf_op jit(solution)/shard_map/gij,gid->gjd/dot_general | solution.py:135
  301.3 7.0 %fusion.149 = f32[2,128,2048]{2,1,0:T(8,128)} fusion(f32[2,128,2048]{2,1,0:T(8,128)} %fusion.143, bf16[2,4096,512]{2,1,0:T(8,128)(2,1)} %all-gather.9.cloned.1.call-done, f32[2,4096,128]{2,1,0:T(8,128)} %convolution_multiply_fusion, f32[2]{0:T(128)S(1)} %copy-done.26, pred[2,4096]{1,0:T(4,128)(4,1)S(1)} %iota_compare_fusion.3, ...), kind=kOutput, calls=%fused_computation.135 | convolution fusion | flops 549486592 | bytes 9126400 | tf_op jit(solution)/shard_map/gij,gid->gjd/dot_general | solution.py:135
  308.3 3.4 fusion.253
  311.7 1.1 fusion.178
  312.8 2.2 scatter_custom_fusion.1
  314.9 1.3 reshape.368
  316.2 7.5 %all-to-all-start.1 = ((f32[128,4,512]{2,1,0:T(4,128)}), f32[128,4,512]{2,1,0:T(4,128)S(1)}, u32[]{:S(2)}, u32[]{:S(2)}) async-start(f32[128,4,512]{2,1,0:T(4,128)} %reshape.368), calls=%async_computation.1 | async-start | bytes 2097152 | tf_op jit(solution)/shard_map/all_to_all | solution.py:178
  325.2 17.9 %all-to-all-done.1 = f32[128,4,512]{2,1,0:T(4,128)S(1)} async-done(((f32[128,4,512]{2,1,0:T(4,128)}), f32[128,4,512]{2,1,0:T(4,128)S(1)}, u32[]{:S(2)}, u32[]{:S(2)}) %all-to-all-start.1) | async-done | bytes 1048608 | tf_op jit(solution)/shard_map/all_to_all | solution.py:178
  343.1 1.3 reshape.390
  344.5 5.6 %scatter_custom_fusion.2 = f32[1024,512]{1,0:T(8,128)} fusion(s32[512]{0:T(512)S(1)} %bitcast.58, f32[512,512]{1,0:T(8,128)} %reshape.390, f32[]{:T(128)} %constant.62.clone.1), kind=kCustom, calls=%fused_computation.136 | custom fusion | flops 262144 | bytes 2097664 | tf_op jit(solution)/shard_map/scatter-add | solution.py:194
  (98 shorter events, 8.9 us)
Async XLA Ops:
  6.5 2.4 copy-start
  6.5 63.1 %all-gather.5.cloned.1.call-start = ((), (), s32[]{:S(2)}) async-start(), calls=%async_computation.2 | async-start | bytes 8650752 | tf_op jit(solution)/shard_map/all_gather | solution.py:49
  7.8 4.3 %copy-start.15 = (f32[2,128]{1,0:T(2,128)}, f32[2,128]{1,0:T(2,128)S(1)}, u32[]{:S(2)}) copy-start(f32[2,128]{1,0:T(2,128)S(1)} %broadcast_multiply_fusion.4) | copy-start | bytes 3076
  9.0 3.1 copy-start.18
  9.0 5.6 %copy-start.20 = (s32[2]{0:T(128)S(1)}, s32[2]{0:T(128)}, u32[]{:S(2)}) copy-start(s32[2]{0:T(128)} %param.10) | copy-start | bytes 28
  13.0 111.4 %all-gather.7.cloned.1.call-start = ((), (), s32[]{:S(2)}) async-start(), calls=%async_computation.3 | async-start | bytes 8650752 | tf_op jit(solution)/shard_map/all_gather | solution.py:50
  13.8 165.5 %all-gather.9.cloned.1.call-start = ((), (), s32[]{:S(2)}) async-start(), calls=%async_computation.4 | async-start | bytes 8650752 | tf_op jit(solution)/shard_map/all_gather | solution.py:108
  14.5 219.4 %all-gather.11.cloned.1.call-start = ((), (), s32[]{:S(2)}) async-start(), calls=%async_computation.5 | async-start | bytes 8650752 | tf_op jit(solution)/shard_map/all_gather | solution.py:109
  14.6 114.9 %copy-start.24 = (f32[2]{0:T(128)}, f32[2]{0:T(128)S(1)}, u32[]{:S(2)}) copy-start(f32[2]{0:T(128)S(1)} %convert_divide_fusion) | copy-start | bytes 28
  14.7 134.2 %copy-start.21 = (pred[2,128]{1,0:T(4,128)(4,1)}, pred[2,128]{1,0:T(4,128)(4,1)S(1)}, u32[]{:S(2)}) copy-start(pred[2,128]{1,0:T(4,128)(4,1)S(1)} %broadcast_compare_fusion) | copy-start | bytes 772
  129.6 2.4 copy-start.10
  129.6 2.4 copy-start.25
  132.0 4.5 %copy-start.2 = (f32[2,128,4096]{2,1,0:T(8,128)}, f32[2,128,4096]{2,1,0:T(8,128)S(1)}, u32[]{:S(2)}) copy-start(f32[2,128,4096]{2,1,0:T(8,128)S(1)} %convolution_multiply_fusion.6) | copy-start | bytes 12582916
  136.6 2.4 copy-start.11
  139.0 6.5 %copy-start.4 = (f32[2,128,4096]{2,1,0:T(8,128)}, f32[2,128,4096]{2,1,0:T(8,128)S(1)}, u32[]{:S(2)}) copy-start(f32[2,128,4096]{2,1,0:T(8,128)S(1)} %convolution_multiply_fusion.5) | copy-start | bytes 12582916
  146.5 2.4 copy-start.12
  148.9 6.5 %copy-start.3 = (f32[2,128,4096]{2,1,0:T(8,128)}, f32[2,128,4096]{2,1,0:T(8,128)S(1)}, u32[]{:S(2)}) copy-start(f32[2,128,4096]{2,1,0:T(8,128)S(1)} %convolution_multiply_fusion.4) | copy-start | bytes 12582916
  155.3 7.3 %copy-start.17 = (s32[2,128]{1,0:T(2,128)S(1)}, s32[2,128]{1,0:T(2,128)}, u32[]{:S(2)}) copy-start(s32[2,128]{1,0:T(2,128)} %param.11) | copy-start | bytes 3076
  157.7 4.8 %copy-start.22 = (pred[2,128]{1,0:T(4,128)(4,1)S(1)}, pred[2,128]{1,0:T(4,128)(4,1)}, u32[]{:S(2)}) copy-start(pred[2,128]{1,0:T(4,128)(4,1)} %copy-done.21) | copy-start | bytes 772
  167.1 149.1 %all-to-all-start = ((s32[128,1,4]{2,1,0:T(1,128)}), s32[128,1,4]{2,1,0:T(1,128)S(1)}, u32[]{:S(2)}, u32[]{:S(2)}) async-start(s32[128,1,4]{2,1,0:T(1,128)} %bitcast.8), calls=%async_computation | async-start | bytes 131072 | tf_op jit(solution)/shard_map/all_to_all | solution.py:185
  179.2 8.8 %copy-start.1 = (bf16[2,4096,512]{2,1,0:T(8,128)(2,1)S(1)}, bf16[2,4096,512]{2,1,0:T(8,128)(2,1)}, u32[]{:S(2)}) copy-start(bf16[2,4096,512]{2,1,0:T(8,128)(2,1)} %all-gather.9.cloned.1.call-done) | copy-start | bytes 25165828
  190.7 43.2 %copy-start.26 = (f32[2]{0:T(128)S(1)}, f32[2]{0:T(128)}, u32[]{:S(2)}) copy-start(f32[2]{0:T(128)} %copy-done.24) | copy-start | bytes 28
  233.9 8.1 %copy-start.7 = (f32[2,4096,128]{2,1,0:T(8,128)S(1)}, f32[2,4096,128]{2,1,0:T(8,128)}, u32[]{:S(2)}) copy-start(f32[2,4096,128]{2,1,0:T(8,128)} %convolution_multiply_fusion.2) | copy-start | bytes 12582916
  233.9 8.1 %copy-start.13 = (pred[4096,128]{1,0:T(8,128)(4,1)S(1)}, pred[4096,128]{1,0:T(8,128)(4,1)}, u32[]{:S(2)}) copy-start(pred[4096,128]{1,0:T(8,128)(4,1)} %iota_compare_fusion) | copy-start | bytes 1572868
  233.9 8.1 %copy-start.23 = (bf16[2,4096,512]{2,1,0:T(8,128)(2,1)S(1)}, bf16[2,4096,512]{2,1,0:T(8,128)(2,1)}, u32[]{:S(2)}) copy-start(bf16[2,4096,512]{2,1,0:T(8,128)(2,1)} %all-gather.11.cloned.1.call-done) | copy-start | bytes 25165828
  242.0 3.3 copy-start.6
  245.3 3.3 copy-start.5
  248.5 3.3 copy-start.9
  301.3 7.0 %copy-start.8 = (bf16[2,128,512]{2,1,0:T(8,128)(2,1)S(1)}, bf16[2,128,512]{2,1,0:T(8,128)(2,1)}, u32[]{:S(2)}) copy-start(bf16[2,128,512]{2,1,0:T(8,128)(2,1)} %param.6) | copy-start | bytes 786436
  301.3 7.0 %copy-start.16 = (f32[2,128]{1,0:T(2,128)S(1)}, f32[2,128]{1,0:T(2,128)}, u32[]{:S(2)}) copy-start(f32[2,128]{1,0:T(2,128)} %copy-done.15) | copy-start | bytes 3076
  301.3 7.0 %copy-start.19 = (f32[2,128]{1,0:T(2,128)S(1)}, f32[2,128]{1,0:T(2,128)}, u32[]{:S(2)}) copy-start(f32[2,128]{1,0:T(2,128)} %copy-done.18) | copy-start | bytes 3076
  308.3 3.4 copy-start.14
  316.2 26.9 %all-to-all-start.1 = ((f32[128,4,512]{2,1,0:T(4,128)}), f32[128,4,512]{2,1,0:T(4,128)S(1)}, u32[]{:S(2)}, u32[]{:S(2)}) async-start(f32[128,4,512]{2,1,0:T(4,128)} %reshape.368), calls=%async_computation.1 | async-start | bytes 2097152 | tf_op jit(solution)/shard_map/all_to_all | solution.py:178
Sparse Core Ops, SparseCore 0:
  13.1 56.4 all-gather.4
  71.9 52.4 all-gather.6
  126.7 52.4 all-gather.8
  181.4 52.4 all-gather.10
where the time goes:
time: 362 us; the launch traced here: 357 us
  waiting for transfers between devices  167 us (46%)
  matrix products  130 us (36%)
  other arithmetic  19 us (5%)
  starting transfers between devices  15.4 us (4%)
  between operations  13.8 us (4%)
  local copies, waits for them, and re-layouts  11.8 us (3%)
    all_gather x1, waiting for transfers between devices, local(): lax.all_gather(k_part, 'seq', axis=1, tiled=True)  53.8 us
    all_gather x1, waiting for transfers between devices, local(): lax.all_gather(v_part, 'seq', axis=1, tiled=True)  50.5 us
    all_gather x1, waiting for transfers between devices, local(): lax.all_gather(grad_attn, 'seq', axis=1, tiled=True)  40.6 us
    dot_general x4, matrix products, local(): jnp.einsum('gij,gjd->gid', grad_score, keys_all[..., head_cols], preferre...  28.4 us
    dot_general x4, matrix products, local(): jnp.einsum('gij,gid->gjd', grad_score, queries_all[..., head_cols], prefe...  28.1 us
    dot_general x4, matrix products, local(): jnp.einsum('gij,gjd->gid', attn_weights, values_all[..., head_cols], pref...  22.4 us
    all_to_all x1, waiting for transfers between devices, local(): lax.all_to_all(send_rows.reshape(owner_count, slot_cap, model_width), ('s...  17.9 us
    dot_general x4, matrix products, local(): jnp.einsum('gij,gid->gjd', attn_weights, grads_all[..., head_cols], prefe...  17.8 us
  transfers between devices with their start and end apart: 6, of which 5 were waited for; matrix products, arithmetic and copies ran while one was open for 41% of the time, Pallas kernels for 0%

commit v1 on v0

v1 whole, which is shorter than its diff:
```python
import functools

import jax
import jax.numpy as jnp
from jax import lax
from jax.experimental import pallas as pl
from jax.experimental.pallas import tpu as pltpu
from jax.sharding import Mesh
from jax.sharding import PartitionSpec as P

HEADS = 4
ROWS_DEV = 1024
D = 512
HD = 128
BLK = 128
CAP = 4
EXT = 128
F32 = jnp.float32
BF16 = jnp.bfloat16
SCALE = HD**-0.5


def dot(a, b):
    return lax.dot_general(a, b, (((1,), (0,)), ((), ())), preferred_element_type=F32)


def dot_t(a, b):
    return lax.dot_general(a, b, (((1,), (1,)), ((), ())), preferred_element_type=F32)


def normalize(values):
    center = values - jnp.mean(values, axis=-1, keepdims=True)
    inverse = lax.rsqrt(jnp.mean(center * center, axis=-1, keepdims=True) + 1e-05)
    return center * inverse, inverse


def silu(values):
    half = 0.5 * values
    return half * jnp.tanh(half) + half


def silu_slope(values):
    half = 0.5 * values
    two_sigma = 1.0 + jnp.tanh(half)
    return 0.5 * two_sigma * (1.0 + values - half * two_sigma)


def project_kernel(events, w_inner, pre, send):
    normed = normalize(events[...].astype(F32))[0].astype(BF16)
    for part, slot in ((0, 2), (1, 0), (2, 1)):
        values = dot(normed, w_inner[:, (part + 1) * D : (part + 2) * D])
        pre[:, part * D : (part + 1) * D] = values
        act = silu(values).astype(BF16)
        for g in range(2):
            for h in range(HEADS):
                piece = act[g * BLK : (g + 1) * BLK, h * HD : (h + 1) * HD]
                for p in range(2):
                    at = ((g * HEADS + h) * 2 + p) * BLK
                    send[at : at + BLK, slot * HD : (slot + 1) * HD] = piece


def gate_kernel(events, grad_out, w_u, w_outer, ids, pre_u, gated, send_g, hot, ext):
    normed = normalize(events[...].astype(F32))[0].astype(BF16)
    values = dot(normed, w_u[...])
    pre_u[...] = values
    grad_gated = dot_t(grad_out[...], w_outer[...])
    gated[...] = grad_gated
    prod = (grad_gated * silu(values).astype(BF16).astype(F32)).astype(BF16)
    for g in range(2):
        for h in range(HEADS):
            at = (g * HEADS + h) * BLK
            send_g[at : at + BLK, :] = prod[g * BLK : (g + 1) * BLK, h * HD : (h + 1) * HD]
    count = 2 * BLK
    id_row = ids[...]
    id_cols = jnp.transpose(jnp.broadcast_to(id_row.astype(F32), (BLK, count))).astype(jnp.int32)
    owner_row = id_row // ROWS_DEV
    owner_col = id_cols[:, :1] // ROWS_DEV
    earlier = lax.broadcasted_iota(jnp.int32, (count, count), 0) < lax.broadcasted_iota(
        jnp.int32, (count, count), 1
    )
    same = jnp.where((owner_col == owner_row) & earlier, 1, 0)
    rank = jnp.sum(same, axis=0, keepdims=True)
    slot = owner_row * CAP + rank
    slots = hot.shape[0]
    hot[...] = jnp.where(
        lax.broadcasted_iota(jnp.int32, (slots, count), 0) == slot, 1.0, 0.0
    ).astype(BF16)
    within = id_cols - (id_cols // ROWS_DEV) * ROWS_DEV
    high = within // 32
    lane = lax.broadcasted_iota(jnp.int32, (count, EXT), 1)
    ext[...] = jnp.where(
        lane == 0, high + 1, jnp.where(lane == 1, within - high * 32, 0)
    ).astype(F32).astype(BF16)


def diagonal(place, core, rows_are_keys):
    row = lax.broadcasted_iota(jnp.int32, (BLK, 2 * BLK), 0) + place[2] * BLK
    lane = lax.broadcasted_iota(jnp.int32, (BLK, 2 * BLK), 1)
    col = lane + jnp.where(lane >= BLK, BLK, 0) + core * BLK
    return row <= col if rows_are_keys else col <= row


def forward_kernel(last, place, inv_len, mine, theirs, *refs):
    if last:
        before, grad, out, stats, queries = refs
    else:
        out, queries = refs
    p = place[0]
    core = place[1]
    if last:
        core = 1 - core
    for m in range(8):
        at = pl.multiple_of((2 * m + p) * BLK, BLK)
        queries[m * BLK : (m + 1) * BLK, :] = mine[pl.ds(at, BLK), :HD]
    mask = diagonal(place, core, False)
    for m in range(8):
        rows = slice(m * BLK, (m + 1) * BLK)
        q = queries[rows, :]
        total = before[rows, :] if last else jnp.zeros((BLK, HD), F32)
        for j in range(m + 1):
            keys = slice(j * 2 * BLK, (j + 1) * 2 * BLK)
            half = dot_t(q, theirs[keys, HD : 2 * HD]) * (0.5 * SCALE)
            attn = half * jnp.tanh(half) + half
            if j == m:
                attn = jnp.where(mask, attn, 0.0)
            total = total + dot(attn.astype(BF16), theirs[keys, 2 * HD :])
        if last:
            total = total * inv_len[0]
            g = grad[rows, :].astype(F32)
            mean = jnp.mean(total, axis=-1, keepdims=True)
            center = total - mean
            square = jnp.sum(center * center, axis=-1, keepdims=True)
            sum_g = jnp.sum(g, axis=-1, keepdims=True)
            sum_ga = jnp.sum(g * center, axis=-1, keepdims=True)
            lane = lax.broadcasted_iota(jnp.int32, (BLK, BLK), 1)
            packed = jnp.where(
                lane == 0, mean, jnp.where(lane == 1, square, jnp.where(lane == 2, sum_g, sum_ga))
            )
            stats[:, rows] = jnp.transpose(packed)[:8, :]
        out[rows, :] = total


def grad_attn_kernel(place, length, attn_out, grad, s0, s1, s2, s3, grad_attn, normed_out):
    parts = [s0[...], s1[...], s2[...], s3[...]]
    means = [part[0:1, :] for part in parts]
    mean = 0.25 * (means[0] + means[1] + means[2] + means[3])
    square = 0.0
    sum_g = 0.0
    sum_ga = 0.0
    for part, own in zip(parts, means):
        shift = own - mean
        square = square + part[1:2, :] + HD * (shift * shift)
        sum_g = sum_g + part[2:3, :]
        sum_ga = sum_ga + part[3:4, :] + part[2:3, :] * shift
    inverse = lax.rsqrt(square * (1.0 / D) + 1e-05)
    mean_g = sum_g * (1.0 / D)
    mean_gn = inverse * sum_ga * (1.0 / D)
    row = lax.broadcasted_iota(jnp.int32, (BLK, 1024), 0)
    packed = jnp.where(
        row == 0, mean, jnp.where(row == 1, inverse, jnp.where(row == 2, mean_g, mean_gn))
    )
    for m in range(8):
        rows = slice(m * BLK, (m + 1) * BLK)
        cols = jnp.transpose(packed[:, rows])
        inv = cols[:, 1:2]
        n = (attn_out[rows, :] - cols[:, 0:1]) * inv
        back = (grad[rows, :].astype(F32) - cols[:, 2:3] - n * cols[:, 3:4]) * inv
        pos = lax.broadcasted_iota(jnp.int32, (BLK, 1), 0) + (m * 4 + place[2]) * BLK
        grad_attn[rows, :] = jnp.where(pos < length[0], back, 0.0).astype(BF16)
        normed_out[rows, :] = n.astype(BF16)


def slopes(raw):
    half = raw * (0.5 * SCALE)
    two_sigma = 1.0 + jnp.tanh(half)
    attn = half * two_sigma
    return two_sigma * (1.0 + (half + half) - attn), attn


def grad_query_kernel(place, inv_len, mine, theirs, grad_attn, normed_out, ret):
    p = place[0]
    masks = [diagonal(place, place[1], False), diagonal(place, 1 - place[1], False)]
    for m in range(8):
        rows = slice(m * BLK, (m + 1) * BLK)
        at = pl.multiple_of((2 * m + p) * BLK, BLK)
        q = mine[pl.ds(at, BLK), :HD]
        ga = grad_attn[rows, :]
        total = jnp.zeros((BLK, HD), F32)
        for j in range(m + 1):
            keys = slice(j * 2 * BLK, (j + 1) * 2 * BLK)
            for src, mask in zip((mine, theirs), masks):
                k = src[keys, HD : 2 * HD]
                slope, _ = slopes(dot_t(q, k))
                score = slope * dot_t(ga, src[keys, 2 * HD :])
                if j == m:
                    score = jnp.where(mask, score, 0.0)
                total = total + dot(score.astype(BF16), k)
        ret[rows, :HD] = normed_out[rows, :]
        ret[rows, HD:] = (total * (0.5 * SCALE * inv_len[0])).astype(BF16)


def grad_key_kernel(place, inv_len, mine, theirs, g_own, g_p, g_c, g_pc, ret, mine_g, theirs_g):
    p = place[0]
    masks = [diagonal(place, place[1], True), diagonal(place, 1 - place[1], True)]
    for m in range(8):
        rows = slice(m * BLK, (m + 1) * BLK)
        here = pl.multiple_of((2 * m + p) * BLK, BLK)
        there = pl.multiple_of((2 * m + 1 - p) * BLK, BLK)
        mine_g[pl.ds(here, BLK), :] = g_own[rows, :]
        mine_g[pl.ds(there, BLK), :] = g_p[rows, :]
        theirs_g[pl.ds(here, BLK), :] = g_c[rows, :]
        theirs_g[pl.ds(there, BLK), :] = g_pc[rows, :]
    for m in range(8):
        rows = slice(m * BLK, (m + 1) * BLK)
        at = pl.multiple_of((2 * m + p) * BLK, BLK)
        k = mine[pl.ds(at, BLK), HD : 2 * HD]
        v = mine[pl.ds(at, BLK), 2 * HD :]
        grad_k = jnp.zeros((BLK, HD), F32)
        grad_v = jnp.zeros((BLK, HD), F32)
        for j in range(m, 8):
            events = slice(j * 2 * BLK, (j + 1) * 2 * BLK)
            for src, src_g, mask in zip((mine, theirs), (mine_g, theirs_g), masks):
                q = src[events, :HD]
                ga = src_g[events, :]
                slope, attn = slopes(dot_t(k, q))
                score = slope * dot_t(v, ga)
                if j == m:
                    score = jnp.where(mask, score, 0.0)
                    attn = jnp.where(mask, attn, 0.0)
                grad_k = grad_k + dot(score.astype(BF16), q)
                grad_v = grad_v + dot(attn.astype(BF16), ga)
        ret[rows, :HD] = (grad_k * (0.5 * SCALE * inv_len[0])).astype(BF16)
        ret[rows, HD:] = (grad_v * inv_len[0]).astype(BF16)


def finish_kernel(
    first, lengths, ret1, ret2, pre_u, pre, gated, events, grad_out, w_inner, hot, ext, send, grads
):
    for g in range(2):
        rows = slice(g * BLK, (g + 1) * BLK)
        for h in range(HEADS):
            cols = slice(h * HD, (h + 1) * HD)
            at = slice((g * HEADS + h) * BLK, (g * HEADS + h + 1) * BLK)
            pieces = (
                (gated[rows, cols] * ret1[at, :HD].astype(F32), pre_u[rows, cols]),
                (ret2[at, HD:].astype(F32), pre[rows, h * HD : (h + 1) * HD]),
                (ret1[at, HD:].astype(F32), pre[rows, D + h * HD : D + (h + 1) * HD]),
                (ret2[at, :HD].astype(F32), pre[rows, 2 * D + h * HD : 2 * D + (h + 1) * HD]),
            )
            for part, (grad, value) in enumerate(pieces):
                grads[rows, part * D + h * HD : part * D + (h + 1) * HD] = (
                    grad * silu_slope(value)
                ).astype(BF16)
    grad_normed = dot_t(grads[...], w_inner[...])
    normed, inverse = normalize(events[...].astype(F32))
    back = inverse * (
        grad_normed
        - jnp.mean(grad_normed, axis=-1, keepdims=True)
        - normed * jnp.mean(grad_normed * normed, axis=-1, keepdims=True)
    )
    total = grad_out[...].astype(F32) + back
    row = lax.broadcasted_iota(jnp.int32, (2 * BLK, 1), 0)
    second = row >= BLK
    pos = first[0] + jnp.where(second, row - BLK, row)
    total = jnp.where(pos < jnp.where(second, lengths[1], lengths[0]), total, 0.0)
    send[:, :D] = dot(hot[...], total.astype(BF16)).astype(BF16)
    send[:, D:] = dot(hot[...], ext[...]).astype(BF16)


def table_kernel(got, table):
    rows = table.shape[0]
    packed = jnp.transpose(got[:, D:].astype(F32))
    dest = ((packed[0:1, :] - 1.0) * 32.0 + packed[1:2, :]).astype(jnp.int32)
    dest = dest - pl.program_id(0) * rows
    hot = jnp.where(
        lax.broadcasted_iota(jnp.int32, (rows, got.shape[0]), 0) == dest, 1.0, 0.0
    ).astype(BF16)
    table[...] = dot(hot, got[:, :D])


def call(kernel, outs, args, scalars=0, scratch=(), flops=0):
    vmem = pl.BlockSpec(memory_space=pltpu.VMEM)
    smem = pl.BlockSpec(memory_space=pltpu.SMEM)
    return pl.pallas_call(
        kernel,
        out_shape=[jax.ShapeDtypeStruct(shape, dtype) for shape, dtype in outs],
        in_specs=[smem] * scalars + [vmem] * (len(args) - scalars),
        out_specs=[vmem] * len(outs),
        scratch_shapes=[pltpu.VMEM(shape, dtype) for shape, dtype in scratch],
        compiler_params=pltpu.CompilerParams(vmem_limit_bytes=48 * 2**20),
        cost_estimate=pl.CostEstimate(flops=flops, bytes_accessed=2**20, transcendentals=0),
    )(*args)


def local(events, grad_out, w_inner, w_outer, valid_lengths, item_ids):
    place_y = lax.axis_index("y")
    place_p = lax.axis_index("p")
    place_c = lax.axis_index("c")
    chip = (place_y * 2 + lax.axis_index("w")) * 2 + place_p
    place = jnp.stack([place_p, place_c, 2 * place_p + place_c]).astype(jnp.int32)
    first = ((chip * 2 + place_c) * BLK).astype(jnp.int32).reshape(1)
    length = lax.dynamic_slice_in_dim(valid_lengths, place_y // 2, 1)
    inv_len = 1.0 / length.astype(F32)
    events = events.reshape(2 * BLK, D)
    grad_out = grad_out.reshape(2 * BLK, D)

    pre, send = call(
        project_kernel,
        [((2 * BLK, 3 * D), F32), ((16 * BLK, 3 * HD), BF16)],
        (events, w_inner),
        flops=10**9,
    )
    mine = lax.all_to_all(send, ("y", "w", "p"), 0, 0, tiled=True)
    swap_c = [(0, 1), (1, 0)]
    theirs = lax.ppermute(mine, "c", swap_c)
    pre_u, gated, send_g, hot, ext = call(
        gate_kernel,
        [
            ((2 * BLK, D), F32),
            ((2 * BLK, D), F32),
            ((8 * BLK, HD), BF16),
            ((CAP * 128, 2 * BLK), BF16),
            ((2 * BLK, EXT), BF16),
        ],
        (events, grad_out, w_inner[:, :D], w_outer, item_ids.reshape(1, 2 * BLK)),
        flops=10**9,
    )
    grad = lax.all_to_all(send_g, ("y", "w"), 0, 0, tiled=True)
    queries = ((1024, HD), BF16)
    (attn_one,) = call(
        functools.partial(forward_kernel, False),
        [((1024, HD), F32)],
        (place, inv_len, mine, mine),
        scalars=2,
        scratch=[queries],
        flops=10**9,
    )
    attn_out, stats = call(
        functools.partial(forward_kernel, True),
        [((1024, HD), F32), ((8, 1024), F32)],
        (place, inv_len, mine, theirs, attn_one, grad),
        scalars=2,
        scratch=[queries],
        flops=10**9,
    )
    others = [
        lax.ppermute(stats, ("y", "w"), [(i, i ^ m) for i in range(8)]) for m in (1, 2, 3)
    ]
    grad_attn, normed_out = call(
        grad_attn_kernel,
        [((1024, HD), BF16), ((1024, HD), BF16)],
        (place, length, attn_out, grad, stats, *others),
        scalars=2,
        flops=10**7,
    )
    grad_p = lax.ppermute(grad_attn, "p", swap_c)
    grad_c = lax.ppermute(grad_attn, "c", swap_c)
    grad_pc = lax.ppermute(grad_p, "c", swap_c)
    (ret1,) = call(
        grad_query_kernel,
        [((1024, 2 * HD), BF16)],
        (place, inv_len, mine, theirs, grad_attn, normed_out),
        scalars=2,
        flops=4 * 10**9,
    )
    got1 = lax.all_to_all(ret1, ("y", "w"), 0, 0, tiled=True)
    (ret2,) = call(
        grad_key_kernel,
        [((1024, 2 * HD), BF16)],
        (place, inv_len, mine, theirs, grad_attn, grad_p, grad_c, grad_pc),
        scalars=2,
        scratch=[((2048, HD), BF16), ((2048, HD), BF16)],
        flops=6 * 10**9,
    )
    got2 = lax.all_to_all(ret2, ("y", "w"), 0, 0, tiled=True)
    (rows,) = call(
        finish_kernel,
        [((CAP * 128, D + EXT), BF16)],
        (
            first,
            valid_lengths,
            got1,
            got2,
            pre_u,
            pre,
            gated,
            events,
            grad_out,
            w_inner,
            hot,
            ext,
        ),
        scalars=2,
        scratch=[((2 * BLK, 4 * D), BF16)],
        flops=10**9,
    )
    got = lax.all_to_all(
        rows.reshape(128, CAP, D + EXT), ("y", "w", "p", "c", "row"), 0, 0, tiled=True
    ).reshape(128 * CAP, D + EXT)
    return pl.pallas_call(
        table_kernel,
        out_shape=jax.ShapeDtypeStruct((ROWS_DEV, D), F32),
        grid=(4,),
        in_specs=[pl.BlockSpec((128 * CAP, D + EXT), lambda i: (0, 0))],
        out_specs=pl.BlockSpec((ROWS_DEV // 4, D), lambda i: (i, 0)),
    )(got)


def solution(mesh):
    fine = Mesh(mesh.devices.reshape(4, 2, 2, 2, 4), ("y", "w", "p", "c", "row"))
    seq = ("y", "w", "p", "c")
    return jax.shard_map(
        local,
        mesh=fine,
        in_specs=(
            P("row", seq, None),
            P("row", seq, None),
            P(),
            P(),
            P("row"),
            P("row", seq),
        ),
        out_specs=P(seq + ("row",), None),
        check_vma=False,
    )
```

time: 362 us -> 161 us (0.44); the launches traced: 357 us -> 161 us
  waiting for transfers between devices: 167 us -> 19.1 us
  matrix products: 130 us -> 0 us
  blocking collectives: 0 us -> 52 us
  Pallas kernels: 0 us -> 44.4 us
  other arithmetic: 19 us -> 0.08 us
  between operations: 13.8 us -> 0.9 us
  starting transfers between devices: 15.4 us -> 27 us
  local copies, waits for them, and re-layouts: 11.8 us -> 17.1 us
    all_gather x4 -> x0, waiting for transfers between devices: 147 us -> none  [the longest x1 53.8 us: local(): lax.all_gather(k_part, 'seq', axis=1, tiled=True)]
    dot_general x27 -> x0, matrix products: 130 us -> none  [the longest x4 28.4 us: local(): jnp.einsum('gij,gjd->gid', grad_score, keys_all[..., head_cols], preferre...]
    all_to_all x0 -> x2, blocking collectives: none -> 52 us  [the longest x1 29.4 us: local(): mine = lax.all_to_all(send, ('y', 'w', 'p'), 0, 0, tiled=True)]
    pallas_call x0 -> x9, Pallas kernels: none -> 44.4 us  [the longest x8 40.6 us: call(): pl.pallas_call(kernel, out_shape=[jax.ShapeDtypeStruct(shape, dtype) for...]
    unnamed x55 -> x46, local copies, waits for them, and re-layouts: 0.12 us -> 15.3 us
    ppermute x0 -> x7, starting transfers between devices: none -> 12.1 us  [the longest x3 4.2 us: local(): lax.ppermute(stats, ('y', 'w'), [(i, i ^ m) for i in range(8)])]
    scatter-add x1 -> x0, other arithmetic: 5.65 us -> none  [local(): table_grad.at[got_ids.reshape(-1)]]
    ppermute x0 -> x7, waiting for transfers between devices: none -> 5.44 us  [the longest x1 2.99 us: local(): grad_p = lax.ppermute(grad_attn, 'p', swap_c)]
  transfers between devices with their start and end apart: 6 -> 10, of which waited for: 5 -> 5; matrix products, arithmetic and copies ran while one was open for 41% -> 0% of each run, Pallas kernels for 0% -> 19%
where the time goes in v1:
time: 161 us
  blocking collectives  52 us (32%)
  Pallas kernels  44.4 us (28%)
  starting transfers between devices  27 us (17%)
  waiting for transfers between devices  19.1 us (12%)
  local copies, waits for them, and re-layouts  17.1 us (11%)
    pallas_call x8, Pallas kernels, call(): pl.pallas_call(kernel, out_shape=[jax.ShapeDtypeStruct(shape, dtype) for...  40.6 us
    all_to_all x1, blocking collectives, local(): mine = lax.all_to_all(send, ('y', 'w', 'p'), 0, 0, tiled=True)  29.4 us
    all_to_all x1, blocking collectives, local(): lax.all_to_all(rows.reshape(128, CAP, D + EXT), ('y', 'w', 'p', 'c', 'row...  22.6 us
    unnamed x46, local copies, waits for them, and re-layouts  15.3 us
    all_to_all x1, waiting for transfers between devices, local(): got2 = lax.all_to_all(ret2, ('y', 'w'), 0, 0, tiled=True)  10.8 us
    all_to_all x1, starting transfers between devices, local(): got2 = lax.all_to_all(ret2, ('y', 'w'), 0, 0, tiled=True)  6.64 us
    all_to_all x1, starting transfers between devices, local(): got1 = lax.all_to_all(ret1, ('y', 'w'), 0, 0, tiled=True)  4.86 us
    ppermute x3, starting transfers between devices, local(): lax.ppermute(stats, ('y', 'w'), [(i, i ^ m) for i in range(8)])  4.2 us
  transfers between devices with their start and end apart: 10, of which 5 were waited for; matrix products, arithmetic and copies ran while one was open for 0% of the time, Pallas kernels for 19%

profile of v1, /device:TPU:1, one launch (start us, length us, event | category | flops | bytes accessed | tf_op | source)
XLA Modules:
  0.0 160.6 jit_solution(6579049780897131318)
XLA Ops:
  0.0 1.6 copy-done
  1.6 0.9 copy-done.12
  2.5 0.9 shard_map.64
  3.5 0.0 copy-start.13
  3.5 0.0 copy-start.22
  3.5 29.4 %all_to_all.49 = bf16[16,128,384]{2,1,0:T(8,128)(2,1)S(1)} all-to-all(bf16[16,128,384]{2,1,0:T(8,128)(2,1)S(1)} %bitcast.25), channel_id=1, replica_groups=mesh['y'=4,'w'=2,'p'=2,'c'=2,'row'=4] {'y','w','p'}, dimensions={0} | all-to-all | bytes 3145728 | tf_op jit(solution)/shard_map/all_to_all | solution.py:313
  32.9 2.0 %collective-permute-start = (bf16[2048,384]{1,0:T(8,128)(2,1)S(1)}, bf16[2048,384]{1,0:T(8,128)(2,1)S(1)}, u32[]{:S(2)}, u32[]{:S(2)}) collective-permute-start(bf16[2048,384]{1,0:T(8,128)(2,1)S(1)} %bitcast.15), channel_id=1, source_target_pairs={{0,4},{4,0},{1,5},{5,1},{2,6},{6,2},{3,7},{7,3},{8,12},{12,8},{9,1... | collective-permute-start | bytes 4718600 | tf_op jit(solution)/shard_map/ppermute | solution.py:315
  35.0 0.0 copy-start.20
  35.0 0.9 shard_map.66
  35.9 0.8 copy-done.8
  36.7 0.8 copy-done.10
  37.5 0.7 copy-done.17
  38.2 0.7 copy-done.19
  38.9 3.4 %all-to-all-start.1 = ((bf16[8,128,128]{2,1,0:T(8,128)(2,1)}), bf16[8,128,128]{2,1,0:T(8,128)(2,1)S(1)}, u32[]{:S(2)}, u32[]{:S(2)}) async-start(bf16[8,128,128]{2,1,0:T(8,128)(2,1)} %bitcast.32), calls=%async_computation.1 | async-start | bytes 524288 | tf_op jit(solution)/shard_map/all_to_all | solution.py:328
  42.4 0.6 dynamic_slice.3.length
  43.6 0.1 pad_add_fusion.place
  43.7 3.5 %shard_map.65.refs_0_ = f32[1024,128]{1,0:T(8,128)S(1)} custom-call(s32[3]{0:T(128)S(1)} %pad_add_fusion.place, f32[1]{0:T(128)S(6)} %div.14.inv_len, bf16[2048,384]{1,0:T(8,128)(2,1)S(1)} %bitcast.16, bf16[2048,384]{1,0:T(8,128)(2,1)S(1)} %bitcast.17), custom_call_target="tpu_custom_call" | custom-call | flops 1000000000 | bytes 1048576 | tf_op jit(solution)/shard_map/pallas_call | solution.py:284
  47.3 0.8 copy-done.5
  48.0 2.9 %all-to-all-done.1 = bf16[8,128,128]{2,1,0:T(8,128)(2,1)S(1)} async-done(((bf16[8,128,128]{2,1,0:T(8,128)(2,1)}), bf16[8,128,128]{2,1,0:T(8,128)(2,1)S(1)}, u32[]{:S(2)}, u32[]{:S(2)}) %all-to-all-start.1) | async-done | bytes 262176 | tf_op jit(solution)/shard_map/all_to_all | solution.py:328
  50.9 1.4 copy-done.6
  52.3 2.5 %shard_map.67 = (f32[1024,128]{1,0:T(8,128)S(1)}, f32[8,1024]{1,0:T(8,128)S(1)}) custom-call(s32[3]{0:T(128)S(1)} %pad_add_fusion.place, f32[1]{0:T(128)S(6)} %div.14.inv_len, bf16[2048,384]{1,0:T(8,128)(2,1)S(1)} %bitcast.18, bf16[2048,384]{1,0:T(8,128)(2,1)S(1)} %collective-permute-done.theirs, f32[1024,128]{1,0:T(8,128)S(1)} %copy-done.6, ...), custom_call_target="tpu_custom_call" | custom-call | flops 1000000000 | bytes 1048576 | tf_op jit(solution)/shard_map/pallas_call | solution.py:284
  54.8 0.9 collective-permute-start.1
  55.7 0.6 collective-permute-start.2
  56.3 2.7 %collective-permute-start.3 = (f32[8,1024]{1,0:T(8,128)S(1)}, f32[8,1024]{1,0:T(8,128)S(1)}, u32[]{:S(2)}, u32[]{:S(2)}) collective-permute-start(f32[8,1024]{1,0:T(8,128)S(1)} %get-tuple-element.19.s0), channel_id=1, source_target_pairs={{0,48},{16,32},{32,16},{48,0},{64,112},{80,96},{96,80},{112,64},{1... | collective-permute-start | bytes 98312 | tf_op jit(solution)/shard_map/ppermute | solution.py:347
  59.0 0.1 collective-permute-done.1.s1
  59.1 2.3 %collective-permute-done.3.s3 = f32[8,1024]{1,0:T(8,128)S(1)} collective-permute-done((f32[8,1024]{1,0:T(8,128)S(1)}, f32[8,1024]{1,0:T(8,128)S(1)}, u32[]{:S(2)}, u32[]{:S(2)}) %collective-permute-start.3) | collective-permute-done | bytes 32800 | tf_op jit(solution)/shard_map/ppermute | solution.py:347
  61.4 2.7 %shard_map.68 = (bf16[1024,128]{1,0:T(8,128)(2,1)}, bf16[1024,128]{1,0:T(8,128)(2,1)S(1)}) custom-call(s32[3]{0:T(128)S(1)} %pad_add_fusion.place, s32[1]{0:T(128)} %dynamic_slice.3.length, f32[1024,128]{1,0:T(8,128)S(1)} %get-tuple-element.18.attn_out, bf16[1024,128]{1,0:T(8,128)(2,1)S(1)} %bitcast.22, f32[8,1024]{1,0:T(8,128)S(1)} %get-tuple-element.19.s0, ...), custom_call_target="tpu_custom_call" | custom-call | flops 10000000 | bytes 1048576 | tf_op jit(solution)/shard_map/pallas_call | solution.py:284
  64.1 0.3 collective-permute-start.4
  64.4 2.5 %collective-permute-start.5 = (bf16[1024,128]{1,0:T(8,128)(2,1)}, bf16[1024,128]{1,0:T(8,128)(2,1)}, u32[]{:S(2)}, u32[]{:S(2)}) collective-permute-start(bf16[1024,128]{1,0:T(8,128)(2,1)} %get-tuple-element.20.grad_attn.g_own), channel_id=1, source_target_pairs={{0,4},{4,0},{1,5},{5,1},{2,6},{6,2},{3,7},{7,3},{8,12},{12,8},{9,1... | collective-permute-start | bytes 786440 | tf_op jit(solution)/shard_map/ppermute | solution.py:357
  66.9 3.0 %collective-permute-done.4.g_p = bf16[1024,128]{1,0:T(8,128)(2,1)S(1)} collective-permute-done((bf16[1024,128]{1,0:T(8,128)(2,1)}, bf16[1024,128]{1,0:T(8,128)(2,1)S(1)}, u32[]{:S(2)}, u32[]{:S(2)}) %collective-permute-start.4) | collective-permute-done | bytes 262176 | tf_op jit(solution)/shard_map/ppermute | solution.py:356
  69.9 3.1 %collective-permute-start.6 = (bf16[1024,128]{1,0:T(8,128)(2,1)S(1)}, bf16[1024,128]{1,0:T(8,128)(2,1)}, u32[]{:S(2)}, u32[]{:S(2)}) collective-permute-start(bf16[1024,128]{1,0:T(8,128)(2,1)S(1)} %collective-permute-done.4.g_p), channel_id=1, source_target_pairs={{0,4},{4,0},{1,5},{5,1},{2,6},{6,2},{3,7},{7,3},{8,12},{12,8},{9,1... | collective-permute-start | bytes 786440 | tf_op jit(solution)/shard_map/ppermute | solution.py:358
  73.1 11.6 %shard_map.69 = bf16[1024,256]{1,0:T(8,128)(2,1)S(1)} custom-call(s32[3]{0:T(128)S(1)} %pad_add_fusion.place, f32[1]{0:T(128)S(6)} %div.14.inv_len, bf16[2048,384]{1,0:T(8,128)(2,1)S(1)} %bitcast.19, bf16[2048,384]{1,0:T(8,128)(2,1)S(1)} %collective-permute-done.theirs, bf16[1024,128]{1,0:T(8,128)(2,1)} %get-tuple-element.20.grad_attn.g_own, ...), custom_call_target="tpu_custom_call" | custom-call | flops 4000000000 | bytes 1048576 | tf_op jit(solution)/shard_map/pallas_call | solution.py:284
  84.7 0.8 copy-done.7
  85.5 4.9 %all-to-all-start.2 = ((bf16[8,128,256]{2,1,0:T(8,128)(2,1)}), bf16[8,128,256]{2,1,0:T(8,128)(2,1)S(1)}, u32[]{:S(2)}, u32[]{:S(2)}) async-start(bf16[8,128,256]{2,1,0:T(8,128)(2,1)} %bitcast.26), calls=%async_computation.2 | async-start | bytes 1048576 | tf_op jit(solution)/shard_map/all_to_all | solution.py:366
  90.4 1.4 copy-done.2
  91.8 14.8 %shard_map.70 = bf16[1024,256]{1,0:T(8,128)(2,1)} custom-call(s32[3]{0:T(128)S(1)} %pad_add_fusion.place, f32[1]{0:T(128)S(6)} %div.14.inv_len, bf16[2048,384]{1,0:T(8,128)(2,1)S(1)} %bitcast.20, bf16[2048,384]{1,0:T(8,128)(2,1)S(1)} %copy-done.2, bf16[1024,128]{1,0:T(8,128)(2,1)} %get-tuple-element.20.grad_attn.g_own, ...), custom_call_target="tpu_custom_call" | custom-call | flops 6000000000 | bytes 1048576 | tf_op jit(solution)/shard_map/pallas_call | solution.py:284
  106.6 6.6 %all-to-all-start.3 = ((bf16[8,128,256]{2,1,0:T(8,128)(2,1)}), bf16[8,128,256]{2,1,0:T(8,128)(2,1)S(1)}, u32[]{:S(2)}, u32[]{:S(2)}) async-start(bf16[8,128,256]{2,1,0:T(8,128)(2,1)} %bitcast.13), calls=%async_computation.3 | async-start | bytes 1048576 | tf_op jit(solution)/shard_map/all_to_all | solution.py:375
  113.2 10.8 %all-to-all-done.3 = bf16[8,128,256]{2,1,0:T(8,128)(2,1)S(1)} async-done(((bf16[8,128,256]{2,1,0:T(8,128)(2,1)}), bf16[8,128,256]{2,1,0:T(8,128)(2,1)S(1)}, u32[]{:S(2)}, u32[]{:S(2)}) %all-to-all-start.3) | async-done | bytes 524320 | tf_op jit(solution)/shard_map/all_to_all | solution.py:375
  124.0 1.4 copy-done.4
  125.4 1.0 copy-done.9
  126.5 1.0 copy-done.11
  127.5 0.9 copy-done.16
  128.5 0.9 copy-done.18
  129.4 3.7 %shard_map.71 = bf16[512,640]{1,0:T(8,128)(2,1)S(1)} custom-call(s32[1]{0:T(128)} %bitcast.first, s32[2]{0:T(128)S(1)} %copy-done.20, bf16[1024,256]{1,0:T(8,128)(2,1)S(1)} %bitcast.23, bf16[1024,256]{1,0:T(8,128)(2,1)S(1)} %bitcast.24, f32[256,512]{1,0:T(8,128)S(1)} %copy-done.9, f32[256,1536]{1,0:T(8,128)S(1)} %copy-done.4, f32[256,512]{1,0:T(8,128)S(1)} %copy-done.11, ...), custom_call_target="tpu_custom_call" | custom-call | flops 1000000000 | bytes 1048576 | tf_op jit(solution)/shard_map/pallas_call | solution.py:284
  133.1 0.2 reshape.30
  133.2 22.6 %all_to_all.50 = bf16[128,4,640]{2,1,0:T(4,128)(2,1)S(1)} all-to-all(bf16[128,4,640]{2,1,0:T(4,128)(2,1)S(1)} %reshape.30), channel_id=1, replica_groups=mesh['y'=4,'w'=2,'p'=2,'c'=2,'row'=4] {'y','w','p','c','row'}, dimensions={0} | all-to-all | bytes 1310720 | tf_op jit(solution)/shard_map/all_to_all | solution.py:397
  155.8 1.0 reshape.31.got
  156.8 3.8 %shard_map.72 = f32[1024,512]{1,0:T(8,128)} custom-call(bf16[512,640]{1,0:T(8,128)(2,1)} %reshape.31.got), custom_call_target="tpu_custom_call" | custom-call | tf_op jit(solution)/shard_map/pallas_call | solution.py:400
  (34 shorter events, 0.1 us)
Async XLA Ops:
  0.0 1.6 copy-start
  1.6 0.9 copy-start.12
  3.5 29.4 %copy-start.3 = (f32[256,1536]{1,0:T(8,128)}, f32[256,1536]{1,0:T(8,128)S(1)}, u32[]{:S(2)}) copy-start(f32[256,1536]{1,0:T(8,128)S(1)} %get-tuple-element.23.pre) | copy-start | bytes 4718596
  3.5 31.5 %copy-start.13 = (bf16[2,128,512]{2,1,0:T(8,128)(2,1)S(1)}, bf16[2,128,512]{2,1,0:T(8,128)(2,1)}, u32[]{:S(2)}) copy-start(bf16[2,128,512]{2,1,0:T(8,128)(2,1)} %param.6) | copy-start | bytes 786436
  3.5 31.5 %copy-start.15 = (bf16[2,128,512]{2,1,0:T(8,128)(2,1)S(1)}, bf16[2,128,512]{2,1,0:T(8,128)(2,1)}, u32[]{:S(2)}) copy-start(bf16[2,128,512]{2,1,0:T(8,128)(2,1)} %param.7) | copy-start | bytes 786436
  3.5 31.5 %copy-start.21 = (bf16[512,512]{1,0:T(8,128)(2,1)S(1)}, bf16[512,512]{1,0:T(8,128)(2,1)}, u32[]{:S(2)}) copy-start(bf16[512,512]{1,0:T(8,128)(2,1)} %w_outer.1) | copy-start | bytes 1572868
  3.5 31.5 %copy-start.22 = (s32[2,128]{1,0:T(2,128)S(1)}, s32[2,128]{1,0:T(2,128)}, u32[]{:S(2)}) copy-start(s32[2,128]{1,0:T(2,128)} %param.11) | copy-start | bytes 3076
  32.9 18.0 %collective-permute-start = (bf16[2048,384]{1,0:T(8,128)(2,1)S(1)}, bf16[2048,384]{1,0:T(8,128)(2,1)S(1)}, u32[]{:S(2)}, u32[]{:S(2)}) collective-permute-start(bf16[2048,384]{1,0:T(8,128)(2,1)S(1)} %bitcast.15), channel_id=1, source_target_pairs={{0,4},{4,0},{1,5},{5,1},{2,6},{6,2},{3,7},{7,3},{8,12},{12,8},{9,1... | collective-permute-start | bytes 4718600 | tf_op jit(solution)/shard_map/ppermute | solution.py:315
  35.0 7.4 %copy-start.20 = (s32[2]{0:T(128)S(1)}, s32[2]{0:T(128)}, u32[]{:S(2)}) copy-start(s32[2]{0:T(128)} %lengths.1) | copy-start | bytes 28
  35.9 0.8 copy-start.8
  36.7 0.8 copy-start.10
  37.5 0.7 copy-start.17
  38.2 0.7 copy-start.19
  38.9 12.0 %all-to-all-start.1 = ((bf16[8,128,128]{2,1,0:T(8,128)(2,1)}), bf16[8,128,128]{2,1,0:T(8,128)(2,1)S(1)}, u32[]{:S(2)}, u32[]{:S(2)}) async-start(bf16[8,128,128]{2,1,0:T(8,128)(2,1)} %bitcast.32), calls=%async_computation.1 | async-start | bytes 524288 | tf_op jit(solution)/shard_map/all_to_all | solution.py:328
  47.2 0.8 copy-start.5
  50.9 22.1 %copy-start.1 = (bf16[2048,384]{1,0:T(8,128)(2,1)}, bf16[2048,384]{1,0:T(8,128)(2,1)S(1)}, u32[]{:S(2)}) copy-start(bf16[2048,384]{1,0:T(8,128)(2,1)S(1)} %collective-permute-done.theirs) | copy-start | bytes 4718596
  50.9 1.4 copy-start.6
  54.8 4.3 %collective-permute-start.1 = (f32[8,1024]{1,0:T(8,128)S(1)}, f32[8,1024]{1,0:T(8,128)S(1)}, u32[]{:S(2)}, u32[]{:S(2)}) collective-permute-start(f32[8,1024]{1,0:T(8,128)S(1)} %get-tuple-element.19.s0), channel_id=1, source_target_pairs={{0,16},{16,0},{32,48},{48,32},{64,80},{80,64},{96,112},{112,96},{1... | collective-permute-start | bytes 98312 | tf_op jit(solution)/shard_map/ppermute | solution.py:347
  55.7 3.4 %collective-permute-start.2 = (f32[8,1024]{1,0:T(8,128)S(1)}, f32[8,1024]{1,0:T(8,128)S(1)}, u32[]{:S(2)}, u32[]{:S(2)}) collective-permute-start(f32[8,1024]{1,0:T(8,128)S(1)} %get-tuple-element.19.s0), channel_id=1, source_target_pairs={{0,32},{16,48},{32,0},{48,16},{64,96},{80,112},{96,64},{112,80},{1... | collective-permute-start | bytes 98312 | tf_op jit(solution)/shard_map/ppermute | solution.py:347
  56.3 5.2 %collective-permute-start.3 = (f32[8,1024]{1,0:T(8,128)S(1)}, f32[8,1024]{1,0:T(8,128)S(1)}, u32[]{:S(2)}, u32[]{:S(2)}) collective-permute-start(f32[8,1024]{1,0:T(8,128)S(1)} %get-tuple-element.19.s0), channel_id=1, source_target_pairs={{0,48},{16,32},{32,16},{48,0},{64,112},{80,96},{96,80},{112,64},{1... | collective-permute-start | bytes 98312 | tf_op jit(solution)/shard_map/ppermute | solution.py:347
  64.1 5.8 %collective-permute-start.4 = (bf16[1024,128]{1,0:T(8,128)(2,1)}, bf16[1024,128]{1,0:T(8,128)(2,1)S(1)}, u32[]{:S(2)}, u32[]{:S(2)}) collective-permute-start(bf16[1024,128]{1,0:T(8,128)(2,1)} %get-tuple-element.20.grad_attn.g_own), channel_id=1, source_target_pairs={{0,8},{8,0},{1,9},{9,1},{2,10},{10,2},{3,11},{11,3},{4,12},{12,4},... | collective-permute-start | bytes 786440 | tf_op jit(solution)/shard_map/ppermute | solution.py:356
  64.4 25.9 %collective-permute-start.5 = (bf16[1024,128]{1,0:T(8,128)(2,1)}, bf16[1024,128]{1,0:T(8,128)(2,1)}, u32[]{:S(2)}, u32[]{:S(2)}) collective-permute-start(bf16[1024,128]{1,0:T(8,128)(2,1)} %get-tuple-element.20.grad_attn.g_own), channel_id=1, source_target_pairs={{0,4},{4,0},{1,5},{5,1},{2,6},{6,2},{3,7},{7,3},{8,12},{12,8},{9,1... | collective-permute-start | bytes 786440 | tf_op jit(solution)/shard_map/ppermute | solution.py:357
  69.9 20.4 %collective-permute-start.6 = (bf16[1024,128]{1,0:T(8,128)(2,1)S(1)}, bf16[1024,128]{1,0:T(8,128)(2,1)}, u32[]{:S(2)}, u32[]{:S(2)}) collective-permute-start(bf16[1024,128]{1,0:T(8,128)(2,1)S(1)} %collective-permute-done.4.g_p), channel_id=1, source_target_pairs={{0,4},{4,0},{1,5},{5,1},{2,6},{6,2},{3,7},{7,3},{8,12},{12,8},{9,1... | collective-permute-start | bytes 786440 | tf_op jit(solution)/shard_map/ppermute | solution.py:358
  84.7 0.8 copy-start.7
  85.5 38.5 %copy-start.14 = (bf16[2,128,512]{2,1,0:T(8,128)(2,1)S(1)}, bf16[2,128,512]{2,1,0:T(8,128)(2,1)}, u32[]{:S(2)}) copy-start(bf16[2,128,512]{2,1,0:T(8,128)(2,1)} %param.6) | copy-start | bytes 786436
  85.5 21.1 %all-to-all-start.2 = ((bf16[8,128,256]{2,1,0:T(8,128)(2,1)}), bf16[8,128,256]{2,1,0:T(8,128)(2,1)S(1)}, u32[]{:S(2)}, u32[]{:S(2)}) async-start(bf16[8,128,256]{2,1,0:T(8,128)(2,1)} %bitcast.26), calls=%async_computation.2 | async-start | bytes 1048576 | tf_op jit(solution)/shard_map/all_to_all | solution.py:366
  90.4 1.4 copy-start.2
  106.6 17.4 %all-to-all-start.3 = ((bf16[8,128,256]{2,1,0:T(8,128)(2,1)}), bf16[8,128,256]{2,1,0:T(8,128)(2,1)S(1)}, u32[]{:S(2)}, u32[]{:S(2)}) async-start(bf16[8,128,256]{2,1,0:T(8,128)(2,1)} %bitcast.13), calls=%async_computation.3 | async-start | bytes 1048576 | tf_op jit(solution)/shard_map/all_to_all | solution.py:375
  124.0 1.4 copy-start.4
  125.4 1.0 copy-start.9
  126.5 1.0 copy-start.11
  127.5 0.9 copy-start.16
  128.5 0.9 copy-start.18

commit v2 on v1

v2 whole, which is shorter than its diff:
```python
import functools

import jax
import jax.numpy as jnp
from jax import lax
from jax.experimental import pallas as pl
from jax.experimental.pallas import tpu as pltpu
from jax.sharding import Mesh
from jax.sharding import PartitionSpec as P

HEADS = 4
ROWS_DEV = 1024
D = 512
HD = 128
BLK = 128
CAP = 4
EXT = 128
F32 = jnp.float32
BF16 = jnp.bfloat16
SCALE = HD**-0.5
VMEM_LIMIT = 24 * 2**20


def dot(a, b):
    return lax.dot_general(a, b, (((1,), (0,)), ((), ())), preferred_element_type=F32)


def dot_t(a, b):
    return lax.dot_general(a, b, (((1,), (1,)), ((), ())), preferred_element_type=F32)


def normalize(values):
    center = values - jnp.mean(values, axis=-1, keepdims=True)
    inverse = lax.rsqrt(jnp.mean(center * center, axis=-1, keepdims=True) + 1e-05)
    return center * inverse, inverse


def silu(values):
    half = 0.5 * values
    return half * jnp.tanh(half) + half


def silu_slope(values):
    half = 0.5 * values
    two_sigma = 1.0 + jnp.tanh(half)
    return 0.5 * two_sigma * (1.0 + values - half * two_sigma)


def project_kernel(events, w_part, pre, send, normed):
    @pl.when(pl.program_id(0) == 0)
    def _():
        normed[...] = normalize(events[...].astype(F32))[0].astype(BF16)

    values = dot(normed[...], w_part[...])
    pre[...] = values
    act = silu(values).astype(BF16)
    for g in range(2):
        for h in range(HEADS):
            piece = act[g * BLK : (g + 1) * BLK, h * HD : (h + 1) * HD]
            for p in range(2):
                at = ((g * HEADS + h) * 2 + p) * BLK
                send[at : at + BLK, :] = piece


def gate_kernel(
    events, grad_out, w_u, w_outer, ids, pre, slope, normed_out, inv_out, send_g, hot, ext
):
    normed, inverse = normalize(events[...].astype(F32))
    normed_out[...] = normed
    inv_out[...] = jnp.broadcast_to(inverse, inv_out.shape)
    values = dot(normed.astype(BF16), w_u[...])
    grad_gated = dot_t(grad_out[...], w_outer[...])
    prod = (grad_gated * silu(values).astype(BF16).astype(F32)).astype(BF16)
    for g in range(2):
        for h in range(HEADS):
            at = (g * HEADS + h) * BLK
            send_g[at : at + BLK, :] = prod[g * BLK : (g + 1) * BLK, h * HD : (h + 1) * HD]
    slope[:, :D] = grad_gated * silu_slope(values)
    slope[:, D:] = silu_slope(pre[...])
    count = 2 * BLK
    id_row = ids[...]
    id_cols = jnp.transpose(jnp.broadcast_to(id_row.astype(F32), (BLK, count))).astype(jnp.int32)
    owner_row = id_row // ROWS_DEV
    owner_col = id_cols[:, :1] // ROWS_DEV
    earlier = lax.broadcasted_iota(jnp.int32, (count, count), 0) < lax.broadcasted_iota(
        jnp.int32, (count, count), 1
    )
    same = jnp.where((owner_col == owner_row) & earlier, 1, 0)
    rank = jnp.sum(same, axis=0, keepdims=True)
    slot = owner_row * CAP + rank
    slots = hot.shape[0]
    hot[...] = jnp.where(
        lax.broadcasted_iota(jnp.int32, (slots, count), 0) == slot, 1.0, 0.0
    ).astype(BF16)
    within = id_cols - (id_cols // ROWS_DEV) * ROWS_DEV
    high = within // 32
    lane = lax.broadcasted_iota(jnp.int32, (count, EXT), 1)
    ext[...] = (
        jnp.where(lane == 0, high + 1, jnp.where(lane == 1, within - high * 32, 0))
        .astype(F32)
        .astype(BF16)
    )


V_COLS, Q_COLS, K_COLS = (slice(i * HD, (i + 1) * HD) for i in range(3))


def my_place():
    p, c = lax.axis_index("p"), lax.axis_index("c")
    return p, c, 2 * p + c


def my_length(lengths):
    return lengths[lax.axis_index("y") // 2]


def inverse_of(length):
    return 1.0 / jnp.full((1, HD), length, jnp.int32).astype(F32)


def query_mask(place, core, count):
    row = lax.broadcasted_iota(jnp.int32, (count, 2 * BLK), 0)
    lane = lax.broadcasted_iota(jnp.int32, (count, 2 * BLK), 1)
    col = lane + jnp.where(lane >= BLK, BLK, 0) + core * BLK
    return (row >= BLK) | (col <= row + place[2] * BLK)


def key_mask(place, core, count):
    row = lax.broadcasted_iota(jnp.int32, (count, 2 * BLK), 0) - (count - BLK)
    lane = lax.broadcasted_iota(jnp.int32, (count, 2 * BLK), 1)
    col = lane + jnp.where(lane >= BLK, BLK, 0) + core * BLK
    return (row < 0) | (row + place[2] * BLK <= col)


def own_blocks(place, src, cols, dst):
    for m in range(8):
        at = pl.multiple_of((2 * m + place[0]) * BLK, BLK)
        dst[m * BLK : (m + 1) * BLK, :] = src[pl.ds(at, BLK), cols]


def forward_kernel(last, lengths, mine, *refs):
    place = my_place()
    inv_len = inverse_of(my_length(lengths))
    if last:
        theirs, before, grad, out, stats, queries = refs
        keys_of, core = theirs, 1 - place[1]
    else:
        out, queries = refs
        keys_of, core = mine, place[1]
    own_blocks(place, mine, Q_COLS, queries)
    out[...] = before[...] if last else jnp.zeros_like(out)
    for j in range(8):
        keys = slice(j * 2 * BLK, (j + 1) * 2 * BLK)
        rows = slice(j * BLK, 8 * BLK)
        half = dot_t(queries[rows, :], keys_of[keys, K_COLS]) * (0.5 * SCALE)
        attn = half * jnp.tanh(half) + half
        attn = jnp.where(query_mask(place, core, (8 - j) * BLK), attn, 0.0)
        out[rows, :] += dot(attn.astype(BF16), keys_of[keys, V_COLS])
    if not last:
        return
    for m in range(8):
        rows = slice(m * BLK, (m + 1) * BLK)
        total = out[rows, :] * inv_len
        out[rows, :] = total
        g = grad[rows, :].astype(F32)
        mean = jnp.mean(total, axis=-1, keepdims=True)
        center = total - mean
        square = jnp.sum(center * center, axis=-1, keepdims=True)
        sum_g = jnp.sum(g, axis=-1, keepdims=True)
        sum_ga = jnp.sum(g * center, axis=-1, keepdims=True)
        lane = lax.broadcasted_iota(jnp.int32, (BLK, BLK), 1)
        packed = jnp.where(
            lane == 0, mean, jnp.where(lane == 1, square, jnp.where(lane == 2, sum_g, sum_ga))
        )
        stats[:, rows] = jnp.transpose(packed)[:8, :]


def grad_attn_kernel(lengths, attn_out, grad, s0, s1, s2, s3, grad_attn, normed_out):
    place = my_place()
    length = my_length(lengths)
    parts = [s0[...], s1[...], s2[...], s3[...]]
    means = [part[0:1, :] for part in parts]
    mean = 0.25 * (means[0] + means[1] + means[2] + means[3])
    square = 0.0
    sum_g = 0.0
    sum_ga = 0.0
    for part, own in zip(parts, means):
        shift = own - mean
        square = square + part[1:2, :] + HD * (shift * shift)
        sum_g = sum_g + part[2:3, :]
        sum_ga = sum_ga + part[3:4, :] + part[2:3, :] * shift
    inverse = lax.rsqrt(square * (1.0 / D) + 1e-05)
    mean_g = sum_g * (1.0 / D)
    mean_gn = inverse * sum_ga * (1.0 / D)
    row = lax.broadcasted_iota(jnp.int32, (BLK, 1024), 0)
    packed = jnp.where(
        row == 0, mean, jnp.where(row == 1, inverse, jnp.where(row == 2, mean_g, mean_gn))
    )
    for m in range(8):
        rows = slice(m * BLK, (m + 1) * BLK)
        cols = jnp.transpose(packed[:, rows])
        inv = cols[:, 1:2]
        n = (attn_out[rows, :] - cols[:, 0:1]) * inv
        back = (grad[rows, :].astype(F32) - cols[:, 2:3] - n * cols[:, 3:4]) * inv
        pos = lax.broadcasted_iota(jnp.int32, (BLK, 1), 0) + (m * 4 + place[2]) * BLK
        grad_attn[rows, :] = jnp.where(pos < length, back, 0.0).astype(BF16)
        normed_out[rows, :] = n.astype(BF16)


def slopes(raw):
    half = raw * (0.5 * SCALE)
    t = jnp.tanh(half)
    two_sigma = 1.0 + t
    return two_sigma + half * (1.0 - t * t), half * two_sigma


def grad_query_kernel(lengths, mine, theirs, grad_attn, ret, queries, total):
    place = my_place()
    inv_len = inverse_of(my_length(lengths))
    own_blocks(place, mine, Q_COLS, queries)
    total[...] = jnp.zeros_like(total)
    for j in range(8):
        keys = slice(j * 2 * BLK, (j + 1) * 2 * BLK)
        rows = slice(j * BLK, 8 * BLK)
        for src, core in ((mine, place[1]), (theirs, 1 - place[1])):
            k = src[keys, K_COLS]
            slope, _ = slopes(dot_t(queries[rows, :], k))
            score = slope * dot_t(grad_attn[rows, :], src[keys, V_COLS])
            score = jnp.where(query_mask(place, core, (8 - j) * BLK), score, 0.0)
            total[rows, :] += dot(score.astype(BF16), k)
    ret[...] = (total[...] * (0.5 * SCALE * inv_len)).astype(BF16)


def grad_key_kernel(
    lengths,
    mine,
    theirs,
    g_own,
    g_p,
    g_c,
    g_pc,
    normed_out,
    grad_q,
    ret,
    mine_g,
    theirs_g,
    keys,
    values,
    grad_k,
    grad_v,
):
    place = my_place()
    inv_len = inverse_of(my_length(lengths))
    p = place[0]
    own_blocks(place, mine, K_COLS, keys)
    own_blocks(place, mine, V_COLS, values)
    for m in range(8):
        rows = slice(m * BLK, (m + 1) * BLK)
        here = pl.multiple_of((2 * m + p) * BLK, BLK)
        there = pl.multiple_of((2 * m + 1 - p) * BLK, BLK)
        mine_g[pl.ds(here, BLK), :] = g_own[rows, :]
        mine_g[pl.ds(there, BLK), :] = g_p[rows, :]
        theirs_g[pl.ds(here, BLK), :] = g_c[rows, :]
        theirs_g[pl.ds(there, BLK), :] = g_pc[rows, :]
    grad_k[...] = jnp.zeros_like(grad_k)
    grad_v[...] = jnp.zeros_like(grad_v)
    for j in range(8):
        events = slice(j * 2 * BLK, (j + 1) * 2 * BLK)
        rows = slice(0, (j + 1) * BLK)
        for src, src_g, core in ((mine, mine_g, place[1]), (theirs, theirs_g, 1 - place[1])):
            q = src[events, Q_COLS]
            ga = src_g[events, :]
            slope, attn = slopes(dot_t(keys[rows, :], q))
            mask = key_mask(place, core, (j + 1) * BLK)
            score = jnp.where(mask, slope * dot_t(values[rows, :], ga), 0.0)
            attn = jnp.where(mask, attn, 0.0)
            grad_k[rows, :] += dot(score.astype(BF16), q)
            grad_v[rows, :] += dot(attn.astype(BF16), ga)
    ret[:, :HD] = normed_out[...]
    ret[:, HD : 2 * HD] = (grad_v[...] * inv_len).astype(BF16)
    ret[:, 2 * HD : 3 * HD] = grad_q[...]
    ret[:, 3 * HD :] = (grad_k[...] * (0.5 * SCALE * inv_len)).astype(BF16)


def finish_kernel(
    lengths, ret, slope, normed, inverse, grad_out, w_inner, hot, ext, send, grads
):
    for g in range(2):
        rows = slice(g * BLK, (g + 1) * BLK)
        for h in range(HEADS):
            at = slice((g * HEADS + h) * BLK, (g * HEADS + h + 1) * BLK)
            for part in range(4):
                cols = slice(part * D + h * HD, part * D + (h + 1) * HD)
                grad = ret[at, part * HD : (part + 1) * HD].astype(F32)
                grads[rows, cols] = (grad * slope[rows, cols]).astype(BF16)
    grad_normed = dot_t(grads[...], w_inner[...])
    back = inverse[:, :1] * (
        grad_normed
        - jnp.mean(grad_normed, axis=-1, keepdims=True)
        - normed[...] * jnp.mean(grad_normed * normed[...], axis=-1, keepdims=True)
    )
    total = grad_out[...].astype(F32) + back
    chip = (lax.axis_index("y") * 2 + lax.axis_index("w")) * 2 + lax.axis_index("p")
    first = (chip * 2 + lax.axis_index("c")) * BLK
    row = lax.broadcasted_iota(jnp.int32, (2 * BLK, 1), 0)
    second = row >= BLK
    pos = first + jnp.where(second, row - BLK, row)
    total = jnp.where(pos < jnp.where(second, lengths[1], lengths[0]), total, 0.0)
    send[:, :D] = dot(hot[...], total.astype(BF16)).astype(BF16)
    send[:, D:] = dot(hot[...], ext[...]).astype(BF16)


def table_kernel(got, table):
    packed = jnp.transpose(got[:, D:].astype(F32))
    dest = ((packed[0:1, :] - 1.0) * 32.0 + packed[1:2, :]).astype(jnp.int32)
    rows = 256
    for i in range(ROWS_DEV // rows):
        hot = jnp.where(
            lax.broadcasted_iota(jnp.int32, (rows, got.shape[0]), 0) == dest - i * rows, 1.0, 0.0
        ).astype(BF16)
        table[i * rows : (i + 1) * rows, :] = dot(hot, got[:, :D])


def call(kernel, outs, args, scalars=1, scratch=(), flops=0):
    vmem = pl.BlockSpec(memory_space=pltpu.VMEM)
    smem = pl.BlockSpec(memory_space=pltpu.SMEM)
    return pl.pallas_call(
        kernel,
        out_shape=[jax.ShapeDtypeStruct(shape, dtype) for shape, dtype in outs],
        in_specs=[smem] * scalars + [vmem] * (len(args) - scalars),
        out_specs=[vmem] * len(outs),
        scratch_shapes=[pltpu.VMEM(shape, dtype) for shape, dtype in scratch],
        compiler_params=pltpu.CompilerParams(vmem_limit_bytes=VMEM_LIMIT),
        cost_estimate=pl.CostEstimate(flops=flops, bytes_accessed=2**20, transcendentals=0),
    )(*args)


def project(events, w_inner):
    return pl.pallas_call(
        project_kernel,
        grid=(3,),
        out_shape=[
            jax.ShapeDtypeStruct((2 * BLK, 3 * D), F32),
            jax.ShapeDtypeStruct((16 * BLK, 3 * HD), BF16),
        ],
        in_specs=[
            pl.BlockSpec((2 * BLK, D), lambda i: (0, 0)),
            pl.BlockSpec((D, D), lambda i: (0, i + 1)),
        ],
        out_specs=[
            pl.BlockSpec((2 * BLK, D), lambda i: (0, i)),
            pl.BlockSpec((16 * BLK, HD), lambda i: (0, i)),
        ],
        scratch_shapes=[pltpu.VMEM((2 * BLK, D), BF16)],
        compiler_params=pltpu.CompilerParams(vmem_limit_bytes=VMEM_LIMIT),
    )(events, w_inner)


def local(events, grad_out, w_inner, w_outer, valid_lengths, item_ids):
    events = events.reshape(2 * BLK, D)
    grad_out = grad_out.reshape(2 * BLK, D)
    pre, send = project(events, w_inner)
    mine = lax.all_to_all(send, ("y", "w", "p"), 0, 0, tiled=True)
    slope, normed, inverse, send_g, hot, ext = call(
        gate_kernel,
        [
            ((2 * BLK, 4 * D), F32),
            ((2 * BLK, D), F32),
            ((2 * BLK, HD), F32),
            ((8 * BLK, HD), BF16),
            ((CAP * 128, 2 * BLK), BF16),
            ((2 * BLK, EXT), BF16),
        ],
        (events, grad_out, w_inner[:, :D], w_outer, item_ids.reshape(1, 2 * BLK), pre),
        scalars=0,
        flops=10**9,
    )
    grad = lax.all_to_all(send_g, ("y", "w"), 0, 0, tiled=True)
    mine, grad = lax.optimization_barrier((mine, grad))
    theirs = lax.ppermute(mine, "c", [(0, 1), (1, 0)])
    queries = ((1024, HD), BF16)
    (attn_one,) = call(
        functools.partial(forward_kernel, False),
        [((1024, HD), F32)],
        (valid_lengths, mine),
        scratch=[queries],
        flops=10**9,
    )
    attn_out, stats = call(
        functools.partial(forward_kernel, True),
        [((1024, HD), F32), ((8, 1024), F32)],
        (valid_lengths, mine, theirs, attn_one, grad),
        scratch=[queries],
        flops=10**9,
    )
    others = [
        lax.ppermute(stats, ("y", "w"), [(i, i ^ m) for i in range(8)]) for m in (1, 2, 3)
    ]
    grad_attn, normed_out = call(
        grad_attn_kernel,
        [((1024, HD), BF16), ((1024, HD), BF16)],
        (valid_lengths, attn_out, grad, stats, *others),
        flops=10**7,
    )
    grad_p, grad_c, grad_pc = [
        lax.ppermute(grad_attn, ("p", "c"), [(i, i ^ m) for i in range(4)]) for m in (2, 1, 3)
    ]
    (grad_q,) = call(
        grad_query_kernel,
        [((1024, HD), BF16)],
        (valid_lengths, mine, theirs, grad_attn),
        scratch=[queries, ((1024, HD), F32)],
        flops=4 * 10**9,
    )
    (ret,) = call(
        grad_key_kernel,
        [((1024, 4 * HD), BF16)],
        (
            valid_lengths,
            mine,
            theirs,
            grad_attn,
            grad_p,
            grad_c,
            grad_pc,
            normed_out,
            grad_q,
        ),
        scratch=[((2048, HD), BF16)] * 2 + [queries] * 2 + [((1024, HD), F32)] * 2,
        flops=6 * 10**9,
    )
    got = lax.all_to_all(ret, ("y", "w"), 0, 0, tiled=True)
    (rows,) = call(
        finish_kernel,
        [((CAP * 128, D + EXT), BF16)],
        (valid_lengths, got, slope, normed, inverse, grad_out, w_inner, hot, ext),
        scratch=[((2 * BLK, 4 * D), BF16)],
        flops=10**9,
    )
    got = lax.all_to_all(
        rows.reshape(128, CAP, D + EXT), ("y", "w", "p", "c", "row"), 0, 0, tiled=True
    ).reshape(128 * CAP, D + EXT)
    (table,) = call(table_kernel, [((ROWS_DEV, D), F32)], (got,), scalars=0)
    return table


def solution(mesh):
    fine = Mesh(mesh.devices.reshape(4, 2, 2, 2, 4), ("y", "w", "p", "c", "row"))
    seq = ("y", "w", "p", "c")
    return jax.shard_map(
        local,
        mesh=fine,
        in_specs=(
            P("row", seq, None),
            P("row", seq, None),
            P(),
            P(),
            P("row"),
            P("row", seq),
        ),
        out_specs=P(seq + ("row",), None),
        check_vma=False,
    )
```

time: 161 us -> 133 us (0.83)
  blocking collectives: 52 us -> 83.2 us
  Pallas kernels: 44.4 us -> 26.6 us
  starting transfers between devices: 27 us -> 10.4 us
  local copies, waits for them, and re-layouts: 17.1 us -> 4.01 us
  waiting for transfers between devices: 19.1 us -> 8.51 us
    all_to_all x0 -> x2, blocking collectives: none -> 36.5 us  [the longest x1 21.6 us: local(): got = lax.all_to_all(ret, ('y', 'w'), 0, 0, tiled=True)]
    pallas_call x8, Pallas kernels: 40.6 us -> 24.8 us  [call(): pl.pallas_call(kernel, out_shape=[jax.ShapeDtypeStruct(shape, dtype) for...]
    all_to_all x3 -> x0, starting transfers between devices: 14.9 us -> none  [the longest x1 6.64 us: local(): got2 = lax.all_to_all(ret2, ('y', 'w'), 0, 0, tiled=True)]
    all_to_all x3 -> x0, waiting for transfers between devices: 13.7 us -> none  [the longest x1 10.8 us: local(): got2 = lax.all_to_all(ret2, ('y', 'w'), 0, 0, tiled=True)]
    unnamed x46 -> x14, local copies, waits for them, and re-layouts: 15.3 us -> 2.56 us
    all_to_all x1, blocking collectives: 29.4 us -> 24 us  [local(): mine = lax.all_to_all(send, ('y', 'w', 'p'), 0, 0, tiled=True)]
    ppermute x4, waiting for transfers between devices: 3 us -> 6.68 us  [the longest x3 5.69 us: local(): lax.ppermute(grad_attn, ('p', 'c'), [(i, i ^ m) for i in range(4)])]
    pallas_call x1, Pallas kernels: 3.77 us -> 1.79 us  [project(): pl.pallas_call(project_kernel, grid=(3,), out_shape=[jax.ShapeDtypeStruct...]
  transfers between devices with their start and end apart: 10 -> 7, of which waited for: 5 -> 4; matrix products, arithmetic and copies ran while one was open for 0% -> 0% of each run, Pallas kernels for 19% -> 6%
where the time goes in v2:
time: 133 us
  blocking collectives  83.2 us (63%)
  Pallas kernels  26.6 us (20%)
  starting transfers between devices  10.4 us (8%)
  waiting for transfers between devices  8.51 us (6%)
  local copies, waits for them, and re-layouts  4.01 us (3%)
    pallas_call x8, Pallas kernels, call(): pl.pallas_call(kernel, out_shape=[jax.ShapeDtypeStruct(shape, dtype) for...  24.8 us
    all_to_all x1, blocking collectives, local(): mine = lax.all_to_all(send, ('y', 'w', 'p'), 0, 0, tiled=True)  24 us
    all_to_all x1, blocking collectives, local(): lax.all_to_all(rows.reshape(128, CAP, D + EXT), ('y', 'w', 'p', 'c', 'row...  22.7 us
    all_to_all x1, blocking collectives, local(): got = lax.all_to_all(ret, ('y', 'w'), 0, 0, tiled=True)  21.6 us
    all_to_all x1, blocking collectives, local(): grad = lax.all_to_all(send_g, ('y', 'w'), 0, 0, tiled=True)  14.9 us
    ppermute x3, waiting for transfers between devices, local(): lax.ppermute(grad_attn, ('p', 'c'), [(i, i ^ m) for i in range(4)])  5.69 us
    ppermute x3, starting transfers between devices, local(): lax.ppermute(stats, ('y', 'w'), [(i, i ^ m) for i in range(8)])  4.16 us
    ppermute x3, starting transfers between devices, local(): lax.ppermute(grad_attn, ('p', 'c'), [(i, i ^ m) for i in range(4)])  3.22 us
  transfers between devices with their start and end apart: 7, of which 4 were waited for; matrix products, arithmetic and copies ran while one was open for 0% of the time, Pallas kernels for 6%

profile of v2, /device:TPU:1, one launch (start us, length us, event | category | flops | bytes accessed | tf_op | source)
XLA Modules:
  0.0 132.8 jit_solution(392356290399434669)
XLA Ops:
  0.0 0.0 copy-start.6
  0.0 0.0 copy-start.5
  0.0 0.0 copy-start.2
  0.0 1.2 slice.3.w_u
  1.2 0.0 copy-start
  1.2 1.6 %copy-done = bf16[512,2048]{1,0:T(8,128)(2,1)S(1)} copy-done((bf16[512,2048]{1,0:T(8,128)(2,1)S(1)}, bf16[512,2048]{1,0:T(8,128)(2,1)}, u32[]{:S(2)}) %copy-start) | copy-done | bytes 2097176
  2.8 0.0 copy-start.3
  2.8 0.9 copy-done.3
  3.7 1.8 %shard_map.64 = (f32[256,1536]{1,0:T(8,128)S(1)}, bf16[2048,384]{1,0:T(8,128)(2,1)S(1)}) custom-call(bf16[256,512]{1,0:T(8,128)(2,1)S(1)} %bitcast.21, bf16[512,2048]{1,0:T(8,128)(2,1)S(1)} %copy-done), custom_call_target="tpu_custom_call" | custom-call | tf_op jit(solution)/shard_map/pallas_call | solution.py:339
  5.5 0.0 copy-done.6
  5.5 0.0 copy-done.5
  5.5 0.0 copy-done.2
  5.5 2.1 %shard_map.65 = (f32[256,2048]{1,0:T(8,128)S(1)}, f32[256,512]{1,0:T(8,128)S(1)}, f32[256,128]{1,0:T(8,128)S(1)}, bf16[1024,128]{1,0:T(8,128)(2,1)S(1)}, bf16[51...) custom-call(bf16[256,512]{1,0:T(8,128)(2,1)S(1)} %bitcast.22, bf16[256,512]{1,0:T(8,128)(2,1)S(1)} %bitcast.19, ...), custom_call_target="tpu_custom_call" | custom-call | flops 1000000000 | bytes 1048576 | tf_op jit(solution)/shard_map/pallas_call | solution.py:327
  7.7 14.9 %all_to_all.40 = bf16[8,128,128]{2,1,0:T(8,128)(2,1)S(1)} all-to-all(bf16[8,128,128]{2,1,0:T(8,128)(2,1)S(1)} %bitcast.23), channel_id=1, replica_groups=mesh['y'=4,'w'=2,'p'=2,'c'=2,'row'=4] {'y','w'}, dimensions={0} | all-to-all | bytes 524288 | tf_op jit(solution)/shard_map/all_to_all | solution.py:378
  22.6 0.0 copy-start.4
  22.6 24.0 %all_to_all.41 = bf16[16,128,384]{2,1,0:T(8,128)(2,1)S(1)} all-to-all(bf16[16,128,384]{2,1,0:T(8,128)(2,1)S(1)} %bitcast.17), channel_id=1, replica_groups=mesh['y'=4,'w'=2,'p'=2,'c'=2,'row'=4] {'y','w','p'}, dimensions={0} | all-to-all | bytes 3145728 | tf_op jit(solution)/shard_map/all_to_all | solution.py:363
  46.6 3.0 %collective-permute-start = (bf16[2048,384]{1,0:T(8,128)(2,1)S(1)}, bf16[2048,384]{1,0:T(8,128)(2,1)S(1)}, u32[]{:S(2)}, u32[]{:S(2)}) collective-permute-start(bf16[2048,384]{1,0:T(8,128)(2,1)S(1)} %bitcast.9), channel_id=1, source_target_pairs={{0,4},{4,0},{1,5},{5,1},{2,6},{6,2},{3,7},{7,3},{8,12},{12,8},{9,1... | collective-permute-start | bytes 4718600 | tf_op jit(solution)/shard_map/ppermute | solution.py:380
  49.6 0.0 copy-done.4
  49.6 2.0 %shard_map.66.refs_1_ = f32[1024,128]{1,0:T(8,128)S(1)} custom-call(s32[2]{0:T(128)S(1)} %copy-done.4, bf16[2048,384]{1,0:T(8,128)(2,1)S(1)} %bitcast.10), custom_call_target="tpu_custom_call" | custom-call | flops 1000000000 | bytes 1048576 | tf_op jit(solution)/shard_map/pallas_call | solution.py:327
  51.6 1.0 collective-permute-done.refs_0_.theirs
  52.6 2.4 %shard_map.67 = (f32[1024,128]{1,0:T(8,128)S(1)}, f32[8,1024]{1,0:T(8,128)S(1)}) custom-call(s32[2]{0:T(128)S(1)} %copy-done.4, bf16[2048,384]{1,0:T(8,128)(2,1)S(1)} %bitcast.11, bf16[2048,384]{1,0:T(8,128)(2,1)S(1)} %collective-permute-done.refs_0_.theirs, f32[1024,128]{1,0:T(8,128)S(1)} %shard_map.66.refs_1_, bf16[1024,128]{1,0:T(8,128)(2,1)S(1)} %bitcast.15), custom_call_target="tpu_custom_call" | custom-call | flops 1000000000 | bytes 1048576 | tf_op jit(solution)/shard_map/pallas_call | solution.py:327
  55.1 0.3 collective-permute-start.3
  55.4 1.1 collective-permute-start.2
  56.5 2.7 %collective-permute-start.1 = (f32[8,1024]{1,0:T(8,128)S(1)}, f32[8,1024]{1,0:T(8,128)S(1)}, u32[]{:S(2)}, u32[]{:S(2)}) collective-permute-start(f32[8,1024]{1,0:T(8,128)S(1)} %get-tuple-element.25.s0), channel_id=1, source_target_pairs={{0,16},{16,0},{32,48},{48,32},{64,80},{80,64},{96,112},{112,96},{1... | collective-permute-start | bytes 98312 | tf_op jit(solution)/shard_map/ppermute | solution.py:397
  59.2 1.0 collective-permute-done.3.s3
  60.2 0.0 collective-permute-done.2.s2
  60.2 0.8 collective-permute-done.1.s1
  61.1 1.4 %shard_map.68 = (bf16[1024,128]{1,0:T(8,128)(2,1)S(1)}, bf16[1024,128]{1,0:T(8,128)(2,1)S(1)}) custom-call(s32[2]{0:T(128)S(1)} %copy-done.4, f32[1024,128]{1,0:T(8,128)S(1)} %get-tuple-element.24.attn_out, bf16[1024,128]{1,0:T(8,128)(2,1)S(1)} %bitcast.16, f32[8,1024]{1,0:T(8,128)S(1)} %get-tuple-element.25.s0, f32[8,1024]{1,0:T(8,128)S(1)} %collective-permute-done.1.s1, ...), custom_call_target="tpu_custom_call" | custom-call | flops 10000000 | bytes 1048576 | tf_op jit(solution)/shard_map/pallas_call | solution.py:327
  62.5 1.8 %collective-permute-start.6 = (bf16[1024,128]{1,0:T(8,128)(2,1)S(1)}, bf16[1024,128]{1,0:T(8,128)(2,1)S(1)}, u32[]{:S(2)}, u32[]{:S(2)}) collective-permute-start(bf16[1024,128]{1,0:T(8,128)(2,1)S(1)} %get-tuple-element.26.grad_attn.g_own), channel_id=1, source_target_pairs={{0,12},{4,8},{8,4},{12,0},{1,13},{5,9},{9,5},{13,1},{2,14},{6,10},... | collective-permute-start | bytes 786440 | tf_op jit(solution)/shard_map/ppermute | solution.py:406
  64.3 0.2 collective-permute-start.5
  64.4 1.3 collective-permute-start.4
  65.7 5.4 %shard_map.69.grad_q = bf16[1024,128]{1,0:T(8,128)(2,1)S(1)} custom-call(s32[2]{0:T(128)S(1)} %copy-done.4, bf16[2048,384]{1,0:T(8,128)(2,1)S(1)} %bitcast.12, bf16[2048,384]{1,0:T(8,128)(2,1)S(1)} %collective-permute-done.refs_0_.theirs, bf16[1024,128]{1,0:T(8,128)(2,1)S(1)} %get-tuple-element.26.grad_attn.g_own), custom_call_target="tpu_custom_call" | custom-call | flops 4000000000 | bytes 1048576 | tf_op jit(solution)/shard_map/pallas_call | solution.py:327
  71.1 0.0 collective-permute-done.6.g_pc
  71.1 0.0 collective-permute-done.5.g_c
  71.1 5.7 %collective-permute-done.4.g_p = bf16[1024,128]{1,0:T(8,128)(2,1)S(1)} collective-permute-done((bf16[1024,128]{1,0:T(8,128)(2,1)S(1)}, bf16[1024,128]{1,0:T(8,128)(2,1)S(1)}, u32[]{:S(2)}, u32[]{:S(2)}) %collective-permute-start.4) | collective-permute-done | bytes 262176 | tf_op jit(solution)/shard_map/ppermute | solution.py:406
  76.8 7.3 %shard_map.70 = bf16[1024,512]{1,0:T(8,128)(2,1)S(1)} custom-call(s32[2]{0:T(128)S(1)} %copy-done.4, bf16[2048,384]{1,0:T(8,128)(2,1)S(1)} %bitcast.13, bf16[2048,384]{1,0:T(8,128)(2,1)S(1)} %collective-permute-done.refs_0_.theirs, bf16[1024,128]{1,0:T(8,128)(2,1)S(1)} %get-tuple-element.26.grad_attn.g_own, ...), custom_call_target="tpu_custom_call" | custom-call | flops 6000000000 | bytes 1048576 | tf_op jit(solution)/shard_map/pallas_call | solution.py:327
  84.1 0.0 copy-start.1
  84.2 21.6 %all_to_all.42 = bf16[8,128,512]{2,1,0:T(8,128)(2,1)S(1)} all-to-all(bf16[8,128,512]{2,1,0:T(8,128)(2,1)S(1)} %bitcast.18), channel_id=1, replica_groups=mesh['y'=4,'w'=2,'p'=2,'c'=2,'row'=4] {'y','w'}, dimensions={0} | all-to-all | bytes 2097152 | tf_op jit(solution)/shard_map/all_to_all | solution.py:432
  105.7 0.0 copy-done.1
  105.7 2.0 %shard_map.71 = bf16[512,640]{1,0:T(8,128)(2,1)S(1)} custom-call(s32[2]{0:T(128)S(1)} %copy-done.4, bf16[1024,512]{1,0:T(8,128)(2,1)S(1)} %bitcast.14, f32[256,2048]{1,0:T(8,128)S(1)} %get-tuple-element.28.slope, f32[256,512]{1,0:T(8,128)S(1)} %get-tuple-element.29.normed, f32[256,128]{1,0:T(8,128)S(1)} %get-tuple-element.30.inverse, ...), custom_call_target="tpu_custom_call" | custom-call | flops 1000000000 | bytes 1048576 | tf_op jit(solution)/shard_map/pallas_call | solution.py:327
  107.7 0.2 reshape.24
  107.9 22.7 %all_to_all.43 = bf16[128,4,640]{2,1,0:T(4,128)(2,1)S(1)} all-to-all(bf16[128,4,640]{2,1,0:T(4,128)(2,1)S(1)} %reshape.24), channel_id=1, replica_groups=mesh['y'=4,'w'=2,'p'=2,'c'=2,'row'=4] {'y','w','p','c','row'}, dimensions={0} | all-to-all | bytes 1310720 | tf_op jit(solution)/shard_map/all_to_all | solution.py:440
  130.6 0.1 reshape.25.got
  130.7 2.1 %shard_map.72 = f32[1024,512]{1,0:T(8,128)} custom-call(bf16[512,640]{1,0:T(8,128)(2,1)S(1)} %reshape.25.got), custom_call_target="tpu_custom_call" | custom-call | bytes 1048576 | tf_op jit(solution)/shard_map/pallas_call | solution.py:327
Async XLA Ops:
  0.0 5.5 %copy-start.6 = (s32[2,128]{1,0:T(2,128)S(1)}, s32[2,128]{1,0:T(2,128)}, u32[]{:S(2)}) copy-start(s32[2,128]{1,0:T(2,128)} %param.11) | copy-start | bytes 3076
  0.0 5.5 %copy-start.5 = (bf16[512,512]{1,0:T(8,128)(2,1)S(1)}, bf16[512,512]{1,0:T(8,128)(2,1)}, u32[]{:S(2)}) copy-start(bf16[512,512]{1,0:T(8,128)(2,1)} %w_outer.1) | copy-start | bytes 1572868
  0.0 5.5 %copy-start.2 = (bf16[2,128,512]{2,1,0:T(8,128)(2,1)S(1)}, bf16[2,128,512]{2,1,0:T(8,128)(2,1)}, u32[]{:S(2)}) copy-start(bf16[2,128,512]{2,1,0:T(8,128)(2,1)} %param.7) | copy-start | bytes 786436
  1.2 1.6 %copy-start = (bf16[512,2048]{1,0:T(8,128)(2,1)S(1)}, bf16[512,2048]{1,0:T(8,128)(2,1)}, u32[]{:S(2)}) copy-start(bf16[512,2048]{1,0:T(8,128)(2,1)} %w_inner.1) | copy-start | bytes 6291460
  2.8 0.9 copy-start.3
  22.6 27.0 %copy-start.4 = (s32[2]{0:T(128)S(1)}, s32[2]{0:T(128)}, u32[]{:S(2)}) copy-start(s32[2]{0:T(128)} %lengths.11) | copy-start | bytes 28
  46.6 6.0 %collective-permute-start = (bf16[2048,384]{1,0:T(8,128)(2,1)S(1)}, bf16[2048,384]{1,0:T(8,128)(2,1)S(1)}, u32[]{:S(2)}, u32[]{:S(2)}) collective-permute-start(bf16[2048,384]{1,0:T(8,128)(2,1)S(1)} %bitcast.9), channel_id=1, source_target_pairs={{0,4},{4,0},{1,5},{5,1},{2,6},{6,2},{3,7},{7,3},{8,12},{12,8},{9,1... | collective-permute-start | bytes 4718600 | tf_op jit(solution)/shard_map/ppermute | solution.py:380
  55.1 5.2 %collective-permute-start.3 = (f32[8,1024]{1,0:T(8,128)S(1)}, f32[8,1024]{1,0:T(8,128)S(1)}, u32[]{:S(2)}, u32[]{:S(2)}) collective-permute-start(f32[8,1024]{1,0:T(8,128)S(1)} %get-tuple-element.25.s0), channel_id=1, source_target_pairs={{0,48},{16,32},{32,16},{48,0},{64,112},{80,96},{96,80},{112,64},{1... | collective-permute-start | bytes 98312 | tf_op jit(solution)/shard_map/ppermute | solution.py:397
  55.4 4.8 %collective-permute-start.2 = (f32[8,1024]{1,0:T(8,128)S(1)}, f32[8,1024]{1,0:T(8,128)S(1)}, u32[]{:S(2)}, u32[]{:S(2)}) collective-permute-start(f32[8,1024]{1,0:T(8,128)S(1)} %get-tuple-element.25.s0), channel_id=1, source_target_pairs={{0,32},{16,48},{32,0},{48,16},{64,96},{80,112},{96,64},{112,80},{1... | collective-permute-start | bytes 98312 | tf_op jit(solution)/shard_map/ppermute | solution.py:397
  56.5 4.6 %collective-permute-start.1 = (f32[8,1024]{1,0:T(8,128)S(1)}, f32[8,1024]{1,0:T(8,128)S(1)}, u32[]{:S(2)}, u32[]{:S(2)}) collective-permute-start(f32[8,1024]{1,0:T(8,128)S(1)} %get-tuple-element.25.s0), channel_id=1, source_target_pairs={{0,16},{16,0},{32,48},{48,32},{64,80},{80,64},{96,112},{112,96},{1... | collective-permute-start | bytes 98312 | tf_op jit(solution)/shard_map/ppermute | solution.py:397
  62.5 8.6 %collective-permute-start.6 = (bf16[1024,128]{1,0:T(8,128)(2,1)S(1)}, bf16[1024,128]{1,0:T(8,128)(2,1)S(1)}, u32[]{:S(2)}, u32[]{:S(2)}) collective-permute-start(bf16[1024,128]{1,0:T(8,128)(2,1)S(1)} %get-tuple-element.26.grad_attn.g_own), channel_id=1, source_target_pairs={{0,12},{4,8},{8,4},{12,0},{1,13},{5,9},{9,5},{13,1},{2,14},{6,10},... | collective-permute-start | bytes 786440 | tf_op jit(solution)/shard_map/ppermute | solution.py:406
  64.3 6.8 %collective-permute-start.5 = (bf16[1024,128]{1,0:T(8,128)(2,1)S(1)}, bf16[1024,128]{1,0:T(8,128)(2,1)S(1)}, u32[]{:S(2)}, u32[]{:S(2)}) collective-permute-start(bf16[1024,128]{1,0:T(8,128)(2,1)S(1)} %get-tuple-element.26.grad_attn.g_own), channel_id=1, source_target_pairs={{0,4},{4,0},{8,12},{12,8},{1,5},{5,1},{9,13},{13,9},{2,6},{6,2},{1... | collective-permute-start | bytes 786440 | tf_op jit(solution)/shard_map/ppermute | solution.py:406
  64.4 12.3 %collective-permute-start.4 = (bf16[1024,128]{1,0:T(8,128)(2,1)S(1)}, bf16[1024,128]{1,0:T(8,128)(2,1)S(1)}, u32[]{:S(2)}, u32[]{:S(2)}) collective-permute-start(bf16[1024,128]{1,0:T(8,128)(2,1)S(1)} %get-tuple-element.26.grad_attn.g_own), channel_id=1, source_target_pairs={{0,8},{4,12},{8,0},{12,4},{1,9},{5,13},{9,1},{13,5},{2,10},{6,14},... | collective-permute-start | bytes 786440 | tf_op jit(solution)/shard_map/ppermute | solution.py:406
  84.1 21.6 %copy-start.1 = (bf16[512,2048]{1,0:T(8,128)(2,1)S(1)}, bf16[512,2048]{1,0:T(8,128)(2,1)}, u32[]{:S(2)}) copy-start(bf16[512,2048]{1,0:T(8,128)(2,1)} %w_inner.1) | copy-start | bytes 6291460

commit v3 on v2

--- a/solution.py
+++ b/solution.py
@@ -18,7 +18,8 @@
 F32 = jnp.float32
 BF16 = jnp.bfloat16
 SCALE = HD**-0.5
-VMEM_LIMIT = 24 * 2**20
+VMEM_LIMIT = 12 * 2**20
+PROJECT_LIMIT = 60 * 2**20
 
 
 def dot(a, b):
@@ -46,37 +47,45 @@
     return 0.5 * two_sigma * (1.0 + values - half * two_sigma)
 
 
-def project_kernel(events, w_part, pre, send, normed):
-    @pl.when(pl.program_id(0) == 0)
-    def _():
-        normed[...] = normalize(events[...].astype(F32))[0].astype(BF16)
-
-    values = dot(normed[...], w_part[...])
-    pre[...] = values
-    act = silu(values).astype(BF16)
-    for g in range(2):
-        for h in range(HEADS):
-            piece = act[g * BLK : (g + 1) * BLK, h * HD : (h + 1) * HD]
-            for p in range(2):
-                at = ((g * HEADS + h) * 2 + p) * BLK
-                send[at : at + BLK, :] = piece
-
-
-def gate_kernel(
-    events, grad_out, w_u, w_outer, ids, pre, slope, normed_out, inv_out, send_g, hot, ext
+def project_kernel(
+    events_hbm, grad_hbm, w_hbm, w_outer_hbm, send, events, grad_out, weights, w_outer, sems
 ):
+    copies = [pltpu.make_async_copy(events_hbm, events, sems.at[4])]
+    for part in (1, 2, 3, 0):
+        cols = slice(part * D, (part + 1) * D)
+        copies.append(pltpu.make_async_copy(w_hbm.at[:, cols], weights.at[part], sems.at[part]))
+    copies.append(pltpu.make_async_copy(w_outer_hbm, w_outer, sems.at[5]))
+    copies.append(pltpu.make_async_copy(grad_hbm, grad_out, sems.at[6]))
+    for copy in copies:
+        copy.start()
+    copies[0].wait()
+    normed = normalize(events[...].astype(F32))[0].astype(BF16)
+    for slot, part in enumerate((1, 2, 3, 0)):
+        copies[slot + 1].wait()
+        act = silu(dot(normed, weights[part])).astype(BF16)
+        if part == 0:
+            copies[5].wait()
+            copies[6].wait()
+            act = (dot_t(grad_out[...], w_outer[...]) * act.astype(F32)).astype(BF16)
+        for g in range(2):
+            for h in range(HEADS):
+                piece = act[g * BLK : (g + 1) * BLK, h * HD : (h + 1) * HD]
+                for p in range(2):
+                    at = ((g * HEADS + h) * 2 + p) * BLK
+                    send[at : at + BLK, slot * HD : (slot + 1) * HD] = piece
+
+
+def gate_kernel(events, grad_out, w_inner, w_outer, ids, slope, normed_out, inv_out, hot, ext):
     normed, inverse = normalize(events[...].astype(F32))
     normed_out[...] = normed
     inv_out[...] = jnp.broadcast_to(inverse, inv_out.shape)
-    values = dot(normed.astype(BF16), w_u[...])
-    grad_gated = dot_t(grad_out[...], w_outer[...])
-    prod = (grad_gated * silu(values).astype(BF16).astype(F32)).astype(BF16)
-    for g in range(2):
-        for h in range(HEADS):
-            at = (g * HEADS + h) * BLK
-            send_g[at : at + BLK, :] = prod[g * BLK : (g + 1) * BLK, h * HD : (h + 1) * HD]
-    slope[:, :D] = grad_gated * silu_slope(values)
-    slope[:, D:] = silu_slope(pre[...])
+    normed = normed.astype(BF16)
+    for part in range(4):
+        cols = slice(part * D, (part + 1) * D)
+        values = silu_slope(dot(normed, w_inner[:, cols]))
+        if part == 0:
+            values = values * dot_t(grad_out[...], w_outer[...])
+        slope[:, cols] = values
     count = 2 * BLK
     id_row = ids[...]
     id_cols = jnp.transpose(jnp.broadcast_to(id_row.astype(F32), (BLK, count))).astype(jnp.int32)
@@ -102,7 +111,7 @@
     )
 
 
-V_COLS, Q_COLS, K_COLS = (slice(i * HD, (i + 1) * HD) for i in range(3))
+V_COLS, Q_COLS, K_COLS, G_COLS = (slice(i * HD, (i + 1) * HD) for i in range(4))
 
 
 def my_place():
@@ -118,18 +127,21 @@
     return 1.0 / jnp.full((1, HD), length, jnp.int32).astype(F32)
 
 
-def query_mask(place, core, count):
-    row = lax.broadcasted_iota(jnp.int32, (count, 2 * BLK), 0)
-    lane = lax.broadcasted_iota(jnp.int32, (count, 2 * BLK), 1)
+def diagonal(place, core, rows_are_keys):
+    row = lax.broadcasted_iota(jnp.int32, (BLK, 2 * BLK), 0) + place[2] * BLK
+    lane = lax.broadcasted_iota(jnp.int32, (BLK, 2 * BLK), 1)
     col = lane + jnp.where(lane >= BLK, BLK, 0) + core * BLK
-    return (row >= BLK) | (col <= row + place[2] * BLK)
-
-
-def key_mask(place, core, count):
-    row = lax.broadcasted_iota(jnp.int32, (count, 2 * BLK), 0) - (count - BLK)
-    lane = lax.broadcasted_iota(jnp.int32, (count, 2 * BLK), 1)
-    col = lane + jnp.where(lane >= BLK, BLK, 0) + core * BLK
-    return (row < 0) | (row + place[2] * BLK <= col)
+    return row <= col if rows_are_keys else col <= row
+
+
+def mask_first(mask, values):
+    first = jnp.where(mask, values[:BLK, :], 0.0)
+    return jnp.concatenate([first, values[BLK:, :]], axis=0) if values.shape[0] > BLK else first
+
+
+def mask_last(mask, values):
+    last = jnp.where(mask, values[-BLK:, :], 0.0)
+    return jnp.concatenate([values[:-BLK, :], last], axis=0) if values.shape[0] > BLK else last
 
 
 def own_blocks(place, src, cols, dst):
@@ -140,24 +152,27 @@
 
 def forward_kernel(last, lengths, mine, *refs):
     place = my_place()
-    inv_len = inverse_of(my_length(lengths))
     if last:
-        theirs, before, grad, out, stats, queries = refs
+        theirs, before, out, stats, grad, queries = refs
         keys_of, core = theirs, 1 - place[1]
+        own_blocks(place, mine, G_COLS, grad)
+        out[...] = before[...]
     else:
         out, queries = refs
         keys_of, core = mine, place[1]
+        out[...] = jnp.zeros_like(out)
     own_blocks(place, mine, Q_COLS, queries)
-    out[...] = before[...] if last else jnp.zeros_like(out)
+    mask = diagonal(place, core, False)
     for j in range(8):
         keys = slice(j * 2 * BLK, (j + 1) * 2 * BLK)
         rows = slice(j * BLK, 8 * BLK)
         half = dot_t(queries[rows, :], keys_of[keys, K_COLS]) * (0.5 * SCALE)
         attn = half * jnp.tanh(half) + half
-        attn = jnp.where(query_mask(place, core, (8 - j) * BLK), attn, 0.0)
+        attn = mask_first(mask, attn)
         out[rows, :] += dot(attn.astype(BF16), keys_of[keys, V_COLS])
     if not last:
         return
+    inv_len = inverse_of(my_length(lengths))
     for m in range(8):
         rows = slice(m * BLK, (m + 1) * BLK)
         total = out[rows, :] * inv_len
@@ -214,27 +229,61 @@
     return two_sigma + half * (1.0 - t * t), half * two_sigma
 
 
-def grad_query_kernel(lengths, mine, theirs, grad_attn, ret, queries, total):
+def grad_query_kernel(last, lengths, mine, *refs):
     place = my_place()
-    inv_len = inverse_of(my_length(lengths))
+    if last:
+        theirs, grad_attn, before, ret, queries, total = refs
+        src, core = theirs, 1 - place[1]
+        total[...] = before[...]
+    else:
+        grad_attn, total, queries = refs
+        src, core = mine, place[1]
+        total[...] = jnp.zeros_like(total)
     own_blocks(place, mine, Q_COLS, queries)
-    total[...] = jnp.zeros_like(total)
+    mask = diagonal(place, core, False)
     for j in range(8):
         keys = slice(j * 2 * BLK, (j + 1) * 2 * BLK)
         rows = slice(j * BLK, 8 * BLK)
-        for src, core in ((mine, place[1]), (theirs, 1 - place[1])):
-            k = src[keys, K_COLS]
-            slope, _ = slopes(dot_t(queries[rows, :], k))
-            score = slope * dot_t(grad_attn[rows, :], src[keys, V_COLS])
-            score = jnp.where(query_mask(place, core, (8 - j) * BLK), score, 0.0)
-            total[rows, :] += dot(score.astype(BF16), k)
-    ret[...] = (total[...] * (0.5 * SCALE * inv_len)).astype(BF16)
+        k = src[keys, K_COLS]
+        slope, _ = slopes(dot_t(queries[rows, :], k))
+        score = slope * dot_t(grad_attn[rows, :], src[keys, V_COLS])
+        score = mask_first(mask, score)
+        total[rows, :] += dot(score.astype(BF16), k)
+    if last:
+        inv_len = inverse_of(my_length(lengths))
+        ret[...] = (total[...] * (0.5 * SCALE * inv_len)).astype(BF16)
+
+
+def packed_rows(j):
+    return slice(j * (j + 1) // 2 * BLK, (j + 1) * (j + 2) // 2 * BLK)
+
+
+def key_scores_kernel(other, mine, *refs):
+    place = my_place()
+    if other:
+        src, slope_out, attn_out, keys = refs
+        core = 1 - place[1]
+    else:
+        slope_out, attn_out, keys = refs
+        src, core = mine, place[1]
+    own_blocks(place, mine, K_COLS, keys)
+    mask = diagonal(place, core, True)
+    for j in range(8):
+        events = slice(j * 2 * BLK, (j + 1) * 2 * BLK)
+        rows = slice(0, (j + 1) * BLK)
+        slope, attn = slopes(dot_t(keys[rows, :], src[events, Q_COLS]))
+        slope_out[packed_rows(j), :] = mask_last(mask, slope)
+        attn_out[packed_rows(j), :] = mask_last(mask, attn).astype(BF16)
 
 
 def grad_key_kernel(
     lengths,
     mine,
     theirs,
+    slope_m,
+    attn_m,
+    slope_t,
+    attn_t,
     g_own,
     g_p,
     g_c,
@@ -244,7 +293,6 @@
     ret,
     mine_g,
     theirs_g,
-    keys,
     values,
     grad_k,
     grad_v,
@@ -252,7 +300,6 @@
     place = my_place()
     inv_len = inverse_of(my_length(lengths))
     p = place[0]
-    own_blocks(place, mine, K_COLS, keys)
     own_blocks(place, mine, V_COLS, values)
     for m in range(8):
         rows = slice(m * BLK, (m + 1) * BLK)
@@ -267,15 +314,14 @@
     for j in range(8):
         events = slice(j * 2 * BLK, (j + 1) * 2 * BLK)
         rows = slice(0, (j + 1) * BLK)
-        for src, src_g, core in ((mine, mine_g, place[1]), (theirs, theirs_g, 1 - place[1])):
-            q = src[events, Q_COLS]
+        for src, src_g, slope, attn in (
+            (mine, mine_g, slope_m, attn_m),
+            (theirs, theirs_g, slope_t, attn_t),
+        ):
             ga = src_g[events, :]
-            slope, attn = slopes(dot_t(keys[rows, :], q))
-            mask = key_mask(place, core, (j + 1) * BLK)
-            score = jnp.where(mask, slope * dot_t(values[rows, :], ga), 0.0)
-            attn = jnp.where(mask, attn, 0.0)
-            grad_k[rows, :] += dot(score.astype(BF16), q)
-            grad_v[rows, :] += dot(attn.astype(BF16), ga)
+            score = slope[packed_rows(j), :] * dot_t(values[rows, :], ga)
+            grad_k[rows, :] += dot(score.astype(BF16), src[events, Q_COLS])
+            grad_v[rows, :] += dot(attn[packed_rows(j), :], ga)
     ret[:, :HD] = normed_out[...]
     ret[:, HD : 2 * HD] = (grad_v[...] * inv_len).astype(BF16)
     ret[:, 2 * HD : 3 * HD] = grad_q[...]
@@ -335,82 +381,107 @@
     )(*args)
 
 
-def project(events, w_inner):
+def project(*args):
+    hbm = pl.BlockSpec(memory_space=pltpu.HBM)
+    vmem = pl.BlockSpec(memory_space=pltpu.VMEM)
     return pl.pallas_call(
         project_kernel,
-        grid=(3,),
-        out_shape=[
-            jax.ShapeDtypeStruct((2 * BLK, 3 * D), F32),
-            jax.ShapeDtypeStruct((16 * BLK, 3 * HD), BF16),
+        out_shape=jax.ShapeDtypeStruct((16 * BLK, 4 * HD), BF16),
+        in_specs=[hbm] * len(args),
+        out_specs=vmem,
+        scratch_shapes=[
+            pltpu.VMEM((2 * BLK, D), BF16),
+            pltpu.VMEM((2 * BLK, D), BF16),
+            pltpu.VMEM((4, D, D), BF16),
+            pltpu.VMEM((D, D), BF16),
+            pltpu.SemaphoreType.DMA((7,)),
         ],
-        in_specs=[
-            pl.BlockSpec((2 * BLK, D), lambda i: (0, 0)),
-            pl.BlockSpec((D, D), lambda i: (0, i + 1)),
-        ],
-        out_specs=[
-            pl.BlockSpec((2 * BLK, D), lambda i: (0, i)),
-            pl.BlockSpec((16 * BLK, HD), lambda i: (0, i)),
-        ],
-        scratch_shapes=[pltpu.VMEM((2 * BLK, D), BF16)],
-        compiler_params=pltpu.CompilerParams(vmem_limit_bytes=VMEM_LIMIT),
-    )(events, w_inner)
+        compiler_params=pltpu.CompilerParams(vmem_limit_bytes=PROJECT_LIMIT),
+    )(*args)
 
 
 def local(events, grad_out, w_inner, w_outer, valid_lengths, item_ids):
     events = events.reshape(2 * BLK, D)
     grad_out = grad_out.reshape(2 * BLK, D)
-    pre, send = project(events, w_inner)
+    rows_bf16, rows_f32 = ((1024, HD), BF16), ((1024, HD), F32)
+    swap_c = [(0, 1), (1, 0)]
+    send = project(events, grad_out, w_inner, w_outer)
     mine = lax.all_to_all(send, ("y", "w", "p"), 0, 0, tiled=True)
-    slope, normed, inverse, send_g, hot, ext = call(
+    slope, normed, inverse, hot, ext = call(
         gate_kernel,
         [
             ((2 * BLK, 4 * D), F32),
             ((2 * BLK, D), F32),
             ((2 * BLK, HD), F32),
-            ((8 * BLK, HD), BF16),
             ((CAP * 128, 2 * BLK), BF16),
             ((2 * BLK, EXT), BF16),
         ],
-        (events, grad_out, w_inner[:, :D], w_outer, item_ids.reshape(1, 2 * BLK), pre),
+        (events, grad_out, w_inner, w_outer, item_ids.reshape(1, 2 * BLK)),
         scalars=0,
-        flops=10**9,
-    )
-    grad = lax.all_to_all(send_g, ("y", "w"), 0, 0, tiled=True)
-    mine, grad = lax.optimization_barrier((mine, grad))
-    theirs = lax.ppermute(mine, "c", [(0, 1), (1, 0)])
-    queries = ((1024, HD), BF16)
+        flops=2 * 10**9,
+    )
+    mine, slope = lax.optimization_barrier((mine, slope))
+    theirs = lax.ppermute(mine, "c", swap_c)
     (attn_one,) = call(
         functools.partial(forward_kernel, False),
-        [((1024, HD), F32)],
+        [rows_f32],
         (valid_lengths, mine),
-        scratch=[queries],
+        scratch=[rows_bf16],
         flops=10**9,
     )
-    attn_out, stats = call(
+    score_shapes = [((36 * BLK, 2 * BLK), F32), ((36 * BLK, 2 * BLK), BF16)]
+    scores_m = call(
+        functools.partial(key_scores_kernel, False),
+        score_shapes,
+        (mine,),
+        scalars=0,
+        scratch=[rows_bf16],
+        flops=10**9,
+    )
+    theirs, scores_m, attn_one = lax.optimization_barrier((theirs, scores_m, attn_one))
+    attn_out, stats, grad = call(
         functools.partial(forward_kernel, True),
-        [((1024, HD), F32), ((8, 1024), F32)],
-        (valid_lengths, mine, theirs, attn_one, grad),
-        scratch=[queries],
+        [rows_f32, ((8, 1024), F32), rows_bf16],
+        (valid_lengths, mine, theirs, attn_one),
+        scratch=[rows_bf16],
         flops=10**9,
     )
     others = [
         lax.ppermute(stats, ("y", "w"), [(i, i ^ m) for i in range(8)]) for m in (1, 2, 3)
     ]
+    scores_t = call(
+        functools.partial(key_scores_kernel, True),
+        score_shapes,
+        (mine, theirs),
+        scalars=0,
+        scratch=[rows_bf16],
+        flops=10**9,
+    )
+    others, scores_t = lax.optimization_barrier((others, scores_t))
     grad_attn, normed_out = call(
         grad_attn_kernel,
-        [((1024, HD), BF16), ((1024, HD), BF16)],
+        [rows_bf16, rows_bf16],
         (valid_lengths, attn_out, grad, stats, *others),
         flops=10**7,
     )
-    grad_p, grad_c, grad_pc = [
-        lax.ppermute(grad_attn, ("p", "c"), [(i, i ^ m) for i in range(4)]) for m in (2, 1, 3)
+    grad_p, grad_c = [
+        lax.ppermute(grad_attn, ("p", "c"), [(i, i ^ m) for i in range(4)]) for m in (2, 1)
     ]
     (grad_q,) = call(
-        grad_query_kernel,
-        [((1024, HD), BF16)],
-        (valid_lengths, mine, theirs, grad_attn),
-        scratch=[queries, ((1024, HD), F32)],
-        flops=4 * 10**9,
+        functools.partial(grad_query_kernel, False),
+        [rows_f32],
+        (valid_lengths, mine, grad_attn),
+        scratch=[rows_bf16],
+        flops=2 * 10**9,
+    )
+    grad_p, grad_q = lax.optimization_barrier((grad_p, grad_q))
+    grad_pc = lax.ppermute(grad_p, "c", swap_c)
+    (grad_q,) = call(
+        functools.partial(grad_query_kernel, True),
+        [rows_bf16],
+        (valid_lengths, mine, theirs, grad_attn, grad_q),
+        scratch=[rows_bf16, rows_f32],
+        flops=2 * 10**9,
     )
     (ret,) = call(
         grad_key_kernel,
@@ -419,6 +490,8 @@
             valid_lengths,
             mine,
             theirs,
+            *scores_m,
+            *scores_t,
             grad_attn,
             grad_p,
             grad_c,
@@ -426,7 +499,7 @@
             normed_out,
             grad_q,
         ),
-        scratch=[((2048, HD), BF16)] * 2 + [queries] * 2 + [((1024, HD), F32)] * 2,
+        scratch=[((2048, HD), BF16)] * 2 + [rows_bf16] + [rows_f32] * 2,
         flops=6 * 10**9,
     )
     got = lax.all_to_all(ret, ("y", "w"), 0, 0, tiled=True)

time: 133 us -> 124 us (0.932)
  blocking collectives: 83.2 us -> 43.4 us
  waiting for transfers between devices: 8.51 us -> 26.4 us
  starting transfers between devices: 10.4 us -> 17.1 us
  Pallas kernels: 26.6 us -> 30.9 us
  local copies, waits for them, and re-layouts: 4.01 us -> 5.54 us
    all_to_all x2 -> x0, blocking collectives: 38.9 us -> none  [the longest x1 24 us: local(): mine = lax.all_to_all(send, ('y', 'w', 'p'), 0, 0, tiled=True)]
    all_to_all x0 -> x1, waiting for transfers between devices: none -> 23.6 us  [local(): mine = lax.all_to_all(send, ('y', 'w', 'p'), 0, 0, tiled=True)]
    all_to_all x0 -> x1, starting transfers between devices: none -> 7.73 us  [local(): mine = lax.all_to_all(send, ('y', 'w', 'p'), 0, 0, tiled=True)]
    ppermute x3 -> x2, waiting for transfers between devices: 5.69 us -> 2.71 us  [local(): lax.ppermute(grad_attn, ('p', 'c'), [(i, i ^ m) for i in range(4)])]
    unnamed x14 -> x26, local copies, waits for them, and re-layouts: 2.56 us -> 5.24 us
    pallas_call x1, Pallas kernels: 1.79 us -> 4.33 us  [project(): pl.pallas_call(project_kernel, out_shape=jax.ShapeDtypeStruct((16 * BLK,...]
    ppermute x3 -> x2, starting transfers between devices: 3.22 us -> 1.36 us  [local(): lax.ppermute(grad_attn, ('p', 'c'), [(i, i ^ m) for i in range(4)])]
    ppermute x3, waiting for transfers between devices: 1.84 us -> 0.01 us  [local(): lax.ppermute(stats, ('y', 'w'), [(i, i ^ m) for i in range(8)])]
  transfers between devices with their start and end apart: 7 -> 8, of which waited for: 4 -> 2; matrix products, arithmetic and copies ran while one was open for 0% -> 0% of each run, Pallas kernels for 6% -> 11%
where the time goes in v3:
time: 124 us
  blocking collectives  43.4 us (35%)
  Pallas kernels  30.9 us (25%)
  waiting for transfers between devices  26.4 us (21%)
  starting transfers between devices  17.1 us (14%)
  local copies, waits for them, and re-layouts  5.54 us (4%)
    pallas_call x11, Pallas kernels, call(): pl.pallas_call(kernel, out_shape=[jax.ShapeDtypeStruct(shape, dtype) for...  26.6 us
    all_to_all x1, waiting for transfers between devices, local(): mine = lax.all_to_all(send, ('y', 'w', 'p'), 0, 0, tiled=True)  23.6 us
    all_to_all x1, blocking collectives, local(): lax.all_to_all(rows.reshape(128, CAP, D + EXT), ('y', 'w', 'p', 'c', 'row...  21.9 us
    all_to_all x1, blocking collectives, local(): got = lax.all_to_all(ret, ('y', 'w'), 0, 0, tiled=True)  21.5 us
    all_to_all x1, starting transfers between devices, local(): mine = lax.all_to_all(send, ('y', 'w', 'p'), 0, 0, tiled=True)  7.73 us
    unnamed x26, local copies, waits for them, and re-layouts  5.24 us
    pallas_call x1, Pallas kernels, project(): pl.pallas_call(project_kernel, out_shape=jax.ShapeDtypeStruct((16 * BLK,...  4.33 us
    ppermute x3, starting transfers between devices, local(): lax.ppermute(stats, ('y', 'w'), [(i, i ^ m) for i in range(8)])  4.16 us
  transfers between devices with their start and end apart: 8, of which 2 were waited for; matrix products, arithmetic and copies ran while one was open for 0% of the time, Pallas kernels for 11%

profile of v3, /device:TPU:1, one launch (start us, length us, event | category | flops | bytes accessed | tf_op | source)
XLA Modules:
  0.0 123.6 jit_solution(13222801473143562397)
XLA Ops:
  0.0 4.3 %shard_map.64 = bf16[2048,512]{1,0:T(8,128)(2,1)} custom-call(bf16[256,512]{1,0:T(8,128)(2,1)} %bitcast.20, bf16[256,512]{1,0:T(8,128)(2,1)} %bitcast.16, bf16[512,2048]{1,0:T(8,128)(2,1)} %w_inner.3, bf16[512,512]{1,0:T(8,128)(2,1)} %w_outer.1), custom_call_target="tpu_custom_call" | custom-call | tf_op jit(solution)/shard_map/pallas_call | solution.py:387
  4.3 0.0 copy-start.4
  4.3 0.0 copy-start.5
  4.4 0.0 copy-start.12
  4.4 7.7 %all-to-all-start = ((bf16[16,128,512]{2,1,0:T(8,128)(2,1)}), bf16[16,128,512]{2,1,0:T(8,128)(2,1)S(1)}, u32[]{:S(2)}, u32[]{:S(2)}) async-start(bf16[16,128,512]{2,1,0:T(8,128)(2,1)} %bitcast.23), calls=%async_computation | async-start | bytes 4194304 | tf_op jit(solution)/shard_map/all_to_all | solution.py:409
  12.1 0.0 copy-done.4
  12.1 0.0 copy-done.5
  12.1 0.0 copy-done.12
  12.1 0.0 copy-start
  12.1 1.6 %copy-done = bf16[512,2048]{1,0:T(8,128)(2,1)S(1)} copy-done((bf16[512,2048]{1,0:T(8,128)(2,1)S(1)}, bf16[512,2048]{1,0:T(8,128)(2,1)}, u32[]{:S(2)}) %copy-start) | copy-done | bytes 2097176
  13.7 0.9 copy-done.8
  14.7 1.6 %shard_map.65 = (f32[256,2048]{1,0:T(8,128)S(1)}, f32[256,512]{1,0:T(8,128)S(1)}, f32[256,128]{1,0:T(8,128)S(1)}, bf16[512,256]{1,0:T(8,128)(2,1)S(1)}, bf16[256,128]{1,0:T(8,128)(2,1)S(1)}) custom-call(bf16[256,512]{1,0:T(8,128)(2,1)S(1)} %bitcast.21, bf16[256,512]{1,0:T(8,128)(2,1)S(1)} %bitcast.17, bf16[512,2048]{1,0:T(8,128)(2,1)S(1)} %copy-done, ...), custom_call_target="tpu_custom_call" | custom-call | flops 2000000000 | bytes 1048576 | tf_op jit(solution)/shard_map/pallas_call | solution.py:373
  16.3 0.0 copy-start.2
  16.3 1.3 %copy-done.2 = f32[256,2048]{1,0:T(8,128)} copy-done((f32[256,2048]{1,0:T(8,128)}, f32[256,2048]{1,0:T(8,128)S(1)}, u32[]{:S(2)}) %copy-start.2) | copy-done | bytes 2097176
  17.6 0.7 copy-done.6
  18.3 0.6 copy-done.9
  19.0 23.6 %all-to-all-done = bf16[16,128,512]{2,1,0:T(8,128)(2,1)S(1)} async-done(((bf16[16,128,512]{2,1,0:T(8,128)(2,1)}), bf16[16,128,512]{2,1,0:T(8,128)(2,1)S(1)}, u32[]{:S(2)}, u32[]{:S(2)}) %all-to-all-start) | async-done | bytes 2097184 | tf_op jit(solution)/shard_map/all_to_all | solution.py:409
  42.6 2.1 %collective-permute-start = (bf16[2048,512]{1,0:T(8,128)(2,1)S(1)}, bf16[2048,512]{1,0:T(8,128)(2,1)S(1)}, u32[]{:S(2)}, u32[]{:S(2)}) collective-permute-start(bf16[2048,512]{1,0:T(8,128)(2,1)S(1)} %bitcast.7), channel_id=1, source_target_pairs={{0,4},{4,0},{1,5},{5,1},{2,6},{6,2},{3,7},{7,3},{8,12},{12,8},{9,1... | collective-permute-start | bytes 6291464 | tf_op jit(solution)/shard_map/ppermute | solution.py:424
  44.7 2.0 %shard_map.66 = (f32[4608,256]{1,0:T(8,128)S(1)}, bf16[4608,256]{1,0:T(8,128)(2,1)S(1)}) custom-call(bf16[2048,512]{1,0:T(8,128)(2,1)S(1)} %bitcast.8), custom_call_target="tpu_custom_call" | custom-call | flops 1000000000 | bytes 1048576 | tf_op jit(solution)/shard_map/pallas_call | solution.py:373
  46.8 0.0 copy-done.11
  46.8 2.0 %shard_map.67.refs_1_ = f32[1024,128]{1,0:T(8,128)S(1)} custom-call(s32[2]{0:T(128)S(1)} %copy-done.11, bf16[2048,512]{1,0:T(8,128)(2,1)S(1)} %bitcast.9), custom_call_target="tpu_custom_call" | custom-call | flops 1000000000 | bytes 1048576 | tf_op jit(solution)/shard_map/pallas_call | solution.py:373
  48.8 0.0 collective-permute-done.refs_0_.theirs
  48.8 2.5 %shard_map.68 = (f32[1024,128]{1,0:T(8,128)S(1)}, f32[8,1024]{1,0:T(8,128)S(1)}, bf16[1024,128]{1,0:T(8,128)(2,1)S(1)}) custom-call(s32[2]{0:T(128)S(1)} %copy-done.11, bf16[2048,512]{1,0:T(8,128)(2,1)S(1)} %bitcast.10, bf16[2048,512]{1,0:T(8,128)(2,1)S(1)} %collective-permute-done.refs_0_.theirs, f32[1024,128]{1,0:T(8,128)S(1)} %shard_map.67.refs_1_), custom_call_target="tpu_custom_call" | custom-call | flops 1000000000 | bytes 1048576 | tf_op jit(solution)/shard_map/pallas_call | solution.py:373
  51.3 0.3 collective-permute-start.3
  51.6 0.2 collective-permute-start.2
  51.7 3.7 %collective-permute-start.1 = (f32[8,1024]{1,0:T(8,128)S(1)}, f32[8,1024]{1,0:T(8,128)S(1)}, u32[]{:S(2)}, u32[]{:S(2)}) collective-permute-start(f32[8,1024]{1,0:T(8,128)S(1)} %get-tuple-element.40.s0), channel_id=1, source_target_pairs={{0,16},{16,0},{32,48},{48,32},{64,80},{80,64},{96,112},{112,96},{1... | collective-permute-start | bytes 98312 | tf_op jit(solution)/shard_map/ppermute | solution.py:450
  55.5 2.1 %shard_map.69 = (f32[4608,256]{1,0:T(8,128)S(1)}, bf16[4608,256]{1,0:T(8,128)(2,1)S(1)}) custom-call(bf16[2048,512]{1,0:T(8,128)(2,1)S(1)} %bitcast.11, bf16[2048,512]{1,0:T(8,128)(2,1)S(1)} %collective-permute-done.refs_0_.theirs), custom_call_target="tpu_custom_call" | custom-call | flops 1000000000 | bytes 1048576 | tf_op jit(solution)/shard_map/pallas_call | solution.py:373
  57.5 0.0 collective-permute-done.3.s3
  57.5 0.0 collective-permute-done.2.s2
  57.5 0.0 collective-permute-done.1.s1
  57.6 1.4 %shard_map.70 = (bf16[1024,128]{1,0:T(8,128)(2,1)S(1)}, bf16[1024,128]{1,0:T(8,128)(2,1)S(1)}) custom-call(s32[2]{0:T(128)S(1)} %copy-done.11, f32[1024,128]{1,0:T(8,128)S(1)} %get-tuple-element.45.attn_out, bf16[1024,128]{1,0:T(8,128)(2,1)S(1)} %get-tuple-element.46.grad, f32[8,1024]{1,0:T(8,128)S(1)} %get-tuple-element.40.s0, ...), custom_call_target="tpu_custom_call" | custom-call | flops 10000000 | bytes 1048576 | tf_op jit(solution)/shard_map/pallas_call | solution.py:373
  59.0 0.1 collective-permute-start.4
  59.1 1.3 %collective-permute-start.5 = (bf16[1024,128]{1,0:T(8,128)(2,1)S(1)}, bf16[1024,128]{1,0:T(8,128)(2,1)S(1)}, u32[]{:S(2)}, u32[]{:S(2)}) collective-permute-start(bf16[1024,128]{1,0:T(8,128)(2,1)S(1)} %get-tuple-element.50.refs_0_.refs_1_.g_own), channel_id=1, source_target_pairs={{0,4},{4,0},{8,12},{12,8},{1,5},{5,1},{9,13},{13,9},{2,6},{6,2},{1... | collective-permute-start | bytes 786440 | tf_op jit(solution)/shard_map/ppermute | solution.py:468
  60.3 2.9 %shard_map.71.refs_2_ = f32[1024,128]{1,0:T(8,128)S(1)} custom-call(s32[2]{0:T(128)S(1)} %copy-done.11, bf16[2048,512]{1,0:T(8,128)(2,1)S(1)} %bitcast.12, bf16[1024,128]{1,0:T(8,128)(2,1)S(1)} %get-tuple-element.50.refs_0_.refs_1_.g_own), custom_call_target="tpu_custom_call" | custom-call | flops 2000000000 | bytes 1048576 | tf_op jit(solution)/shard_map/pallas_call | solution.py:373
  63.3 2.7 %collective-permute-done.4.g_p = bf16[1024,128]{1,0:T(8,128)(2,1)S(1)} collective-permute-done((bf16[1024,128]{1,0:T(8,128)(2,1)S(1)}, bf16[1024,128]{1,0:T(8,128)(2,1)S(1)}, u32[]{:S(2)}, u32[]{:S(2)}) %collective-permute-start.4) | collective-permute-done | bytes 262176 | tf_op jit(solution)/shard_map/ppermute | solution.py:468
  66.0 1.8 %collective-permute-start.6 = (bf16[1024,128]{1,0:T(8,128)(2,1)S(1)}, bf16[1024,128]{1,0:T(8,128)(2,1)S(1)}, u32[]{:S(2)}, u32[]{:S(2)}) collective-permute-start(bf16[1024,128]{1,0:T(8,128)(2,1)S(1)} %collective-permute-done.4.g_p), channel_id=1, source_target_pairs={{0,4},{4,0},{1,5},{5,1},{2,6},{6,2},{3,7},{7,3},{8,12},{12,8},{9,1... | collective-permute-start | bytes 786440 | tf_op jit(solution)/shard_map/ppermute | solution.py:478
  67.8 3.0 %shard_map.72.grad_q = bf16[1024,128]{1,0:T(8,128)(2,1)S(1)} custom-call(s32[2]{0:T(128)S(1)} %copy-done.11, bf16[2048,512]{1,0:T(8,128)(2,1)S(1)} %bitcast.13, bf16[2048,512]{1,0:T(8,128)(2,1)S(1)} %collective-permute-done.refs_0_.theirs, bf16[1024,128]{1,0:T(8,128)(2,1)S(1)} %get-tuple-element.50.refs_0_.refs_1_.g_own, f32[1024,128]{1,0:T(8,128)S(1)} %shard_map.71.refs_2_), custom_call_target="tpu_custom_call" | custom-call | flops 2000000000 | bytes 1048576 | tf_op jit(solution)/shard_map/pallas_call | solution.py:373
  70.8 0.0 collective-permute-done.5.g_c
  70.8 0.0 collective-permute-done.6.g_pc
  70.9 4.9 %shard_map.73 = bf16[1024,512]{1,0:T(8,128)(2,1)S(1)} custom-call(s32[2]{0:T(128)S(1)} %copy-done.11, bf16[2048,512]{1,0:T(8,128)(2,1)S(1)} %bitcast.14, bf16[2048,512]{1,0:T(8,128)(2,1)S(1)} %collective-permute-done.refs_0_.theirs, f32[4608,256]{1,0:T(8,128)S(1)} %get-tuple-element.37.slope_m, bf16[4608,256]{1,0:T(8,128)(2,1)S(1)} %get-tuple-element.38.attn_m, ...), custom_call_target="tpu_custom_call" | custom-call | flops 6000000000 | bytes 1048576 | tf_op jit(solution)/shard_map/pallas_call | solution.py:373
  75.8 0.0 copy-start.1
  75.8 21.5 %all_to_all.28 = bf16[8,128,512]{2,1,0:T(8,128)(2,1)S(1)} all-to-all(bf16[8,128,512]{2,1,0:T(8,128)(2,1)S(1)} %bitcast.19), channel_id=1, replica_groups=mesh['y'=4,'w'=2,'p'=2,'c'=2,'row'=4] {'y','w'}, dimensions={0} | all-to-all | bytes 2097152 | tf_op jit(solution)/shard_map/all_to_all | solution.py:505
  97.3 0.0 copy-done.7
  97.3 2.0 %shard_map.74 = bf16[512,640]{1,0:T(8,128)(2,1)S(1)} custom-call(s32[2]{0:T(128)S(1)} %copy-done.11, bf16[1024,512]{1,0:T(8,128)(2,1)S(1)} %bitcast.15, f32[256,2048]{1,0:T(8,128)S(1)} %copy-done.3, f32[256,512]{1,0:T(8,128)S(1)} %get-tuple-element.55.normed, f32[256,128]{1,0:T(8,128)S(1)} %get-tuple-element.56.inverse, bf16[256,512]{1,0:T(8,128)(2,1)S(1)} %bitcast.18, ...), custom_call_target="tpu_custom_call" | custom-call | flops 1000000000 | bytes 1048576 | tf_op jit(solution)/shard_map/pallas_call | solution.py:373
  99.3 0.2 reshape.22
  99.5 21.9 %all_to_all.29 = bf16[128,4,640]{2,1,0:T(4,128)(2,1)S(1)} all-to-all(bf16[128,4,640]{2,1,0:T(4,128)(2,1)S(1)} %reshape.22), channel_id=1, replica_groups=mesh['y'=4,'w'=2,'p'=2,'c'=2,'row'=4] {'y','w','p','c','row'}, dimensions={0} | all-to-all | bytes 1310720 | tf_op jit(solution)/shard_map/all_to_all | solution.py:513
  121.4 0.1 reshape.23.got
  121.5 2.1 %shard_map.75 = f32[1024,512]{1,0:T(8,128)} custom-call(bf16[512,640]{1,0:T(8,128)(2,1)S(1)} %reshape.23.got), custom_call_target="tpu_custom_call" | custom-call | bytes 1048576 | tf_op jit(solution)/shard_map/pallas_call | solution.py:373
  (10 shorter events, 0.0 us)
Async XLA Ops:
  4.3 7.8 %copy-start.4 = (bf16[2,128,512]{2,1,0:T(8,128)(2,1)S(1)}, bf16[2,128,512]{2,1,0:T(8,128)(2,1)}, u32[]{:S(2)}) copy-start(bf16[2,128,512]{2,1,0:T(8,128)(2,1)} %param.7) | copy-start | bytes 786436
  4.3 7.8 %copy-start.5 = (bf16[512,512]{1,0:T(8,128)(2,1)S(1)}, bf16[512,512]{1,0:T(8,128)(2,1)}, u32[]{:S(2)}) copy-start(bf16[512,512]{1,0:T(8,128)(2,1)} %w_outer.1) | copy-start | bytes 1572868
  4.4 7.8 %copy-start.12 = (s32[2,128]{1,0:T(2,128)S(1)}, s32[2,128]{1,0:T(2,128)}, u32[]{:S(2)}) copy-start(s32[2,128]{1,0:T(2,128)} %param.11) | copy-start | bytes 3076
  4.4 38.2 %all-to-all-start = ((bf16[16,128,512]{2,1,0:T(8,128)(2,1)}), bf16[16,128,512]{2,1,0:T(8,128)(2,1)S(1)}, u32[]{:S(2)}, u32[]{:S(2)}) async-start(bf16[16,128,512]{2,1,0:T(8,128)(2,1)} %bitcast.23), calls=%async_computation | async-start | bytes 4194304 | tf_op jit(solution)/shard_map/all_to_all | solution.py:409
  12.1 1.6 %copy-start = (bf16[512,2048]{1,0:T(8,128)(2,1)S(1)}, bf16[512,2048]{1,0:T(8,128)(2,1)}, u32[]{:S(2)}) copy-start(bf16[512,2048]{1,0:T(8,128)(2,1)} %w_inner.3) | copy-start | bytes 6291460
  13.7 0.9 copy-start.8
  16.3 1.3 %copy-start.2 = (f32[256,2048]{1,0:T(8,128)}, f32[256,2048]{1,0:T(8,128)S(1)}, u32[]{:S(2)}) copy-start(f32[256,2048]{1,0:T(8,128)S(1)} %get-tuple-element.54.slope) | copy-start | bytes 6291460
  17.6 0.7 copy-start.6
  18.3 0.6 copy-start.9
  19.0 27.8 %copy-start.11 = (s32[2]{0:T(128)S(1)}, s32[2]{0:T(128)}, u32[]{:S(2)}) copy-start(s32[2]{0:T(128)} %lengths.13) | copy-start | bytes 28
  42.6 6.2 %collective-permute-start = (bf16[2048,512]{1,0:T(8,128)(2,1)S(1)}, bf16[2048,512]{1,0:T(8,128)(2,1)S(1)}, u32[]{:S(2)}, u32[]{:S(2)}) collective-permute-start(bf16[2048,512]{1,0:T(8,128)(2,1)S(1)} %bitcast.7), channel_id=1, source_target_pairs={{0,4},{4,0},{1,5},{5,1},{2,6},{6,2},{3,7},{7,3},{8,12},{12,8},{9,1... | collective-permute-start | bytes 6291464 | tf_op jit(solution)/shard_map/ppermute | solution.py:424
  51.3 6.2 %collective-permute-start.3 = (f32[8,1024]{1,0:T(8,128)S(1)}, f32[8,1024]{1,0:T(8,128)S(1)}, u32[]{:S(2)}, u32[]{:S(2)}) collective-permute-start(f32[8,1024]{1,0:T(8,128)S(1)} %get-tuple-element.40.s0), channel_id=1, source_target_pairs={{0,48},{16,32},{32,16},{48,0},{64,112},{80,96},{96,80},{112,64},{1... | collective-permute-start | bytes 98312 | tf_op jit(solution)/shard_map/ppermute | solution.py:450
  51.6 6.0 %collective-permute-start.2 = (f32[8,1024]{1,0:T(8,128)S(1)}, f32[8,1024]{1,0:T(8,128)S(1)}, u32[]{:S(2)}, u32[]{:S(2)}) collective-permute-start(f32[8,1024]{1,0:T(8,128)S(1)} %get-tuple-element.40.s0), channel_id=1, source_target_pairs={{0,32},{16,48},{32,0},{48,16},{64,96},{80,112},{96,64},{112,80},{1... | collective-permute-start | bytes 98312 | tf_op jit(solution)/shard_map/ppermute | solution.py:450
  51.7 5.8 %collective-permute-start.1 = (f32[8,1024]{1,0:T(8,128)S(1)}, f32[8,1024]{1,0:T(8,128)S(1)}, u32[]{:S(2)}, u32[]{:S(2)}) collective-permute-start(f32[8,1024]{1,0:T(8,128)S(1)} %get-tuple-element.40.s0), channel_id=1, source_target_pairs={{0,16},{16,0},{32,48},{48,32},{64,80},{80,64},{96,112},{112,96},{1... | collective-permute-start | bytes 98312 | tf_op jit(solution)/shard_map/ppermute | solution.py:450
  59.0 7.0 %collective-permute-start.4 = (bf16[1024,128]{1,0:T(8,128)(2,1)S(1)}, bf16[1024,128]{1,0:T(8,128)(2,1)S(1)}, u32[]{:S(2)}, u32[]{:S(2)}) collective-permute-start(bf16[1024,128]{1,0:T(8,128)(2,1)S(1)} %get-tuple-element.50.refs_0_.refs_1_.g_own), channel_id=1, source_target_pairs={{0,8},{4,12},{8,0},{12,4},{1,9},{5,13},{9,1},{13,5},{2,10},{6,14},... | collective-permute-start | bytes 786440 | tf_op jit(solution)/shard_map/ppermute | solution.py:468
  59.1 11.7 %collective-permute-start.5 = (bf16[1024,128]{1,0:T(8,128)(2,1)S(1)}, bf16[1024,128]{1,0:T(8,128)(2,1)S(1)}, u32[]{:S(2)}, u32[]{:S(2)}) collective-permute-start(bf16[1024,128]{1,0:T(8,128)(2,1)S(1)} %get-tuple-element.50.refs_0_.refs_1_.g_own), channel_id=1, source_target_pairs={{0,4},{4,0},{8,12},{12,8},{1,5},{5,1},{9,13},{13,9},{2,6},{6,2},{1... | collective-permute-start | bytes 786440 | tf_op jit(solution)/shard_map/ppermute | solution.py:468
  66.0 4.8 %collective-permute-start.6 = (bf16[1024,128]{1,0:T(8,128)(2,1)S(1)}, bf16[1024,128]{1,0:T(8,128)(2,1)S(1)}, u32[]{:S(2)}, u32[]{:S(2)}) collective-permute-start(bf16[1024,128]{1,0:T(8,128)(2,1)S(1)} %collective-permute-done.4.g_p), channel_id=1, source_target_pairs={{0,4},{4,0},{1,5},{5,1},{2,6},{6,2},{3,7},{7,3},{8,12},{12,8},{9,1... | collective-permute-start | bytes 786440 | tf_op jit(solution)/shard_map/ppermute | solution.py:478
  70.8 26.4 %copy-start.3 = (f32[256,2048]{1,0:T(8,128)S(1)}, f32[256,2048]{1,0:T(8,128)}, u32[]{:S(2)}) copy-start(f32[256,2048]{1,0:T(8,128)} %copy-done.2) | copy-start | bytes 6291460
  70.8 26.4 %copy-start.7 = (bf16[512,256]{1,0:T(8,128)(2,1)S(1)}, bf16[512,256]{1,0:T(8,128)(2,1)}, u32[]{:S(2)}) copy-start(bf16[512,256]{1,0:T(8,128)(2,1)} %copy-done.6) | copy-start | bytes 786436
  70.9 26.4 %copy-start.10 = (bf16[256,128]{1,0:T(8,128)(2,1)S(1)}, bf16[256,128]{1,0:T(8,128)(2,1)}, u32[]{:S(2)}) copy-start(bf16[256,128]{1,0:T(8,128)(2,1)} %copy-done.9) | copy-start | bytes 196612
  75.8 21.5 %copy-start.1 = (bf16[512,2048]{1,0:T(8,128)(2,1)S(1)}, bf16[512,2048]{1,0:T(8,128)(2,1)}, u32[]{:S(2)}) copy-start(bf16[512,2048]{1,0:T(8,128)(2,1)} %w_inner.3) | copy-start | bytes 6291460

commit v4 on v3

--- a/solution.py
+++ b/solution.py
@@ -48,7 +48,7 @@
 
 
 def project_kernel(
-    events_hbm, grad_hbm, w_hbm, w_outer_hbm, send, events, grad_out, weights, w_outer, sems
+    events_hbm, grad_hbm, w_hbm, w_outer_hbm, send, events, grad_out, weights, w_outer, parts, sems
 ):
     copies = [pltpu.make_async_copy(events_hbm, events, sems.at[4])]
     for part in (1, 2, 3, 0):
@@ -58,6 +58,7 @@
     copies.append(pltpu.make_async_copy(grad_hbm, grad_out, sems.at[6]))
     for copy in copies:
         copy.start()
+    leaving = []
     copies[0].wait()
     normed = normalize(events[...].astype(F32))[0].astype(BF16)
     for slot, part in enumerate((1, 2, 3, 0)):
@@ -72,7 +73,12 @@
                 piece = act[g * BLK : (g + 1) * BLK, h * HD : (h + 1) * HD]
                 for p in range(2):
                     at = ((g * HEADS + h) * 2 + p) * BLK
-                    send[at : at + BLK, slot * HD : (slot + 1) * HD] = piece
+                    parts[slot, at : at + BLK, :] = piece
+        cols = slice(slot * HD, (slot + 1) * HD)
+        leaving.append(pltpu.make_async_copy(parts.at[slot], send.at[:, cols], sems.at[7 + slot]))
+        leaving[-1].start()
+    for copy in leaving:
+        copy.wait()
 
 
 def gate_kernel(events, grad_out, w_inner, w_outer, ids, slope, normed_out, inv_out, hot, ext):
@@ -229,29 +235,21 @@
     return two_sigma + half * (1.0 - t * t), half * two_sigma
 
 
-def grad_query_kernel(last, lengths, mine, *refs):
+def grad_query_kernel(lengths, mine, theirs, grad_attn, ret, queries, total):
     place = my_place()
-    if last:
-        theirs, grad_attn, before, ret, queries, total = refs
-        src, core = theirs, 1 - place[1]
-        total[...] = before[...]
-    else:
-        grad_attn, total, queries = refs
-        src, core = mine, place[1]
-        total[...] = jnp.zeros_like(total)
+    total[...] = jnp.zeros_like(total)
     own_blocks(place, mine, Q_COLS, queries)
-    mask = diagonal(place, core, False)
+    masks = [diagonal(place, place[1], False), diagonal(place, 1 - place[1], False)]
     for j in range(8):
         keys = slice(j * 2 * BLK, (j + 1) * 2 * BLK)
         rows = slice(j * BLK, 8 * BLK)
-        k = src[keys, K_COLS]
-        slope, _ = slopes(dot_t(queries[rows, :], k))
-        score = slope * dot_t(grad_attn[rows, :], src[keys, V_COLS])
-        score = mask_first(mask, score)
-        total[rows, :] += dot(score.astype(BF16), k)
-    if last:
-        inv_len = inverse_of(my_length(lengths))
-        ret[...] = (total[...] * (0.5 * SCALE * inv_len)).astype(BF16)
+        for src, mask in zip((mine, theirs), masks):
+            k = src[keys, K_COLS]
+            slope, _ = slopes(dot_t(queries[rows, :], k))
+            score = slope * dot_t(grad_attn[rows, :], src[keys, V_COLS])
+            total[rows, :] += dot(mask_first(mask, score).astype(BF16), k)
+    inv_len = inverse_of(my_length(lengths))
+    ret[...] = (total[...] * (0.5 * SCALE * inv_len)).astype(BF16)
 
 
 def packed_rows(j):
@@ -276,56 +274,38 @@
         attn_out[packed_rows(j), :] = mask_last(mask, attn).astype(BF16)
 
 
-def grad_key_kernel(
-    lengths,
-    mine,
-    theirs,
-    slope_m,
-    attn_m,
-    slope_t,
-    attn_t,
-    g_own,
-    g_p,
-    g_c,
-    g_pc,
-    normed_out,
-    grad_q,
-    ret,
-    mine_g,
-    theirs_g,
-    values,
-    grad_k,
-    grad_v,
-):
+def grad_key_kernel(last, lengths, mine, *refs):
     place = my_place()
-    inv_len = inverse_of(my_length(lengths))
     p = place[0]
+    if last:
+        theirs, slope, attn, g_here, g_there, k_before, v_before, normed_out, grad_q, *refs = refs
+        ret, src_g, values, grad_k, grad_v = refs
+        src = theirs
+        grad_k[...] = k_before[...]
+        grad_v[...] = v_before[...]
+    else:
+        slope, attn, g_here, g_there, grad_k, grad_v, src_g, values = refs
+        src = mine
+        grad_k[...] = jnp.zeros_like(grad_k)
+        grad_v[...] = jnp.zeros_like(grad_v)
     own_blocks(place, mine, V_COLS, values)
     for m in range(8):
         rows = slice(m * BLK, (m + 1) * BLK)
-        here = pl.multiple_of((2 * m + p) * BLK, BLK)
-        there = pl.multiple_of((2 * m + 1 - p) * BLK, BLK)
-        mine_g[pl.ds(here, BLK), :] = g_own[rows, :]
-        mine_g[pl.ds(there, BLK), :] = g_p[rows, :]
-        theirs_g[pl.ds(here, BLK), :] = g_c[rows, :]
-        theirs_g[pl.ds(there, BLK), :] = g_pc[rows, :]
-    grad_k[...] = jnp.zeros_like(grad_k)
-    grad_v[...] = jnp.zeros_like(grad_v)
+        src_g[pl.ds(pl.multiple_of((2 * m + p) * BLK, BLK), BLK), :] = g_here[rows, :]
+        src_g[pl.ds(pl.multiple_of((2 * m + 1 - p) * BLK, BLK), BLK), :] = g_there[rows, :]
     for j in range(8):
         events = slice(j * 2 * BLK, (j + 1) * 2 * BLK)
         rows = slice(0, (j + 1) * BLK)
-        for src, src_g, slope, attn in (
-            (mine, mine_g, slope_m, attn_m),
-            (theirs, theirs_g, slope_t, attn_t),
-        ):
-            ga = src_g[events, :]
-            score = slope[packed_rows(j), :] * dot_t(values[rows, :], ga)
-            grad_k[rows, :] += dot(score.astype(BF16), src[events, Q_COLS])
-            grad_v[rows, :] += dot(attn[packed_rows(j), :], ga)
-    ret[:, :HD] = normed_out[...]
-    ret[:, HD : 2 * HD] = (grad_v[...] * inv_len).astype(BF16)
-    ret[:, 2 * HD : 3 * HD] = grad_q[...]
-    ret[:, 3 * HD :] = (grad_k[...] * (0.5 * SCALE * inv_len)).astype(BF16)
+        ga = src_g[events, :]
+        score = slope[packed_rows(j), :] * dot_t(values[rows, :], ga)
+        grad_k[rows, :] += dot(score.astype(BF16), src[events, Q_COLS])
+        grad_v[rows, :] += dot(attn[packed_rows(j), :], ga)
+    if last:
+        inv_len = inverse_of(my_length(lengths))
+        ret[:, :HD] = normed_out[...]
+        ret[:, HD : 2 * HD] = (grad_v[...] * inv_len).astype(BF16)
+        ret[:, 2 * HD : 3 * HD] = grad_q[...]
+        ret[:, 3 * HD :] = (grad_k[...] * (0.5 * SCALE * inv_len)).astype(BF16)
 
 
 def finish_kernel(
@@ -356,15 +336,19 @@
     send[:, D:] = dot(hot[...], ext[...]).astype(BF16)
 
 
-def table_kernel(got, table):
+def table_kernel(got, table, stage, sems):
     packed = jnp.transpose(got[:, D:].astype(F32))
     dest = ((packed[0:1, :] - 1.0) * 32.0 + packed[1:2, :]).astype(jnp.int32)
-    rows = 256
-    for i in range(ROWS_DEV // rows):
-        hot = jnp.where(
-            lax.broadcasted_iota(jnp.int32, (rows, got.shape[0]), 0) == dest - i * rows, 1.0, 0.0
-        ).astype(BF16)
-        table[i * rows : (i + 1) * rows, :] = dot(hot, got[:, :D])
+    leaving = []
+    for i in range(ROWS_DEV // BLK):
+        rows = slice(i * BLK, (i + 1) * BLK)
+        row = lax.broadcasted_iota(jnp.int32, (BLK, got.shape[0]), 0) + i * BLK
+        hot = jnp.where(row == dest, 1.0, 0.0).astype(BF16)
+        stage[rows, :] = dot(hot, got[:, :D])
+        leaving.append(pltpu.make_async_copy(stage.at[rows], table.at[rows], sems.at[i]))
+        leaving[-1].start()
+    for copy in leaving:
+        copy.wait()
 
 
 def call(kernel, outs, args, scalars=1, scratch=(), flops=0):
@@ -383,18 +367,18 @@
 
 def project(*args):
     hbm = pl.BlockSpec(memory_space=pltpu.HBM)
-    vmem = pl.BlockSpec(memory_space=pltpu.VMEM)
     return pl.pallas_call(
         project_kernel,
         out_shape=jax.ShapeDtypeStruct((16 * BLK, 4 * HD), BF16),
         in_specs=[hbm] * len(args),
-        out_specs=vmem,
+        out_specs=hbm,
         scratch_shapes=[
             pltpu.VMEM((2 * BLK, D), BF16),
             pltpu.VMEM((2 * BLK, D), BF16),
             pltpu.VMEM((4, D, D), BF16),
             pltpu.VMEM((D, D), BF16),
-            pltpu.SemaphoreType.DMA((7,)),
+            pltpu.VMEM((4, 16 * BLK, HD), BF16),
+            pltpu.SemaphoreType.DMA((11,)),
         ],
         compiler_params=pltpu.CompilerParams(vmem_limit_bytes=PROJECT_LIMIT),
     )(*args)
@@ -468,39 +452,38 @@
         lax.ppermute(grad_attn, ("p", "c"), [(i, i ^ m) for i in range(4)]) for m in (2, 1)
     ]
     (grad_q,) = call(
-        functools.partial(grad_query_kernel, False),
-        [rows_f32],
-        (valid_lengths, mine, grad_attn),
-        scratch=[rows_bf16],
-        flops=2 * 10**9,
+        grad_query_kernel,
+        [rows_bf16],
+        (valid_lengths, mine, theirs, grad_attn),
+        scratch=[rows_bf16, rows_f32],
+        flops=4 * 10**9,
     )
     grad_p, grad_q = lax.optimization_barrier((grad_p, grad_q))
     grad_pc = lax.ppermute(grad_p, "c", swap_c)
-    (grad_q,) = call(
-        functools.partial(grad_query_kernel, True),
-        [rows_bf16],
-        (valid_lengths, mine, theirs, grad_attn, grad_q),
-        scratch=[rows_bf16, rows_f32],
-        flops=2 * 10**9,
+    grad_k, grad_v = call(
+        functools.partial(grad_key_kernel, False),
+        [rows_f32, rows_f32],
+        (valid_lengths, mine, *scores_m, grad_attn, grad_p),
+        scratch=[((2048, HD), BF16), rows_bf16],
+        flops=3 * 10**9,
     )
     (ret,) = call(
-        grad_key_kernel,
+        functools.partial(grad_key_kernel, True),
         [((1024, 4 * HD), BF16)],
         (
             valid_lengths,
             mine,
             theirs,
-            *scores_m,
             *scores_t,
-            grad_attn,
-            grad_p,
             grad_c,
             grad_pc,
+            grad_k,
+            grad_v,
             normed_out,
             grad_q,
         ),
-        scratch=[((2048, HD), BF16)] * 2 + [rows_bf16] + [rows_f32] * 2,
-        flops=6 * 10**9,
+        scratch=[((2048, HD), BF16), rows_bf16, rows_f32, rows_f32],
+        flops=3 * 10**9,
     )
     got = lax.all_to_all(ret, ("y", "w"), 0, 0, tiled=True)
     (rows,) = call(
@@ -513,8 +496,14 @@
     got = lax.all_to_all(
         rows.reshape(128, CAP, D + EXT), ("y", "w", "p", "c", "row"), 0, 0, tiled=True
     ).reshape(128 * CAP, D + EXT)
-    (table,) = call(table_kernel, [((ROWS_DEV, D), F32)], (got,), scalars=0)
-    return table
+    return pl.pallas_call(
+        table_kernel,
+        out_shape=jax.ShapeDtypeStruct((ROWS_DEV, D), F32),
+        in_specs=[pl.BlockSpec(memory_space=pltpu.VMEM)],
+        out_specs=pl.BlockSpec(memory_space=pltpu.HBM),
+        scratch_shapes=[pltpu.VMEM((ROWS_DEV, D), F32), pltpu.SemaphoreType.DMA((8,))],
+        compiler_params=pltpu.CompilerParams(vmem_limit_bytes=VMEM_LIMIT),
+    )(got)
 
 
 def solution(mesh):

time: 124 us -> 121 us (0.976)
  waiting for transfers between devices: 26.4 us -> 23.9 us
    ppermute x2, waiting for transfers between devices: 2.71 us -> 0.23 us  [local(): lax.ppermute(grad_attn, ('p', 'c'), [(i, i ^ m) for i in range(4)])]
    pallas_call x0 -> x1, Pallas kernels: none -> 1.67 us  [local(): pl.pallas_call(table_kernel, out_shape=jax.ShapeDtypeStruct((ROWS_DEV, D)...]
    pallas_call x11 -> x10, Pallas kernels: 26.6 us -> 24.9 us  [call(): pl.pallas_call(kernel, out_shape=[jax.ShapeDtypeStruct(shape, dtype) for...]
  transfers between devices with their start and end apart: 8 -> 8, of which waited for: 2 -> 2; matrix products, arithmetic and copies ran while one was open for 0% -> 0% of each run, Pallas kernels for 11% -> 13%
where the time goes in v4:
time: 121 us
  blocking collectives  43.4 us (36%)
  Pallas kernels  30.4 us (25%)
  waiting for transfers between devices  23.9 us (20%)
  starting transfers between devices  17.1 us (14%)
  local copies, waits for them, and re-layouts  5.53 us (5%)
    pallas_call x10, Pallas kernels, call(): pl.pallas_call(kernel, out_shape=[jax.ShapeDtypeStruct(shape, dtype) for...  24.9 us
    all_to_all x1, waiting for transfers between devices, local(): mine = lax.all_to_all(send, ('y', 'w', 'p'), 0, 0, tiled=True)  23.7 us
    all_to_all x1, blocking collectives, local(): lax.all_to_all(rows.reshape(128, CAP, D + EXT), ('y', 'w', 'p', 'c', 'row...  21.9 us
    all_to_all x1, blocking collectives, local(): got = lax.all_to_all(ret, ('y', 'w'), 0, 0, tiled=True)  21.5 us
    all_to_all x1, starting transfers between devices, local(): mine = lax.all_to_all(send, ('y', 'w', 'p'), 0, 0, tiled=True)  7.73 us
    unnamed x26, local copies, waits for them, and re-layouts  5.22 us
    ppermute x3, starting transfers between devices, local(): lax.ppermute(stats, ('y', 'w'), [(i, i ^ m) for i in range(8)])  4.16 us
    pallas_call x1, Pallas kernels, project(): pl.pallas_call(project_kernel, out_shape=jax.ShapeDtypeStruct((16 * BLK,...  3.79 us
  transfers between devices with their start and end apart: 8, of which 2 were waited for; matrix products, arithmetic and copies ran while one was open for 0% of the time, Pallas kernels for 13%

profile of v4, /device:TPU:1, one launch (start us, length us, event | category | flops | bytes accessed | tf_op | source)
XLA Modules:
  0.0 120.8 jit_solution(9429000832877757695)
XLA Ops:
  0.0 3.8 %shard_map.64 = bf16[2048,512]{1,0:T(8,128)(2,1)} custom-call(bf16[256,512]{1,0:T(8,128)(2,1)} %bitcast.20, bf16[256,512]{1,0:T(8,128)(2,1)} %bitcast.17, bf16[512,2048]{1,0:T(8,128)(2,1)} %w_inner.3, bf16[512,512]{1,0:T(8,128)(2,1)} %w_outer.1), custom_call_target="tpu_custom_call" | custom-call | tf_op jit(solution)/shard_map/pallas_call | solution.py:370
  3.8 0.0 copy-start.4
  3.8 0.0 copy-start.5
  3.8 0.0 copy-start.12
  3.8 7.7 %all-to-all-start = ((bf16[16,128,512]{2,1,0:T(8,128)(2,1)}), bf16[16,128,512]{2,1,0:T(8,128)(2,1)S(1)}, u32[]{:S(2)}, u32[]{:S(2)}) async-start(bf16[16,128,512]{2,1,0:T(8,128)(2,1)} %bitcast.23), calls=%async_computation | async-start | bytes 4194304 | tf_op jit(solution)/shard_map/all_to_all | solution.py:393
  11.6 0.0 copy-done.4
  11.6 0.0 copy-done.5
  11.6 0.0 copy-start
  11.6 1.6 %copy-done = bf16[512,2048]{1,0:T(8,128)(2,1)S(1)} copy-done((bf16[512,2048]{1,0:T(8,128)(2,1)S(1)}, bf16[512,2048]{1,0:T(8,128)(2,1)}, u32[]{:S(2)}) %copy-start) | copy-done | bytes 2097176
  13.2 0.9 copy-done.8
  14.1 1.6 %shard_map.65 = (f32[256,2048]{1,0:T(8,128)S(1)}, f32[256,512]{1,0:T(8,128)S(1)}, f32[256,128]{1,0:T(8,128)S(1)}, bf16[512,256]{1,0:T(8,128)(2,1)S(1)}, bf16[256,128]{1,0:T(8,128)(2,1)S(1)}) custom-call(bf16[256,512]{1,0:T(8,128)(2,1)S(1)} %bitcast.21, bf16[256,512]{1,0:T(8,128)(2,1)S(1)} %bitcast.18, bf16[512,2048]{1,0:T(8,128)(2,1)S(1)} %copy-done, ...), custom_call_target="tpu_custom_call" | custom-call | flops 2000000000 | bytes 1048576 | tf_op jit(solution)/shard_map/pallas_call | solution.py:357
  15.8 1.3 %copy-done.2 = f32[256,2048]{1,0:T(8,128)} copy-done((f32[256,2048]{1,0:T(8,128)}, f32[256,2048]{1,0:T(8,128)S(1)}, u32[]{:S(2)}) %copy-start.2) | copy-done | bytes 2097176
  17.1 0.7 copy-done.6
  17.8 0.6 copy-done.9
  18.4 23.7 %all-to-all-done = bf16[16,128,512]{2,1,0:T(8,128)(2,1)S(1)} async-done(((bf16[16,128,512]{2,1,0:T(8,128)(2,1)}), bf16[16,128,512]{2,1,0:T(8,128)(2,1)S(1)}, u32[]{:S(2)}, u32[]{:S(2)}) %all-to-all-start) | async-done | bytes 2097184 | tf_op jit(solution)/shard_map/all_to_all | solution.py:393
  42.1 2.1 %collective-permute-start = (bf16[2048,512]{1,0:T(8,128)(2,1)S(1)}, bf16[2048,512]{1,0:T(8,128)(2,1)S(1)}, u32[]{:S(2)}, u32[]{:S(2)}) collective-permute-start(bf16[2048,512]{1,0:T(8,128)(2,1)S(1)} %bitcast.7), channel_id=1, source_target_pairs={{0,4},{4,0},{1,5},{5,1},{2,6},{6,2},{3,7},{7,3},{8,12},{12,8},{9,1... | collective-permute-start | bytes 6291464 | tf_op jit(solution)/shard_map/ppermute | solution.py:408
  44.2 2.0 %shard_map.66 = (f32[4608,256]{1,0:T(8,128)S(1)}, bf16[4608,256]{1,0:T(8,128)(2,1)S(1)}) custom-call(bf16[2048,512]{1,0:T(8,128)(2,1)S(1)} %bitcast.8), custom_call_target="tpu_custom_call" | custom-call | flops 1000000000 | bytes 1048576 | tf_op jit(solution)/shard_map/pallas_call | solution.py:357
  46.2 2.0 %shard_map.67.refs_1_ = f32[1024,128]{1,0:T(8,128)S(1)} custom-call(s32[2]{0:T(128)S(1)} %copy-done.11, bf16[2048,512]{1,0:T(8,128)(2,1)S(1)} %bitcast.9), custom_call_target="tpu_custom_call" | custom-call | flops 1000000000 | bytes 1048576 | tf_op jit(solution)/shard_map/pallas_call | solution.py:357
  48.3 0.0 collective-permute-done.refs_0_.theirs
  48.3 2.5 %shard_map.68 = (f32[1024,128]{1,0:T(8,128)S(1)}, f32[8,1024]{1,0:T(8,128)S(1)}, bf16[1024,128]{1,0:T(8,128)(2,1)S(1)}) custom-call(s32[2]{0:T(128)S(1)} %copy-done.11, bf16[2048,512]{1,0:T(8,128)(2,1)S(1)} %bitcast.10, bf16[2048,512]{1,0:T(8,128)(2,1)S(1)} %collective-permute-done.refs_0_.theirs, f32[1024,128]{1,0:T(8,128)S(1)} %shard_map.67.refs_1_), custom_call_target="tpu_custom_call" | custom-call | flops 1000000000 | bytes 1048576 | tf_op jit(solution)/shard_map/pallas_call | solution.py:357
  50.8 0.3 collective-permute-start.3
  51.0 0.2 collective-permute-start.2
  51.2 3.7 %collective-permute-start.1 = (f32[8,1024]{1,0:T(8,128)S(1)}, f32[8,1024]{1,0:T(8,128)S(1)}, u32[]{:S(2)}, u32[]{:S(2)}) collective-permute-start(f32[8,1024]{1,0:T(8,128)S(1)} %get-tuple-element.40.s0), channel_id=1, source_target_pairs={{0,16},{16,0},{32,48},{48,32},{64,80},{80,64},{96,112},{112,96},{1... | collective-permute-start | bytes 98312 | tf_op jit(solution)/shard_map/ppermute | solution.py:434
  54.9 2.1 %shard_map.69 = (f32[4608,256]{1,0:T(8,128)S(1)}, bf16[4608,256]{1,0:T(8,128)(2,1)S(1)}) custom-call(bf16[2048,512]{1,0:T(8,128)(2,1)S(1)} %bitcast.11, bf16[2048,512]{1,0:T(8,128)(2,1)S(1)} %collective-permute-done.refs_0_.theirs), custom_call_target="tpu_custom_call" | custom-call | flops 1000000000 | bytes 1048576 | tf_op jit(solution)/shard_map/pallas_call | solution.py:357
  57.0 0.0 collective-permute-done.3.s3
  57.0 0.0 collective-permute-done.2.s2
  57.0 0.0 collective-permute-done.1.s1
  57.0 1.4 %shard_map.70 = (bf16[1024,128]{1,0:T(8,128)(2,1)S(1)}, bf16[1024,128]{1,0:T(8,128)(2,1)S(1)}) custom-call(s32[2]{0:T(128)S(1)} %copy-done.11, f32[1024,128]{1,0:T(8,128)S(1)} %get-tuple-element.45.attn_out, bf16[1024,128]{1,0:T(8,128)(2,1)S(1)} %get-tuple-element.46.grad, f32[8,1024]{1,0:T(8,128)S(1)} %get-tuple-element.40.s0, ...), custom_call_target="tpu_custom_call" | custom-call | flops 10000000 | bytes 1048576 | tf_op jit(solution)/shard_map/pallas_call | solution.py:357
  58.5 0.1 collective-permute-start.5
  58.5 1.3 %collective-permute-start.4 = (bf16[1024,128]{1,0:T(8,128)(2,1)S(1)}, bf16[1024,128]{1,0:T(8,128)(2,1)S(1)}, u32[]{:S(2)}, u32[]{:S(2)}) collective-permute-start(bf16[1024,128]{1,0:T(8,128)(2,1)S(1)} %get-tuple-element.50.grad_attn.refs_2_), channel_id=1, source_target_pairs={{0,4},{4,0},{8,12},{12,8},{1,5},{5,1},{9,13},{13,9},{2,6},{6,2},{1... | collective-permute-start | bytes 786440 | tf_op jit(solution)/shard_map/ppermute | solution.py:452
  59.8 5.4 %shard_map.71.refs_8_ = bf16[1024,128]{1,0:T(8,128)(2,1)S(1)} custom-call(s32[2]{0:T(128)S(1)} %copy-done.11, bf16[2048,512]{1,0:T(8,128)(2,1)S(1)} %bitcast.12, bf16[2048,512]{1,0:T(8,128)(2,1)S(1)} %collective-permute-done.refs_0_.theirs, bf16[1024,128]{1,0:T(8,128)(2,1)S(1)} %get-tuple-element.50.grad_attn.refs_2_), custom_call_target="tpu_custom_call" | custom-call | flops 4000000000 | bytes 1048576 | tf_op jit(solution)/shard_map/pallas_call | solution.py:357
  65.2 0.2 collective-permute-done.5.refs_3_
  65.5 1.8 %collective-permute-start.6 = (bf16[1024,128]{1,0:T(8,128)(2,1)S(1)}, bf16[1024,128]{1,0:T(8,128)(2,1)S(1)}, u32[]{:S(2)}, u32[]{:S(2)}) collective-permute-start(bf16[1024,128]{1,0:T(8,128)(2,1)S(1)} %collective-permute-done.5.refs_3_), channel_id=1, source_target_pairs={{0,4},{4,0},{1,5},{5,1},{2,6},{6,2},{3,7},{7,3},{8,12},{12,8},{9,1... | collective-permute-start | bytes 786440 | tf_op jit(solution)/shard_map/ppermute | solution.py:462
  67.3 2.9 %shard_map.72 = (f32[1024,128]{1,0:T(8,128)S(1)}, f32[1024,128]{1,0:T(8,128)S(1)}) custom-call(s32[2]{0:T(128)S(1)} %copy-done.11, bf16[2048,512]{1,0:T(8,128)(2,1)S(1)} %bitcast.13, f32[4608,256]{1,0:T(8,128)S(1)} %get-tuple-element.52.refs_0_, bf16[4608,256]{1,0:T(8,128)(2,1)S(1)} %get-tuple-element.53.refs_1_, ...), custom_call_target="tpu_custom_call" | custom-call | flops 3000000000 | bytes 1048576 | tf_op jit(solution)/shard_map/pallas_call | solution.py:357
  70.2 0.0 collective-permute-done.4.refs_3_
  70.2 0.0 collective-permute-done.6.refs_4_
  70.2 0.0 copy-start.3
  70.2 0.0 copy-start.7
  70.2 0.0 copy-start.10
  70.2 3.0 %shard_map.73 = bf16[1024,512]{1,0:T(8,128)(2,1)S(1)} custom-call(s32[2]{0:T(128)S(1)} %copy-done.11, bf16[2048,512]{1,0:T(8,128)(2,1)S(1)} %bitcast.14, bf16[2048,512]{1,0:T(8,128)(2,1)S(1)} %collective-permute-done.refs_0_.theirs, f32[4608,256]{1,0:T(8,128)S(1)} %get-tuple-element.43.refs_1_, bf16[4608,256]{1,0:T(8,128)(2,1)S(1)} %get-tuple-element.44.refs_2_, ...), custom_call_target="tpu_custom_call" | custom-call | flops 3000000000 | bytes 1048576 | tf_op jit(solution)/shard_map/pallas_call | solution.py:357
  73.2 0.0 copy-start.1
  73.2 21.5 %all_to_all.28 = bf16[8,128,512]{2,1,0:T(8,128)(2,1)S(1)} all-to-all(bf16[8,128,512]{2,1,0:T(8,128)(2,1)S(1)} %bitcast.15), channel_id=1, replica_groups=mesh['y'=4,'w'=2,'p'=2,'c'=2,'row'=4] {'y','w'}, dimensions={0} | all-to-all | bytes 2097152 | tf_op jit(solution)/shard_map/all_to_all | solution.py:488
  94.7 0.0 copy-done.7
  94.7 2.0 %shard_map.74 = bf16[512,640]{1,0:T(8,128)(2,1)S(1)} custom-call(s32[2]{0:T(128)S(1)} %copy-done.11, bf16[1024,512]{1,0:T(8,128)(2,1)S(1)} %bitcast.16, f32[256,2048]{1,0:T(8,128)S(1)} %copy-done.3, f32[256,512]{1,0:T(8,128)S(1)} %get-tuple-element.59.normed, f32[256,128]{1,0:T(8,128)S(1)} %get-tuple-element.60.inverse, bf16[256,512]{1,0:T(8,128)(2,1)S(1)} %bitcast.19, ...), custom_call_target="tpu_custom_call" | custom-call | flops 1000000000 | bytes 1048576 | tf_op jit(solution)/shard_map/pallas_call | solution.py:357
  96.7 0.2 reshape.22
  96.9 21.9 %all_to_all.29 = bf16[128,4,640]{2,1,0:T(4,128)(2,1)S(1)} all-to-all(bf16[128,4,640]{2,1,0:T(4,128)(2,1)S(1)} %reshape.22), channel_id=1, replica_groups=mesh['y'=4,'w'=2,'p'=2,'c'=2,'row'=4] {'y','w','p','c','row'}, dimensions={0} | all-to-all | bytes 1310720 | tf_op jit(solution)/shard_map/all_to_all | solution.py:496
  118.8 0.1 reshape.23.got
  119.0 1.7 %shard_map.75 = f32[1024,512]{1,0:T(8,128)} custom-call(bf16[512,640]{1,0:T(8,128)(2,1)S(1)} %reshape.23.got), custom_call_target="tpu_custom_call" | custom-call | tf_op jit(solution)/shard_map/pallas_call | solution.py:499
  (10 shorter events, 0.0 us)
Async XLA Ops:
  3.8 7.8 %copy-start.4 = (bf16[2,128,512]{2,1,0:T(8,128)(2,1)S(1)}, bf16[2,128,512]{2,1,0:T(8,128)(2,1)}, u32[]{:S(2)}) copy-start(bf16[2,128,512]{2,1,0:T(8,128)(2,1)} %param.7) | copy-start | bytes 786436
  3.8 7.8 %copy-start.5 = (bf16[512,512]{1,0:T(8,128)(2,1)S(1)}, bf16[512,512]{1,0:T(8,128)(2,1)}, u32[]{:S(2)}) copy-start(bf16[512,512]{1,0:T(8,128)(2,1)} %w_outer.1) | copy-start | bytes 1572868
  3.8 7.8 %copy-start.12 = (s32[2,128]{1,0:T(2,128)S(1)}, s32[2,128]{1,0:T(2,128)}, u32[]{:S(2)}) copy-start(s32[2,128]{1,0:T(2,128)} %param.11) | copy-start | bytes 3076
  3.8 38.2 %all-to-all-start = ((bf16[16,128,512]{2,1,0:T(8,128)(2,1)}), bf16[16,128,512]{2,1,0:T(8,128)(2,1)S(1)}, u32[]{:S(2)}, u32[]{:S(2)}) async-start(bf16[16,128,512]{2,1,0:T(8,128)(2,1)} %bitcast.23), calls=%async_computation | async-start | bytes 4194304 | tf_op jit(solution)/shard_map/all_to_all | solution.py:393
  11.6 1.6 %copy-start = (bf16[512,2048]{1,0:T(8,128)(2,1)S(1)}, bf16[512,2048]{1,0:T(8,128)(2,1)}, u32[]{:S(2)}) copy-start(bf16[512,2048]{1,0:T(8,128)(2,1)} %w_inner.3) | copy-start | bytes 6291460
  13.2 0.9 copy-start.8
  15.8 1.3 %copy-start.2 = (f32[256,2048]{1,0:T(8,128)}, f32[256,2048]{1,0:T(8,128)S(1)}, u32[]{:S(2)}) copy-start(f32[256,2048]{1,0:T(8,128)S(1)} %get-tuple-element.58.slope) | copy-start | bytes 6291460
  17.1 0.7 copy-start.6
  17.8 0.6 copy-start.9
  18.4 27.8 %copy-start.11 = (s32[2]{0:T(128)S(1)}, s32[2]{0:T(128)}, u32[]{:S(2)}) copy-start(s32[2]{0:T(128)} %lengths.13) | copy-start | bytes 28
  42.1 6.2 %collective-permute-start = (bf16[2048,512]{1,0:T(8,128)(2,1)S(1)}, bf16[2048,512]{1,0:T(8,128)(2,1)S(1)}, u32[]{:S(2)}, u32[]{:S(2)}) collective-permute-start(bf16[2048,512]{1,0:T(8,128)(2,1)S(1)} %bitcast.7), channel_id=1, source_target_pairs={{0,4},{4,0},{1,5},{5,1},{2,6},{6,2},{3,7},{7,3},{8,12},{12,8},{9,1... | collective-permute-start | bytes 6291464 | tf_op jit(solution)/shard_map/ppermute | solution.py:408
  50.8 6.2 %collective-permute-start.3 = (f32[8,1024]{1,0:T(8,128)S(1)}, f32[8,1024]{1,0:T(8,128)S(1)}, u32[]{:S(2)}, u32[]{:S(2)}) collective-permute-start(f32[8,1024]{1,0:T(8,128)S(1)} %get-tuple-element.40.s0), channel_id=1, source_target_pairs={{0,48},{16,32},{32,16},{48,0},{64,112},{80,96},{96,80},{112,64},{1... | collective-permute-start | bytes 98312 | tf_op jit(solution)/shard_map/ppermute | solution.py:434
  51.0 6.0 %collective-permute-start.2 = (f32[8,1024]{1,0:T(8,128)S(1)}, f32[8,1024]{1,0:T(8,128)S(1)}, u32[]{:S(2)}, u32[]{:S(2)}) collective-permute-start(f32[8,1024]{1,0:T(8,128)S(1)} %get-tuple-element.40.s0), channel_id=1, source_target_pairs={{0,32},{16,48},{32,0},{48,16},{64,96},{80,112},{96,64},{112,80},{1... | collective-permute-start | bytes 98312 | tf_op jit(solution)/shard_map/ppermute | solution.py:434
  51.2 5.8 %collective-permute-start.1 = (f32[8,1024]{1,0:T(8,128)S(1)}, f32[8,1024]{1,0:T(8,128)S(1)}, u32[]{:S(2)}, u32[]{:S(2)}) collective-permute-start(f32[8,1024]{1,0:T(8,128)S(1)} %get-tuple-element.40.s0), channel_id=1, source_target_pairs={{0,16},{16,0},{32,48},{48,32},{64,80},{80,64},{96,112},{112,96},{1... | collective-permute-start | bytes 98312 | tf_op jit(solution)/shard_map/ppermute | solution.py:434
  58.5 7.0 %collective-permute-start.5 = (bf16[1024,128]{1,0:T(8,128)(2,1)S(1)}, bf16[1024,128]{1,0:T(8,128)(2,1)S(1)}, u32[]{:S(2)}, u32[]{:S(2)}) collective-permute-start(bf16[1024,128]{1,0:T(8,128)(2,1)S(1)} %get-tuple-element.50.grad_attn.refs_2_), channel_id=1, source_target_pairs={{0,8},{4,12},{8,0},{12,4},{1,9},{5,13},{9,1},{13,5},{2,10},{6,14},... | collective-permute-start | bytes 786440 | tf_op jit(solution)/shard_map/ppermute | solution.py:452
  58.5 11.6 %collective-permute-start.4 = (bf16[1024,128]{1,0:T(8,128)(2,1)S(1)}, bf16[1024,128]{1,0:T(8,128)(2,1)S(1)}, u32[]{:S(2)}, u32[]{:S(2)}) collective-permute-start(bf16[1024,128]{1,0:T(8,128)(2,1)S(1)} %get-tuple-element.50.grad_attn.refs_2_), channel_id=1, source_target_pairs={{0,4},{4,0},{8,12},{12,8},{1,5},{5,1},{9,13},{13,9},{2,6},{6,2},{1... | collective-permute-start | bytes 786440 | tf_op jit(solution)/shard_map/ppermute | solution.py:452
  65.5 4.7 %collective-permute-start.6 = (bf16[1024,128]{1,0:T(8,128)(2,1)S(1)}, bf16[1024,128]{1,0:T(8,128)(2,1)S(1)}, u32[]{:S(2)}, u32[]{:S(2)}) collective-permute-start(bf16[1024,128]{1,0:T(8,128)(2,1)S(1)} %collective-permute-done.5.refs_3_), channel_id=1, source_target_pairs={{0,4},{4,0},{1,5},{5,1},{2,6},{6,2},{3,7},{7,3},{8,12},{12,8},{9,1... | collective-permute-start | bytes 786440 | tf_op jit(solution)/shard_map/ppermute | solution.py:462
  70.2 24.5 %copy-start.3 = (f32[256,2048]{1,0:T(8,128)S(1)}, f32[256,2048]{1,0:T(8,128)}, u32[]{:S(2)}) copy-start(f32[256,2048]{1,0:T(8,128)} %copy-done.2) | copy-start | bytes 6291460
  70.2 24.5 %copy-start.7 = (bf16[512,256]{1,0:T(8,128)(2,1)S(1)}, bf16[512,256]{1,0:T(8,128)(2,1)}, u32[]{:S(2)}) copy-start(bf16[512,256]{1,0:T(8,128)(2,1)} %copy-done.6) | copy-start | bytes 786436
  70.2 24.5 %copy-start.10 = (bf16[256,128]{1,0:T(8,128)(2,1)S(1)}, bf16[256,128]{1,0:T(8,128)(2,1)}, u32[]{:S(2)}) copy-start(bf16[256,128]{1,0:T(8,128)(2,1)} %copy-done.9) | copy-start | bytes 196612
  73.2 21.5 %copy-start.1 = (bf16[512,2048]{1,0:T(8,128)(2,1)S(1)}, bf16[512,2048]{1,0:T(8,128)(2,1)}, u32[]{:S(2)}) copy-start(bf16[512,2048]{1,0:T(8,128)(2,1)} %w_inner.3) | copy-start | bytes 6291460

commit v5 on v4

--- a/solution.py
+++ b/solution.py
@@ -72,7 +72,7 @@
             for h in range(HEADS):
                 piece = act[g * BLK : (g + 1) * BLK, h * HD : (h + 1) * HD]
                 for p in range(2):
-                    at = ((g * HEADS + h) * 2 + p) * BLK
+                    at = (p * 8 + g * HEADS + h) * BLK
                     parts[slot, at : at + BLK, :] = piece
         cols = slice(slot * HD, (slot + 1) * HD)
         leaving.append(pltpu.make_async_copy(parts.at[slot], send.at[:, cols], sems.at[7 + slot]))
@@ -102,7 +102,8 @@
     )
     same = jnp.where((owner_col == owner_row) & earlier, 1, 0)
     rank = jnp.sum(same, axis=0, keepdims=True)
-    slot = owner_row * CAP + rank
+    dest = (owner_row // 4 % 2) * 64 + owner_row // 8 * 4 + owner_row % 4
+    slot = dest * CAP + rank
     slots = hot.shape[0]
     hot[...] = jnp.where(
         lax.broadcasted_iota(jnp.int32, (slots, count), 0) == slot, 1.0, 0.0
@@ -118,11 +119,11 @@
 
 
 V_COLS, Q_COLS, K_COLS, G_COLS = (slice(i * HD, (i + 1) * HD) for i in range(4))
+GRP = 2 * BLK
 
 
 def my_place():
-    p, c = lax.axis_index("p"), lax.axis_index("c")
-    return p, c, 2 * p + c
+    return lax.axis_index("p"), lax.axis_index("c")
 
 
 def my_length(lengths):
@@ -133,49 +134,58 @@
     return 1.0 / jnp.full((1, HD), length, jnp.int32).astype(F32)
 
 
-def diagonal(place, core, rows_are_keys):
-    row = lax.broadcasted_iota(jnp.int32, (BLK, 2 * BLK), 0) + place[2] * BLK
-    lane = lax.broadcasted_iota(jnp.int32, (BLK, 2 * BLK), 1)
-    col = lane + jnp.where(lane >= BLK, BLK, 0) + core * BLK
+def at_rows(p, start, count):
+    return pl.ds(pl.multiple_of(p * 1024 + start, GRP), count)
+
+
+def diagonal(row_place, col_place, rows_are_keys):
+    def start(place):
+        return (4 * place[0] + place[1]) * BLK
+
+    row = lax.broadcasted_iota(jnp.int32, (GRP, GRP), 0)
+    col = lax.broadcasted_iota(jnp.int32, (GRP, GRP), 1)
+    row = jnp.where(row >= BLK, row + BLK, row) + start(row_place)
+    col = jnp.where(col >= BLK, col + BLK, col) + start(col_place)
     return row <= col if rows_are_keys else col <= row
 
 
 def mask_first(mask, values):
-    first = jnp.where(mask, values[:BLK, :], 0.0)
-    return jnp.concatenate([first, values[BLK:, :]], axis=0) if values.shape[0] > BLK else first
+    first = jnp.where(mask, values[:GRP, :], 0.0)
+    return jnp.concatenate([first, values[GRP:, :]], axis=0) if values.shape[0] > GRP else first
 
 
 def mask_last(mask, values):
-    last = jnp.where(mask, values[-BLK:, :], 0.0)
-    return jnp.concatenate([values[:-BLK, :], last], axis=0) if values.shape[0] > BLK else last
-
-
-def own_blocks(place, src, cols, dst):
-    for m in range(8):
-        at = pl.multiple_of((2 * m + place[0]) * BLK, BLK)
-        dst[m * BLK : (m + 1) * BLK, :] = src[pl.ds(at, BLK), cols]
+    last = jnp.where(mask, values[-GRP:, :], 0.0)
+    return jnp.concatenate([values[:-GRP, :], last], axis=0) if values.shape[0] > GRP else last
+
+
+def query_rows(y, part):
+    start = (y * (9 - y) + part * (4 - y)) * GRP
+    return slice(start, start + (4 - y) * GRP)
 
 
 def forward_kernel(last, lengths, mine, *refs):
     place = my_place()
+    p = place[0]
     if last:
-        theirs, before, out, stats, grad, queries = refs
+        theirs, before, out, slope_out, stats, grad = refs
         keys_of, core = theirs, 1 - place[1]
-        own_blocks(place, mine, G_COLS, grad)
+        grad[...] = mine[at_rows(p, 0, 1024), G_COLS]
         out[...] = before[...]
     else:
-        out, queries = refs
+        out, slope_out = refs
         keys_of, core = mine, place[1]
         out[...] = jnp.zeros_like(out)
-    own_blocks(place, mine, Q_COLS, queries)
-    mask = diagonal(place, core, False)
-    for j in range(8):
-        keys = slice(j * 2 * BLK, (j + 1) * 2 * BLK)
-        rows = slice(j * BLK, 8 * BLK)
-        half = dot_t(queries[rows, :], keys_of[keys, K_COLS]) * (0.5 * SCALE)
-        attn = half * jnp.tanh(half) + half
-        attn = mask_first(mask, attn)
-        out[rows, :] += dot(attn.astype(BF16), keys_of[keys, V_COLS])
+    for y in range(4):
+        rows = slice(y * GRP, 1024)
+        queries = mine[at_rows(p, y * GRP, 1024 - y * GRP), Q_COLS]
+        for part in range(2):
+            keys = slice(part * 1024 + y * GRP, part * 1024 + (y + 1) * GRP)
+            slope, attn = slopes(dot_t(queries, keys_of[keys, K_COLS]))
+            mask = diagonal(place, (part, core), False)
+            slope_out[query_rows(y, part), :] = mask_first(mask, slope)
+            attn = mask_first(mask, attn)
+            out[rows, :] += dot(attn.astype(BF16), keys_of[keys, V_COLS])
     if not last:
         return
     inv_len = inverse_of(my_length(lengths))
@@ -197,7 +207,7 @@
 
 
 def grad_attn_kernel(lengths, attn_out, grad, s0, s1, s2, s3, grad_attn, normed_out):
-    place = my_place()
+    p, c = my_place()
     length = my_length(lengths)
     parts = [s0[...], s1[...], s2[...], s3[...]]
     means = [part[0:1, :] for part in parts]
@@ -223,7 +233,8 @@
         inv = cols[:, 1:2]
         n = (attn_out[rows, :] - cols[:, 0:1]) * inv
         back = (grad[rows, :].astype(F32) - cols[:, 2:3] - n * cols[:, 3:4]) * inv
-        pos = lax.broadcasted_iota(jnp.int32, (BLK, 1), 0) + (m * 4 + place[2]) * BLK
+        pos = lax.broadcasted_iota(jnp.int32, (BLK, 1), 0)
+        pos = pos + (m // 2 * 8 + 4 * p + m % 2 * 2 + c) * BLK
         grad_attn[rows, :] = jnp.where(pos < length, back, 0.0).astype(BF16)
         normed_out[rows, :] = n.astype(BF16)
 
@@ -235,71 +246,72 @@
     return two_sigma + half * (1.0 - t * t), half * two_sigma
 
 
-def grad_query_kernel(lengths, mine, theirs, grad_attn, ret, queries, total):
-    place = my_place()
+def grad_query_kernel(lengths, mine, theirs, slope_m, slope_t, grad_attn, ret, total):
     total[...] = jnp.zeros_like(total)
-    own_blocks(place, mine, Q_COLS, queries)
-    masks = [diagonal(place, place[1], False), diagonal(place, 1 - place[1], False)]
-    for j in range(8):
-        keys = slice(j * 2 * BLK, (j + 1) * 2 * BLK)
-        rows = slice(j * BLK, 8 * BLK)
-        for src, mask in zip((mine, theirs), masks):
-            k = src[keys, K_COLS]
-            slope, _ = slopes(dot_t(queries[rows, :], k))
-            score = slope * dot_t(grad_attn[rows, :], src[keys, V_COLS])
-            total[rows, :] += dot(mask_first(mask, score).astype(BF16), k)
+    for y in range(4):
+        rows = slice(y * GRP, 1024)
+        for part in range(2):
+            keys = slice(part * 1024 + y * GRP, part * 1024 + (y + 1) * GRP)
+            for src, slope in ((mine, slope_m), (theirs, slope_t)):
+                score = slope[query_rows(y, part), :] * dot_t(grad_attn[rows, :], src[keys, V_COLS])
+                total[rows, :] += dot(score.astype(BF16), src[keys, K_COLS])
     inv_len = inverse_of(my_length(lengths))
     ret[...] = (total[...] * (0.5 * SCALE * inv_len)).astype(BF16)
 
 
-def packed_rows(j):
-    return slice(j * (j + 1) // 2 * BLK, (j + 1) * (j + 2) // 2 * BLK)
-
-
-def key_scores_kernel(other, mine, *refs):
+PACKED = 20 * GRP
+
+
+def packed_rows(y, other):
+    start = (y + 1) * (y + other) * GRP
+    return slice(start, start + (y + 1) * GRP)
+
+
+def key_scores_kernel(theirs_too, mine, *refs):
     place = my_place()
-    if other:
-        src, slope_out, attn_out, keys = refs
+    p = place[0]
+    if theirs_too:
+        src, slope_out, attn_out = refs
         core = 1 - place[1]
     else:
-        slope_out, attn_out, keys = refs
+        slope_out, attn_out = refs
         src, core = mine, place[1]
-    own_blocks(place, mine, K_COLS, keys)
-    mask = diagonal(place, core, True)
-    for j in range(8):
-        events = slice(j * 2 * BLK, (j + 1) * 2 * BLK)
-        rows = slice(0, (j + 1) * BLK)
-        slope, attn = slopes(dot_t(keys[rows, :], src[events, Q_COLS]))
-        slope_out[packed_rows(j), :] = mask_last(mask, slope)
-        attn_out[packed_rows(j), :] = mask_last(mask, attn).astype(BF16)
+    for y in range(4):
+        count = (y + 1) * GRP
+        keys = mine[at_rows(p, 0, count), K_COLS]
+        for other in range(2):
+            part = 1 - p if other else p
+            slope, attn = slopes(dot_t(keys, src[at_rows(part, y * GRP, GRP), Q_COLS]))
+            mask = diagonal(place, (part, core), True)
+            rows = packed_rows(y, other)
+            slope_out[rows, :] = mask_last(mask, slope)
+            attn_out[rows, :] = mask_last(mask, attn).astype(BF16)
 
 
 def grad_key_kernel(last, lengths, mine, *refs):
-    place = my_place()
-    p = place[0]
+    p = lax.axis_index("p")
     if last:
         theirs, slope, attn, g_here, g_there, k_before, v_before, normed_out, grad_q, *refs = refs
-        ret, src_g, values, grad_k, grad_v = refs
+        ret, grad_k, grad_v = refs
         src = theirs
         grad_k[...] = k_before[...]
         grad_v[...] = v_before[...]
     else:
-        slope, attn, g_here, g_there, grad_k, grad_v, src_g, values = refs
+        slope, attn, g_here, g_there, grad_k, grad_v = refs
         src = mine
         grad_k[...] = jnp.zeros_like(grad_k)
         grad_v[...] = jnp.zeros_like(grad_v)
-    own_blocks(place, mine, V_COLS, values)
-    for m in range(8):
-        rows = slice(m * BLK, (m + 1) * BLK)
-        src_g[pl.ds(pl.multiple_of((2 * m + p) * BLK, BLK), BLK), :] = g_here[rows, :]
-        src_g[pl.ds(pl.multiple_of((2 * m + 1 - p) * BLK, BLK), BLK), :] = g_there[rows, :]
-    for j in range(8):
-        events = slice(j * 2 * BLK, (j + 1) * 2 * BLK)
-        rows = slice(0, (j + 1) * BLK)
-        ga = src_g[events, :]
-        score = slope[packed_rows(j), :] * dot_t(values[rows, :], ga)
-        grad_k[rows, :] += dot(score.astype(BF16), src[events, Q_COLS])
-        grad_v[rows, :] += dot(attn[packed_rows(j), :], ga)
+    for y in range(4):
+        count = (y + 1) * GRP
+        rows = slice(0, count)
+        values = mine[at_rows(p, 0, count), V_COLS]
+        for other, grad_attn in enumerate((g_here, g_there)):
+            ga = grad_attn[y * GRP : (y + 1) * GRP, :]
+            q = src[at_rows(1 - p if other else p, y * GRP, GRP), Q_COLS]
+            packed = packed_rows(y, other)
+            score = slope[packed, :] * dot_t(values, ga)
+            grad_k[rows, :] += dot(score.astype(BF16), q)
+            grad_v[rows, :] += dot(attn[packed, :], ga)
     if last:
         inv_len = inverse_of(my_length(lengths))
         ret[:, :HD] = normed_out[...]
@@ -326,7 +338,7 @@
         - normed[...] * jnp.mean(grad_normed * normed[...], axis=-1, keepdims=True)
     )
     total = grad_out[...].astype(F32) + back
-    chip = (lax.axis_index("y") * 2 + lax.axis_index("w")) * 2 + lax.axis_index("p")
+    chip = (lax.axis_index("y") * 2 + lax.axis_index("p")) * 2 + lax.axis_index("w")
     first = (chip * 2 + lax.axis_index("c")) * BLK
     row = lax.broadcasted_iota(jnp.int32, (2 * BLK, 1), 0)
     second = row >= BLK
@@ -390,7 +402,7 @@
     rows_bf16, rows_f32 = ((1024, HD), BF16), ((1024, HD), F32)
     swap_c = [(0, 1), (1, 0)]
     send = project(events, grad_out, w_inner, w_outer)
-    mine = lax.all_to_all(send, ("y", "w", "p"), 0, 0, tiled=True)
+    mine = lax.all_to_all(send, ("p", "y", "w"), 0, 0, tiled=True)
     slope, normed, inverse, hot, ext = call(
         gate_kernel,
         [
@@ -406,28 +418,17 @@
     )
     mine, slope = lax.optimization_barrier((mine, slope))
     theirs = lax.ppermute(mine, "c", swap_c)
-    (attn_one,) = call(
+    score_shapes = [((PACKED, GRP), F32), ((PACKED, GRP), BF16)]
+    attn_one, slope_m = call(
         functools.partial(forward_kernel, False),
-        [rows_f32],
+        [rows_f32, score_shapes[0]],
         (valid_lengths, mine),
-        scratch=[rows_bf16],
         flops=10**9,
     )
-    score_shapes = [((36 * BLK, 2 * BLK), F32), ((36 * BLK, 2 * BLK), BF16)]
-    scores_m = call(
-        functools.partial(key_scores_kernel, False),
-        score_shapes,
-        (mine,),
-        scalars=0,
-        scratch=[rows_bf16],
-        flops=10**9,
-    )
-    theirs, scores_m, attn_one = lax.optimization_barrier((theirs, scores_m, attn_one))
-    attn_out, stats, grad = call(
+    attn_out, slope_t, stats, grad = call(
         functools.partial(forward_kernel, True),
-        [rows_f32, ((8, 1024), F32), rows_bf16],
+        [rows_f32, score_shapes[0], ((8, 1024), F32), rows_bf16],
         (valid_lengths, mine, theirs, attn_one),
-        scratch=[rows_bf16],
         flops=10**9,
     )
     others = [
@@ -438,7 +439,6 @@
         score_shapes,
         (mine, theirs),
         scalars=0,
-        scratch=[rows_bf16],
         flops=10**9,
     )
     others, scores_t = lax.optimization_barrier((others, scores_t))
@@ -451,20 +451,27 @@
     grad_p, grad_c = [
         lax.ppermute(grad_attn, ("p", "c"), [(i, i ^ m) for i in range(4)]) for m in (2, 1)
     ]
+    mine_late, grad_attn = lax.optimization_barrier((mine, grad_attn))
+    scores_m = call(
+        functools.partial(key_scores_kernel, False),
+        score_shapes,
+        (mine_late,),
+        scalars=0,
+        flops=10**9,
+    )
     (grad_q,) = call(
         grad_query_kernel,
         [rows_bf16],
-        (valid_lengths, mine, theirs, grad_attn),
-        scratch=[rows_bf16, rows_f32],
+        (valid_lengths, mine, theirs, slope_m, slope_t, grad_attn),
+        scratch=[rows_f32],
         flops=4 * 10**9,
     )
-    grad_p, grad_q = lax.optimization_barrier((grad_p, grad_q))
+    grad_p, grad_q, scores_m = lax.optimization_barrier((grad_p, grad_q, scores_m))
     grad_pc = lax.ppermute(grad_p, "c", swap_c)
     grad_k, grad_v = call(
         functools.partial(grad_key_kernel, False),
         [rows_f32, rows_f32],
         (valid_lengths, mine, *scores_m, grad_attn, grad_p),
-        scratch=[((2048, HD), BF16), rows_bf16],
         flops=3 * 10**9,
     )
     (ret,) = call(
@@ -482,7 +489,7 @@
             normed_out,
             grad_q,
         ),
-        scratch=[((2048, HD), BF16), rows_bf16, rows_f32, rows_f32],
+        scratch=[rows_f32, rows_f32],
         flops=3 * 10**9,
     )
     got = lax.all_to_all(ret, ("y", "w"), 0, 0, tiled=True)
@@ -494,7 +501,7 @@
         flops=10**9,
     )
     got = lax.all_to_all(
-        rows.reshape(128, CAP, D + EXT), ("y", "w", "p", "c", "row"), 0, 0, tiled=True
+        rows.reshape(128, CAP, D + EXT), ("c", "y", "p", "w", "row"), 0, 0, tiled=True
     ).reshape(128 * CAP, D + EXT)
     return pl.pallas_call(
         table_kernel,
@@ -507,8 +514,8 @@
 
 
 def solution(mesh):
-    fine = Mesh(mesh.devices.reshape(4, 2, 2, 2, 4), ("y", "w", "p", "c", "row"))
-    seq = ("y", "w", "p", "c")
+    fine = Mesh(mesh.devices.reshape(4, 2, 2, 2, 4), ("y", "p", "w", "c", "row"))
+    seq = ("y", "p", "w", "c")
     return jax.shard_map(
         local,
         mesh=fine,

time: 121 us -> 120 us (level)
    ppermute x2, starting transfers between devices: 1.37 us -> 3.89 us  [local(): lax.ppermute(grad_attn, ('p', 'c'), [(i, i ^ m) for i in range(4)])]
    ppermute x3, starting transfers between devices: 4.16 us -> 2.65 us  [local(): lax.ppermute(stats, ('y', 'w'), [(i, i ^ m) for i in range(8)])]
    ppermute x1, starting transfers between devices: 1.78 us -> 0.49 us  [local(): grad_pc = lax.ppermute(grad_p, 'c', swap_c)]
    all_to_all x1, blocking collectives: 21.5 us -> 20.2 us  [local(): got = lax.all_to_all(ret, ('y', 'w'), 0, 0, tiled=True)]
where the time goes in v5:
time: 120 us
  blocking collectives  42.3 us (35%)
  Pallas kernels  30.8 us (26%)
  waiting for transfers between devices  23.7 us (20%)
  starting transfers between devices  16.9 us (14%)
  local copies, waits for them, and re-layouts  5.54 us (5%)
    pallas_call x10, Pallas kernels, call(): pl.pallas_call(kernel, out_shape=[jax.ShapeDtypeStruct(shape, dtype) for...  25.4 us
    all_to_all x1, waiting for transfers between devices, local(): mine = lax.all_to_all(send, ('p', 'y', 'w'), 0, 0, tiled=True)  22.8 us
    all_to_all x1, blocking collectives, local(): lax.all_to_all(rows.reshape(128, CAP, D + EXT), ('c', 'y', 'p', 'w', 'row...  22 us
    all_to_all x1, blocking collectives, local(): got = lax.all_to_all(ret, ('y', 'w'), 0, 0, tiled=True)  20.2 us
    all_to_all x1, starting transfers between devices, local(): mine = lax.all_to_all(send, ('p', 'y', 'w'), 0, 0, tiled=True)  7.73 us
    unnamed x26, local copies, waits for them, and re-layouts  5.24 us
    ppermute x2, starting transfers between devices, local(): lax.ppermute(grad_attn, ('p', 'c'), [(i, i ^ m) for i in range(4)])  3.89 us
    pallas_call x1, Pallas kernels, project(): pl.pallas_call(project_kernel, out_shape=jax.ShapeDtypeStruct((16 * BLK,...  3.79 us
  transfers between devices with their start and end apart: 8, of which 2 were waited for; matrix products, arithmetic and copies ran while one was open for 0% of the time, Pallas kernels for 13%

profile of v5, /device:TPU:1, one launch (start us, length us, event | category | flops | bytes accessed | tf_op | source)
XLA Modules:
  0.0 119.7 jit_solution(6025383483086526764)
XLA Ops:
  0.0 3.8 %shard_map.64 = bf16[2048,512]{1,0:T(8,128)(2,1)} custom-call(bf16[256,512]{1,0:T(8,128)(2,1)} %bitcast.20, bf16[256,512]{1,0:T(8,128)(2,1)} %bitcast.17, bf16[512,2048]{1,0:T(8,128)(2,1)} %w_inner.3, bf16[512,512]{1,0:T(8,128)(2,1)} %w_outer.1), custom_call_target="tpu_custom_call" | custom-call | tf_op jit(solution)/shard_map/pallas_call | solution.py:382
  3.8 0.0 copy-start.4
  3.8 0.0 copy-start.5
  3.8 0.0 copy-start.12
  3.8 7.7 %all-to-all-start = ((bf16[16,128,512]{2,1,0:T(8,128)(2,1)}), bf16[16,128,512]{2,1,0:T(8,128)(2,1)S(1)}, u32[]{:S(2)}, u32[]{:S(2)}) async-start(bf16[16,128,512]{2,1,0:T(8,128)(2,1)} %bitcast.23), calls=%async_computation | async-start | bytes 4194304 | tf_op jit(solution)/shard_map/all_to_all | solution.py:405
  11.6 0.0 copy-done.4
  11.6 0.0 copy-done.5
  11.6 0.0 copy-done.12
  11.6 0.0 copy-start
  11.6 1.6 %copy-done = bf16[512,2048]{1,0:T(8,128)(2,1)S(1)} copy-done((bf16[512,2048]{1,0:T(8,128)(2,1)S(1)}, bf16[512,2048]{1,0:T(8,128)(2,1)}, u32[]{:S(2)}) %copy-start) | copy-done | bytes 2097176
  13.2 0.9 copy-done.8
  14.1 1.6 %shard_map.65 = (f32[256,2048]{1,0:T(8,128)S(1)}, f32[256,512]{1,0:T(8,128)S(1)}, f32[256,128]{1,0:T(8,128)S(1)}, bf16[512,256]{1,0:T(8,128)(2,1)S(1)}, bf16[256,128]{1,0:T(8,128)(2,1)S(1)}) custom-call(bf16[256,512]{1,0:T(8,128)(2,1)S(1)} %bitcast.21, bf16[256,512]{1,0:T(8,128)(2,1)S(1)} %bitcast.18, bf16[512,2048]{1,0:T(8,128)(2,1)S(1)} %copy-done, ...), custom_call_target="tpu_custom_call" | custom-call | flops 2000000000 | bytes 1048576 | tf_op jit(solution)/shard_map/pallas_call | solution.py:369
  15.8 0.0 copy-start.2
  15.8 1.3 %copy-done.2 = f32[256,2048]{1,0:T(8,128)} copy-done((f32[256,2048]{1,0:T(8,128)}, f32[256,2048]{1,0:T(8,128)S(1)}, u32[]{:S(2)}) %copy-start.2) | copy-done | bytes 2097176
  17.1 0.7 copy-done.6
  17.8 0.6 copy-done.9
  18.4 22.8 %all-to-all-done = bf16[16,128,512]{2,1,0:T(8,128)(2,1)S(1)} async-done(((bf16[16,128,512]{2,1,0:T(8,128)(2,1)}), bf16[16,128,512]{2,1,0:T(8,128)(2,1)S(1)}, u32[]{:S(2)}, u32[]{:S(2)}) %all-to-all-start) | async-done | bytes 2097184 | tf_op jit(solution)/shard_map/all_to_all | solution.py:405
  41.3 2.1 %collective-permute-start = (bf16[2048,512]{1,0:T(8,128)(2,1)S(1)}, bf16[2048,512]{1,0:T(8,128)(2,1)S(1)}, u32[]{:S(2)}, u32[]{:S(2)}) collective-permute-start(bf16[2048,512]{1,0:T(8,128)(2,1)S(1)} %bitcast.7), channel_id=1, source_target_pairs={{0,4},{4,0},{1,5},{5,1},{2,6},{6,2},{3,7},{7,3},{8,12},{12,8},{9,1... | collective-permute-start | bytes 6291464 | tf_op jit(solution)/shard_map/ppermute | solution.py:420
  43.4 0.0 copy-done.11
  43.4 2.9 %shard_map.66 = (f32[1024,128]{1,0:T(8,128)S(1)}, f32[5120,256]{1,0:T(8,128)S(1)}) custom-call(s32[2]{0:T(128)S(1)} %copy-done.11, bf16[2048,512]{1,0:T(8,128)(2,1)S(1)} %bitcast.8), custom_call_target="tpu_custom_call" | custom-call | flops 1000000000 | bytes 1048576 | tf_op jit(solution)/shard_map/pallas_call | solution.py:369
  46.3 0.9 collective-permute-done.refs_0_.theirs
  47.2 3.3 %shard_map.67 = (f32[1024,128]{1,0:T(8,128)S(1)}, f32[5120,256]{1,0:T(8,128)S(1)}, f32[8,1024]{1,0:T(8,128)S(1)}, bf16[1024,128]{1,0:T(8,128)(2,1)S(1)}) custom-call(s32[2]{0:T(128)S(1)} %copy-done.11, bf16[2048,512]{1,0:T(8,128)(2,1)S(1)} %bitcast.9, bf16[2048,512]{1,0:T(8,128)(2,1)S(1)} %collective-permute-done.refs_0_.theirs, ...), custom_call_target="tpu_custom_call" | custom-call | flops 1000000000 | bytes 1048576 | tf_op jit(solution)/shard_map/pallas_call | solution.py:369
  50.5 0.0 collective-permute-start.3
  50.5 1.6 %collective-permute-start.2 = (f32[8,1024]{1,0:T(8,128)S(1)}, f32[8,1024]{1,0:T(8,128)S(1)}, u32[]{:S(2)}, u32[]{:S(2)}) collective-permute-start(f32[8,1024]{1,0:T(8,128)S(1)} %get-tuple-element.40.s0), channel_id=1, source_target_pairs={{0,32},{8,40},{32,0},{40,8},{64,96},{72,104},{96,64},{104,72},{1,3... | collective-permute-start | bytes 98312 | tf_op jit(solution)/shard_map/ppermute | solution.py:435
  52.1 1.1 collective-permute-start.1
  53.2 2.4 %shard_map.68 = (f32[5120,256]{1,0:T(8,128)S(1)}, bf16[5120,256]{1,0:T(8,128)(2,1)S(1)}) custom-call(bf16[2048,512]{1,0:T(8,128)(2,1)S(1)} %bitcast.10, bf16[2048,512]{1,0:T(8,128)(2,1)S(1)} %collective-permute-done.refs_0_.theirs), custom_call_target="tpu_custom_call" | custom-call | flops 1000000000 | bytes 1048576 | tf_op jit(solution)/shard_map/pallas_call | solution.py:369
  55.5 0.0 collective-permute-done.3.s3
  55.5 0.0 collective-permute-done.2.s2
  55.5 0.0 collective-permute-done.1.s1
  55.6 1.4 %shard_map.69 = (bf16[1024,128]{1,0:T(8,128)(2,1)S(1)}, bf16[1024,128]{1,0:T(8,128)(2,1)S(1)}) custom-call(s32[2]{0:T(128)S(1)} %copy-done.11, f32[1024,128]{1,0:T(8,128)S(1)} %get-tuple-element.45.attn_out, bf16[1024,128]{1,0:T(8,128)(2,1)S(1)} %get-tuple-element.46.grad, f32[8,1024]{1,0:T(8,128)S(1)} %get-tuple-element.40.s0, ...), custom_call_target="tpu_custom_call" | custom-call | flops 10000000 | bytes 1048576 | tf_op jit(solution)/shard_map/pallas_call | solution.py:369
  57.0 1.5 %collective-permute-start.5 = (bf16[1024,128]{1,0:T(8,128)(2,1)S(1)}, bf16[1024,128]{1,0:T(8,128)(2,1)S(1)}, u32[]{:S(2)}, u32[]{:S(2)}) collective-permute-start(bf16[1024,128]{1,0:T(8,128)(2,1)S(1)} %get-tuple-element.53.grad_attn.refs_2_), channel_id=1, source_target_pairs={{0,16},{4,20},{16,0},{20,4},{1,17},{5,21},{17,1},{21,5},{2,18},{6,... | collective-permute-start | bytes 786440 | tf_op jit(solution)/shard_map/ppermute | solution.py:452
  58.5 2.4 %collective-permute-start.4 = (bf16[1024,128]{1,0:T(8,128)(2,1)S(1)}, bf16[1024,128]{1,0:T(8,128)(2,1)S(1)}, u32[]{:S(2)}, u32[]{:S(2)}) collective-permute-start(bf16[1024,128]{1,0:T(8,128)(2,1)S(1)} %get-tuple-element.53.grad_attn.refs_2_), channel_id=1, source_target_pairs={{0,4},{4,0},{16,20},{20,16},{1,5},{5,1},{17,21},{21,17},{2,6},{6,2... | collective-permute-start | bytes 786440 | tf_op jit(solution)/shard_map/ppermute | solution.py:452
  60.9 2.3 %shard_map.71 = (f32[5120,256]{1,0:T(8,128)S(1)}, bf16[5120,256]{1,0:T(8,128)(2,1)S(1)}) custom-call(bf16[2048,512]{1,0:T(8,128)(2,1)S(1)} %bitcast.11), custom_call_target="tpu_custom_call" | custom-call | flops 1000000000 | bytes 1048576 | tf_op jit(solution)/shard_map/pallas_call | solution.py:369
  63.2 3.6 %shard_map.70.refs_8_ = bf16[1024,128]{1,0:T(8,128)(2,1)S(1)} custom-call(s32[2]{0:T(128)S(1)} %copy-done.11, bf16[2048,512]{1,0:T(8,128)(2,1)S(1)} %bitcast.12, bf16[2048,512]{1,0:T(8,128)(2,1)S(1)} %collective-permute-done.refs_0_.theirs, f32[5120,256]{1,0:T(8,128)S(1)} %get-tuple-element.51.slope_m, f32[5120,256]{1,0:T(8,128)S(1)} %get-tuple-element.52.slope_t, ...), custom_call_target="tpu_custom_call" | custom-call | flops 4000000000 | bytes 1048576 | tf_op jit(solution)/shard_map/pallas_call | solution.py:369
  66.8 0.0 collective-permute-done.5.refs_3_
  66.8 0.5 collective-permute-start.6
  67.3 3.0 %shard_map.72 = (f32[1024,128]{1,0:T(8,128)S(1)}, f32[1024,128]{1,0:T(8,128)S(1)}) custom-call(s32[2]{0:T(128)S(1)} %copy-done.11, bf16[2048,512]{1,0:T(8,128)(2,1)S(1)} %bitcast.13, f32[5120,256]{1,0:T(8,128)S(1)} %get-tuple-element.58.refs_0_, bf16[5120,256]{1,0:T(8,128)(2,1)S(1)} %get-tuple-element.59.refs_1_, ...), custom_call_target="tpu_custom_call" | custom-call | flops 3000000000 | bytes 1048576 | tf_op jit(solution)/shard_map/pallas_call | solution.py:369
  70.3 0.0 collective-permute-done.4.refs_3_
  70.3 0.0 collective-permute-done.6.refs_4_
  70.3 3.0 %shard_map.73 = bf16[1024,512]{1,0:T(8,128)(2,1)S(1)} custom-call(s32[2]{0:T(128)S(1)} %copy-done.11, bf16[2048,512]{1,0:T(8,128)(2,1)S(1)} %bitcast.14, bf16[2048,512]{1,0:T(8,128)(2,1)S(1)} %collective-permute-done.refs_0_.theirs, f32[5120,256]{1,0:T(8,128)S(1)} %get-tuple-element.43.refs_1_, bf16[5120,256]{1,0:T(8,128)(2,1)S(1)} %get-tuple-element.44.refs_2_, ...), custom_call_target="tpu_custom_call" | custom-call | flops 3000000000 | bytes 1048576 | tf_op jit(solution)/shard_map/pallas_call | solution.py:369
  73.3 0.0 copy-start.1
  73.3 20.2 %all_to_all.28 = bf16[8,128,512]{2,1,0:T(8,128)(2,1)S(1)} all-to-all(bf16[8,128,512]{2,1,0:T(8,128)(2,1)S(1)} %bitcast.15), channel_id=1, replica_groups=mesh['y'=4,'p'=2,'w'=2,'c'=2,'row'=4] {'y','w'}, dimensions={0} | all-to-all | bytes 2097152 | tf_op jit(solution)/shard_map/all_to_all | solution.py:495
  93.6 0.0 copy-done.7
  93.6 1.9 %shard_map.74 = bf16[512,640]{1,0:T(8,128)(2,1)S(1)} custom-call(s32[2]{0:T(128)S(1)} %copy-done.11, bf16[1024,512]{1,0:T(8,128)(2,1)S(1)} %bitcast.16, f32[256,2048]{1,0:T(8,128)S(1)} %copy-done.3, f32[256,512]{1,0:T(8,128)S(1)} %get-tuple-element.65.normed, f32[256,128]{1,0:T(8,128)S(1)} %get-tuple-element.66.inverse, bf16[256,512]{1,0:T(8,128)(2,1)S(1)} %bitcast.19, ...), custom_call_target="tpu_custom_call" | custom-call | flops 1000000000 | bytes 1048576 | tf_op jit(solution)/shard_map/pallas_call | solution.py:369
  95.5 0.2 reshape.22
  95.7 22.0 %all_to_all.29 = bf16[128,4,640]{2,1,0:T(4,128)(2,1)S(1)} all-to-all(bf16[128,4,640]{2,1,0:T(4,128)(2,1)S(1)} %reshape.22), channel_id=1, replica_groups=mesh['y'=4,'p'=2,'w'=2,'c'=2,'row'=4] {'c','y','p','w','row'}, dimensions={0} | all-to-all | bytes 1310720 | tf_op jit(solution)/shard_map/all_to_all | solution.py:503
  117.7 0.1 reshape.23.got
  117.8 1.7 %shard_map.75 = f32[1024,512]{1,0:T(8,128)} custom-call(bf16[512,640]{1,0:T(8,128)(2,1)S(1)} %reshape.23.got), custom_call_target="tpu_custom_call" | custom-call | tf_op jit(solution)/shard_map/pallas_call | solution.py:506
  (10 shorter events, 0.0 us)
Async XLA Ops:
  3.8 7.8 %copy-start.4 = (bf16[2,128,512]{2,1,0:T(8,128)(2,1)S(1)}, bf16[2,128,512]{2,1,0:T(8,128)(2,1)}, u32[]{:S(2)}) copy-start(bf16[2,128,512]{2,1,0:T(8,128)(2,1)} %param.7) | copy-start | bytes 786436
  3.8 7.8 %copy-start.5 = (bf16[512,512]{1,0:T(8,128)(2,1)S(1)}, bf16[512,512]{1,0:T(8,128)(2,1)}, u32[]{:S(2)}) copy-start(bf16[512,512]{1,0:T(8,128)(2,1)} %w_outer.1) | copy-start | bytes 1572868
  3.8 7.8 %copy-start.12 = (s32[2,128]{1,0:T(2,128)S(1)}, s32[2,128]{1,0:T(2,128)}, u32[]{:S(2)}) copy-start(s32[2,128]{1,0:T(2,128)} %param.11) | copy-start | bytes 3076
  3.8 37.4 %all-to-all-start = ((bf16[16,128,512]{2,1,0:T(8,128)(2,1)}), bf16[16,128,512]{2,1,0:T(8,128)(2,1)S(1)}, u32[]{:S(2)}, u32[]{:S(2)}) async-start(bf16[16,128,512]{2,1,0:T(8,128)(2,1)} %bitcast.23), calls=%async_computation | async-start | bytes 4194304 | tf_op jit(solution)/shard_map/all_to_all | solution.py:405
  11.6 1.6 %copy-start = (bf16[512,2048]{1,0:T(8,128)(2,1)S(1)}, bf16[512,2048]{1,0:T(8,128)(2,1)}, u32[]{:S(2)}) copy-start(bf16[512,2048]{1,0:T(8,128)(2,1)} %w_inner.3) | copy-start | bytes 6291460
  13.2 0.9 copy-start.8
  14.1 29.2 %copy-start.11 = (s32[2]{0:T(128)S(1)}, s32[2]{0:T(128)}, u32[]{:S(2)}) copy-start(s32[2]{0:T(128)} %lengths.13) | copy-start | bytes 28
  15.8 1.3 %copy-start.2 = (f32[256,2048]{1,0:T(8,128)}, f32[256,2048]{1,0:T(8,128)S(1)}, u32[]{:S(2)}) copy-start(f32[256,2048]{1,0:T(8,128)S(1)} %get-tuple-element.64.slope) | copy-start | bytes 6291460
  17.1 0.7 copy-start.6
  17.8 0.6 copy-start.9
  41.3 5.9 %collective-permute-start = (bf16[2048,512]{1,0:T(8,128)(2,1)S(1)}, bf16[2048,512]{1,0:T(8,128)(2,1)S(1)}, u32[]{:S(2)}, u32[]{:S(2)}) collective-permute-start(bf16[2048,512]{1,0:T(8,128)(2,1)S(1)} %bitcast.7), channel_id=1, source_target_pairs={{0,4},{4,0},{1,5},{5,1},{2,6},{6,2},{3,7},{7,3},{8,12},{12,8},{9,1... | collective-permute-start | bytes 6291464 | tf_op jit(solution)/shard_map/ppermute | solution.py:420
  50.5 5.0 %collective-permute-start.3 = (f32[8,1024]{1,0:T(8,128)S(1)}, f32[8,1024]{1,0:T(8,128)S(1)}, u32[]{:S(2)}, u32[]{:S(2)}) collective-permute-start(f32[8,1024]{1,0:T(8,128)S(1)} %get-tuple-element.40.s0), channel_id=1, source_target_pairs={{0,40},{8,32},{32,8},{40,0},{64,104},{72,96},{96,72},{104,64},{1,4... | collective-permute-start | bytes 98312 | tf_op jit(solution)/shard_map/ppermute | solution.py:435
  50.5 5.0 %collective-permute-start.2 = (f32[8,1024]{1,0:T(8,128)S(1)}, f32[8,1024]{1,0:T(8,128)S(1)}, u32[]{:S(2)}, u32[]{:S(2)}) collective-permute-start(f32[8,1024]{1,0:T(8,128)S(1)} %get-tuple-element.40.s0), channel_id=1, source_target_pairs={{0,32},{8,40},{32,0},{40,8},{64,96},{72,104},{96,64},{104,72},{1,3... | collective-permute-start | bytes 98312 | tf_op jit(solution)/shard_map/ppermute | solution.py:435
  52.1 3.5 %collective-permute-start.1 = (f32[8,1024]{1,0:T(8,128)S(1)}, f32[8,1024]{1,0:T(8,128)S(1)}, u32[]{:S(2)}, u32[]{:S(2)}) collective-permute-start(f32[8,1024]{1,0:T(8,128)S(1)} %get-tuple-element.40.s0), channel_id=1, source_target_pairs={{0,8},{8,0},{32,40},{40,32},{64,72},{72,64},{96,104},{104,96},{1,9... | collective-permute-start | bytes 98312 | tf_op jit(solution)/shard_map/ppermute | solution.py:435
  57.0 9.8 %collective-permute-start.5 = (bf16[1024,128]{1,0:T(8,128)(2,1)S(1)}, bf16[1024,128]{1,0:T(8,128)(2,1)S(1)}, u32[]{:S(2)}, u32[]{:S(2)}) collective-permute-start(bf16[1024,128]{1,0:T(8,128)(2,1)S(1)} %get-tuple-element.53.grad_attn.refs_2_), channel_id=1, source_target_pairs={{0,16},{4,20},{16,0},{20,4},{1,17},{5,21},{17,1},{21,5},{2,18},{6,... | collective-permute-start | bytes 786440 | tf_op jit(solution)/shard_map/ppermute | solution.py:452
  58.5 11.8 %collective-permute-start.4 = (bf16[1024,128]{1,0:T(8,128)(2,1)S(1)}, bf16[1024,128]{1,0:T(8,128)(2,1)S(1)}, u32[]{:S(2)}, u32[]{:S(2)}) collective-permute-start(bf16[1024,128]{1,0:T(8,128)(2,1)S(1)} %get-tuple-element.53.grad_attn.refs_2_), channel_id=1, source_target_pairs={{0,4},{4,0},{16,20},{20,16},{1,5},{5,1},{17,21},{21,17},{2,6},{6,2... | collective-permute-start | bytes 786440 | tf_op jit(solution)/shard_map/ppermute | solution.py:452
  66.8 3.5 %collective-permute-start.6 = (bf16[1024,128]{1,0:T(8,128)(2,1)S(1)}, bf16[1024,128]{1,0:T(8,128)(2,1)S(1)}, u32[]{:S(2)}, u32[]{:S(2)}) collective-permute-start(bf16[1024,128]{1,0:T(8,128)(2,1)S(1)} %collective-permute-done.5.refs_3_), channel_id=1, source_target_pairs={{0,4},{4,0},{1,5},{5,1},{2,6},{6,2},{3,7},{7,3},{8,12},{12,8},{9,1... | collective-permute-start | bytes 786440 | tf_op jit(solution)/shard_map/ppermute | solution.py:470
  70.3 23.3 %copy-start.3 = (f32[256,2048]{1,0:T(8,128)S(1)}, f32[256,2048]{1,0:T(8,128)}, u32[]{:S(2)}) copy-start(f32[256,2048]{1,0:T(8,128)} %copy-done.2) | copy-start | bytes 6291460
  70.3 23.3 %copy-start.7 = (bf16[512,256]{1,0:T(8,128)(2,1)S(1)}, bf16[512,256]{1,0:T(8,128)(2,1)}, u32[]{:S(2)}) copy-start(bf16[512,256]{1,0:T(8,128)(2,1)} %copy-done.6) | copy-start | bytes 786436
  70.3 23.3 %copy-start.10 = (bf16[256,128]{1,0:T(8,128)(2,1)S(1)}, bf16[256,128]{1,0:T(8,128)(2,1)}, u32[]{:S(2)}) copy-start(bf16[256,128]{1,0:T(8,128)(2,1)} %copy-done.9) | copy-start | bytes 196612
  73.3 20.2 %copy-start.1 = (bf16[512,2048]{1,0:T(8,128)(2,1)S(1)}, bf16[512,2048]{1,0:T(8,128)(2,1)}, u32[]{:S(2)}) copy-start(bf16[512,2048]{1,0:T(8,128)(2,1)} %w_inner.3) | copy-start | bytes 6291460

commit v6 on v5

--- a/solution.py
+++ b/solution.py
@@ -51,7 +51,7 @@
     events_hbm, grad_hbm, w_hbm, w_outer_hbm, send, events, grad_out, weights, w_outer, parts, sems
 ):
     copies = [pltpu.make_async_copy(events_hbm, events, sems.at[4])]
-    for part in (1, 2, 3, 0):
+    for part in (1, 3, 2, 0):
         cols = slice(part * D, (part + 1) * D)
         copies.append(pltpu.make_async_copy(w_hbm.at[:, cols], weights.at[part], sems.at[part]))
     copies.append(pltpu.make_async_copy(w_outer_hbm, w_outer, sems.at[5]))
@@ -61,7 +61,7 @@
     leaving = []
     copies[0].wait()
     normed = normalize(events[...].astype(F32))[0].astype(BF16)
-    for slot, part in enumerate((1, 2, 3, 0)):
+    for slot, part in enumerate((1, 3, 2, 0)):
         copies[slot + 1].wait()
         act = silu(dot(normed, weights[part])).astype(BF16)
         if part == 0:
@@ -71,9 +71,8 @@
         for g in range(2):
             for h in range(HEADS):
                 piece = act[g * BLK : (g + 1) * BLK, h * HD : (h + 1) * HD]
-                for p in range(2):
-                    at = (p * 8 + g * HEADS + h) * BLK
-                    parts[slot, at : at + BLK, :] = piece
+                at = (g * HEADS + h) * BLK
+                parts[slot, at : at + BLK, :] = piece
         cols = slice(slot * HD, (slot + 1) * HD)
         leaving.append(pltpu.make_async_copy(parts.at[slot], send.at[:, cols], sems.at[7 + slot]))
         leaving[-1].start()
@@ -118,7 +117,7 @@
     )
 
 
-V_COLS, Q_COLS, K_COLS, G_COLS = (slice(i * HD, (i + 1) * HD) for i in range(4))
+V_COLS, K_COLS, Q_COLS, G_COLS = (slice(i * HD, (i + 1) * HD) for i in range(4))
 GRP = 2 * BLK
 
 
@@ -132,10 +131,6 @@
 
 def inverse_of(length):
     return 1.0 / jnp.full((1, HD), length, jnp.int32).astype(F32)
-
-
-def at_rows(p, start, count):
-    return pl.ds(pl.multiple_of(p * 1024 + start, GRP), count)
 
 
 def diagonal(row_place, col_place, rows_are_keys):
@@ -159,41 +154,44 @@
     return jnp.concatenate([values[:-GRP, :], last], axis=0) if values.shape[0] > GRP else last
 
 
-def query_rows(y, part):
-    start = (y * (9 - y) + part * (4 - y)) * GRP
+def part_place(part):
+    p, c = my_place()
+    return (1 - p if part & 2 else p), (1 - c if part & 1 else c)
+
+
+def query_rows(y):
+    start = y * (9 - y) // 2 * GRP
     return slice(start, start + (4 - y) * GRP)
 
 
-def forward_kernel(last, lengths, mine, *refs):
-    place = my_place()
-    p = place[0]
-    if last:
-        theirs, before, out, slope_out, stats, grad = refs
-        keys_of, core = theirs, 1 - place[1]
-        grad[...] = mine[at_rows(p, 0, 1024), G_COLS]
-        out[...] = before[...]
-    else:
-        out, slope_out = refs
-        keys_of, core = mine, place[1]
-        out[...] = jnp.zeros_like(out)
+def forward_kernel(part_ids, lengths, own, *refs):
+    count = len(part_ids)
+    first, last = part_ids[0] == 0, part_ids[-1] == 3
+    keys_of, refs = refs[:count], refs[count:]
+    if not first:
+        before, *refs = refs
+    out, *refs = refs
+    slopes_out, refs = refs[:count], refs[count:]
+    out[...] = jnp.zeros_like(out) if first else before[...]
     for y in range(4):
         rows = slice(y * GRP, 1024)
-        queries = mine[at_rows(p, y * GRP, 1024 - y * GRP), Q_COLS]
-        for part in range(2):
-            keys = slice(part * 1024 + y * GRP, part * 1024 + (y + 1) * GRP)
-            slope, attn = slopes(dot_t(queries, keys_of[keys, K_COLS]))
-            mask = diagonal(place, (part, core), False)
-            slope_out[query_rows(y, part), :] = mask_first(mask, slope)
+        queries = own[rows, Q_COLS]
+        keys = slice(y * GRP, (y + 1) * GRP)
+        for part, src, slope_out in zip(part_ids, keys_of, slopes_out):
+            slope, attn = slopes(dot_t(queries, src[keys, K_COLS]))
+            mask = diagonal(my_place(), part_place(part), False)
+            slope_out[query_rows(y), :] = mask_first(mask, slope)
             attn = mask_first(mask, attn)
-            out[rows, :] += dot(attn.astype(BF16), keys_of[keys, V_COLS])
+            out[rows, :] += dot(attn.astype(BF16), src[keys, V_COLS])
     if not last:
         return
+    (stats,) = refs
     inv_len = inverse_of(my_length(lengths))
     for m in range(8):
         rows = slice(m * BLK, (m + 1) * BLK)
         total = out[rows, :] * inv_len
         out[rows, :] = total
-        g = grad[rows, :].astype(F32)
+        g = own[rows, G_COLS].astype(F32)
         mean = jnp.mean(total, axis=-1, keepdims=True)
         center = total - mean
         square = jnp.sum(center * center, axis=-1, keepdims=True)
@@ -206,7 +204,7 @@
         stats[:, rows] = jnp.transpose(packed)[:8, :]
 
 
-def grad_attn_kernel(lengths, attn_out, grad, s0, s1, s2, s3, grad_attn, normed_out):
+def grad_attn_kernel(lengths, attn_out, own, s0, s1, s2, s3, grad_attn, normed_out):
     p, c = my_place()
     length = my_length(lengths)
     parts = [s0[...], s1[...], s2[...], s3[...]]
@@ -215,8 +213,8 @@
     square = 0.0
     sum_g = 0.0
     sum_ga = 0.0
-    for part, own in zip(parts, means):
-        shift = own - mean
+    for part, local_mean in zip(parts, means):
+        shift = local_mean - mean
         square = square + part[1:2, :] + HD * (shift * shift)
         sum_g = sum_g + part[2:3, :]
         sum_ga = sum_ga + part[3:4, :] + part[2:3, :] * shift
@@ -232,7 +230,7 @@
         cols = jnp.transpose(packed[:, rows])
         inv = cols[:, 1:2]
         n = (attn_out[rows, :] - cols[:, 0:1]) * inv
-        back = (grad[rows, :].astype(F32) - cols[:, 2:3] - n * cols[:, 3:4]) * inv
+        back = (own[rows, G_COLS].astype(F32) - cols[:, 2:3] - n * cols[:, 3:4]) * inv
         pos = lax.broadcasted_iota(jnp.int32, (BLK, 1), 0)
         pos = pos + (m // 2 * 8 + 4 * p + m % 2 * 2 + c) * BLK
         grad_attn[rows, :] = jnp.where(pos < length, back, 0.0).astype(BF16)
@@ -246,72 +244,58 @@
     return two_sigma + half * (1.0 - t * t), half * two_sigma
 
 
-def grad_query_kernel(lengths, mine, theirs, slope_m, slope_t, grad_attn, ret, total):
+def grad_query_kernel(lengths, grad_attn, *refs):
+    keys_of, slopes_of, (ret, total) = refs[:4], refs[4:8], refs[8:]
     total[...] = jnp.zeros_like(total)
     for y in range(4):
         rows = slice(y * GRP, 1024)
-        for part in range(2):
-            keys = slice(part * 1024 + y * GRP, part * 1024 + (y + 1) * GRP)
-            for src, slope in ((mine, slope_m), (theirs, slope_t)):
-                score = slope[query_rows(y, part), :] * dot_t(grad_attn[rows, :], src[keys, V_COLS])
-                total[rows, :] += dot(score.astype(BF16), src[keys, K_COLS])
+        keys = slice(y * GRP, (y + 1) * GRP)
+        for src, slope in zip(keys_of, slopes_of):
+            score = slope[query_rows(y), :] * dot_t(grad_attn[rows, :], src[keys, V_COLS])
+            total[rows, :] += dot(score.astype(BF16), src[keys, K_COLS])
     inv_len = inverse_of(my_length(lengths))
     ret[...] = (total[...] * (0.5 * SCALE * inv_len)).astype(BF16)
 
 
-PACKED = 20 * GRP
-
-
-def packed_rows(y, other):
-    start = (y + 1) * (y + other) * GRP
+PACKED = 10 * GRP
+
+
+def packed_rows(y):
+    start = y * (y + 1) // 2 * GRP
     return slice(start, start + (y + 1) * GRP)
 
 
-def key_scores_kernel(theirs_too, mine, *refs):
-    place = my_place()
-    p = place[0]
-    if theirs_too:
-        src, slope_out, attn_out = refs
-        core = 1 - place[1]
-    else:
-        slope_out, attn_out = refs
-        src, core = mine, place[1]
+def key_scores_kernel(part_ids, own, *refs):
+    queries_of, outs = refs[:2], (refs[2:4], refs[4:6])
     for y in range(4):
-        count = (y + 1) * GRP
-        keys = mine[at_rows(p, 0, count), K_COLS]
-        for other in range(2):
-            part = 1 - p if other else p
-            slope, attn = slopes(dot_t(keys, src[at_rows(part, y * GRP, GRP), Q_COLS]))
-            mask = diagonal(place, (part, core), True)
-            rows = packed_rows(y, other)
-            slope_out[rows, :] = mask_last(mask, slope)
-            attn_out[rows, :] = mask_last(mask, attn).astype(BF16)
-
-
-def grad_key_kernel(last, lengths, mine, *refs):
-    p = lax.axis_index("p")
+        keys = own[: (y + 1) * GRP, K_COLS]
+        events = slice(y * GRP, (y + 1) * GRP)
+        for part, src, (slope_out, attn_out) in zip(part_ids, queries_of, outs):
+            slope, attn = slopes(dot_t(keys, src[events, :]))
+            mask = diagonal(my_place(), part_place(part), True)
+            slope_out[packed_rows(y), :] = mask_last(mask, slope)
+            attn_out[packed_rows(y), :] = mask_last(mask, attn).astype(BF16)
+
+
+def grad_key_kernel(last, lengths, own, *refs):
+    queries_of, scores, grads_of, refs = refs[:2], (refs[2:4], refs[4:6]), refs[6:8], refs[8:]
     if last:
-        theirs, slope, attn, g_here, g_there, k_before, v_before, normed_out, grad_q, *refs = refs
-        ret, grad_k, grad_v = refs
-        src = theirs
+        k_before, v_before, normed_out, grad_q, ret, grad_k, grad_v = refs
         grad_k[...] = k_before[...]
         grad_v[...] = v_before[...]
     else:
-        slope, attn, g_here, g_there, grad_k, grad_v = refs
-        src = mine
+        grad_k, grad_v = refs
         grad_k[...] = jnp.zeros_like(grad_k)
         grad_v[...] = jnp.zeros_like(grad_v)
     for y in range(4):
-        count = (y + 1) * GRP
-        rows = slice(0, count)
-        values = mine[at_rows(p, 0, count), V_COLS]
-        for other, grad_attn in enumerate((g_here, g_there)):
-            ga = grad_attn[y * GRP : (y + 1) * GRP, :]
-            q = src[at_rows(1 - p if other else p, y * GRP, GRP), Q_COLS]
-            packed = packed_rows(y, other)
-            score = slope[packed, :] * dot_t(values, ga)
-            grad_k[rows, :] += dot(score.astype(BF16), q)
-            grad_v[rows, :] += dot(attn[packed, :], ga)
+        rows = slice(0, (y + 1) * GRP)
+        events = slice(y * GRP, (y + 1) * GRP)
+        values = own[rows, V_COLS]
+        for q, (slope, attn), grad_attn in zip(queries_of, scores, grads_of):
+            ga = grad_attn[events, :]
+            score = slope[packed_rows(y), :] * dot_t(values, ga)
+            grad_k[rows, :] += dot(score.astype(BF16), q[events, :])
+            grad_v[rows, :] += dot(attn[packed_rows(y), :], ga)
     if last:
         inv_len = inverse_of(my_length(lengths))
         ret[:, :HD] = normed_out[...]
@@ -381,7 +365,7 @@
     hbm = pl.BlockSpec(memory_space=pltpu.HBM)
     return pl.pallas_call(
         project_kernel,
-        out_shape=jax.ShapeDtypeStruct((16 * BLK, 4 * HD), BF16),
+        out_shape=jax.ShapeDtypeStruct((8 * BLK, 4 * HD), BF16),
         in_specs=[hbm] * len(args),
         out_specs=hbm,
         scratch_shapes=[
@@ -389,7 +373,7 @@
             pltpu.VMEM((2 * BLK, D), BF16),
             pltpu.VMEM((4, D, D), BF16),
             pltpu.VMEM((D, D), BF16),
-            pltpu.VMEM((4, 16 * BLK, HD), BF16),
+            pltpu.VMEM((4, 8 * BLK, HD), BF16),
             pltpu.SemaphoreType.DMA((11,)),
         ],
         compiler_params=pltpu.CompilerParams(vmem_limit_bytes=PROJECT_LIMIT),
@@ -400,9 +384,9 @@
     events = events.reshape(2 * BLK, D)
     grad_out = grad_out.reshape(2 * BLK, D)
     rows_bf16, rows_f32 = ((1024, HD), BF16), ((1024, HD), F32)
-    swap_c = [(0, 1), (1, 0)]
+    swap = [(0, 1), (1, 0)]
     send = project(events, grad_out, w_inner, w_outer)
-    mine = lax.all_to_all(send, ("p", "y", "w"), 0, 0, tiled=True)
+    own = lax.all_to_all(send, ("y", "w"), 0, 0, tiled=True)
     slope, normed, inverse, hot, ext = call(
         gate_kernel,
         [
@@ -416,62 +400,66 @@
         scalars=0,
         flops=2 * 10**9,
     )
-    mine, slope = lax.optimization_barrier((mine, slope))
-    theirs = lax.ppermute(mine, "c", swap_c)
-    score_shapes = [((PACKED, GRP), F32), ((PACKED, GRP), BF16)]
-    attn_one, slope_m = call(
-        functools.partial(forward_kernel, False),
-        [rows_f32, score_shapes[0]],
-        (valid_lengths, mine),
-        flops=10**9,
-    )
-    attn_out, slope_t, stats, grad = call(
-        functools.partial(forward_kernel, True),
-        [rows_f32, score_shapes[0], ((8, 1024), F32), rows_bf16],
-        (valid_lengths, mine, theirs, attn_one),
-        flops=10**9,
-    )
+    own, slope = lax.optimization_barrier((own, slope))
+    slope_shape, score_shapes = ((PACKED, GRP), F32), [((PACKED, GRP), F32), ((PACKED, GRP), BF16)]
+    vk, q = own[:, : 2 * HD], own[:, Q_COLS]
+    vk_p = lax.ppermute(vk, "p", swap)
+    vk_c = lax.ppermute(vk, "c", swap)
+    q_c = lax.ppermute(q, "c", swap)
+
+    def forward(part_ids, keys, before, extra=()):
+        return call(
+            functools.partial(forward_kernel, part_ids),
+            [rows_f32] + [slope_shape] * len(keys) + list(extra),
+            (valid_lengths, own, *keys, *before),
+            flops=10**9 * len(keys) // 2,
+        )
+
+    def key_scores(part_ids, src, queries):
+        return call(
+            functools.partial(key_scores_kernel, part_ids),
+            score_shapes * 2,
+            (src, *queries),
+            scalars=0,
+            flops=10**9,
+        )
+
+    attn_out, slope_o, slope_c = forward((0, 1), (own, vk_c), ())
+    scores_one = key_scores((0, 1), own, (q, q_c))
+    vk_p, attn_out, scores_one, q_late = lax.optimization_barrier((vk_p, attn_out, scores_one, q))
+    vk_pc = lax.ppermute(vk_p, "c", swap)
+    q_p = lax.ppermute(q_late, "p", swap)
+    attn_out, slope_p = forward((2,), (vk_p,), (attn_out,))
+    attn_out, slope_pc, stats = forward((3,), (vk_pc,), (attn_out,), [((8, 1024), F32)])
     others = [
         lax.ppermute(stats, ("y", "w"), [(i, i ^ m) for i in range(8)]) for m in (1, 2, 3)
     ]
-    scores_t = call(
-        functools.partial(key_scores_kernel, True),
-        score_shapes,
-        (mine, theirs),
-        scalars=0,
-        flops=10**9,
-    )
-    others, scores_t = lax.optimization_barrier((others, scores_t))
+    q_p, others = lax.optimization_barrier((q_p, others))
+    q_pc = lax.ppermute(q_p, "c", swap)
     grad_attn, normed_out = call(
         grad_attn_kernel,
         [rows_bf16, rows_bf16],
-        (valid_lengths, attn_out, grad, stats, *others),
+        (valid_lengths, attn_out, own, stats, *others),
         flops=10**7,
     )
     grad_p, grad_c = [
         lax.ppermute(grad_attn, ("p", "c"), [(i, i ^ m) for i in range(4)]) for m in (2, 1)
     ]
-    mine_late, grad_attn = lax.optimization_barrier((mine, grad_attn))
-    scores_m = call(
-        functools.partial(key_scores_kernel, False),
-        score_shapes,
-        (mine_late,),
-        scalars=0,
-        flops=10**9,
-    )
+    own_late, grad_attn = lax.optimization_barrier((own, grad_attn))
+    scores_two = key_scores((2, 3), own_late, (q_p, q_pc))
     (grad_q,) = call(
         grad_query_kernel,
         [rows_bf16],
-        (valid_lengths, mine, theirs, slope_m, slope_t, grad_attn),
+        (valid_lengths, grad_attn, own, vk_c, vk_p, vk_pc, slope_o, slope_c, slope_p, slope_pc),
         scratch=[rows_f32],
         flops=4 * 10**9,
     )
-    grad_p, grad_q, scores_m = lax.optimization_barrier((grad_p, grad_q, scores_m))
-    grad_pc = lax.ppermute(grad_p, "c", swap_c)
+    grad_p, grad_q, scores_two = lax.optimization_barrier((grad_p, grad_q, scores_two))
+    grad_pc = lax.ppermute(grad_p, "c", swap)
     grad_k, grad_v = call(
         functools.partial(grad_key_kernel, False),
         [rows_f32, rows_f32],
-        (valid_lengths, mine, *scores_m, grad_attn, grad_p),
+        (valid_lengths, own, q, q_c, *scores_one, grad_attn, grad_c),
         flops=3 * 10**9,
     )
     (ret,) = call(
@@ -479,10 +467,11 @@
         [((1024, 4 * HD), BF16)],
         (
             valid_lengths,
-            mine,
-            theirs,
-            *scores_t,
-            grad_c,
+            own,
+            q_p,
+            q_pc,
+            *scores_two,
+            grad_p,
             grad_pc,
             grad_k,
             grad_v,

time: 120 us -> 117 us (0.975)
  waiting for transfers between devices: 23.7 us -> 17.1 us
  starting transfers between devices: 16.9 us -> 21.8 us
  blocking collectives: 42.3 us -> 40.1 us
    all_to_all x1, waiting for transfers between devices: 22.8 us -> 7.4 us  [local(): own = lax.all_to_all(send, ('y', 'w'), 0, 0, tiled=True)]
    ppermute x2 -> x7, starting transfers between devices: 2.6 us -> 9.7 us  [the longest x1 2.46 us: local(): vk_p = lax.ppermute(vk, 'p', swap)]
    ppermute x2 -> x7, waiting for transfers between devices: 0.9 us -> 6.96 us  [the longest x1 5.61 us: local(): vk_p = lax.ppermute(vk, 'p', swap)]
    all_to_all x1, starting transfers between devices: 7.73 us -> 5.96 us  [local(): own = lax.all_to_all(send, ('y', 'w'), 0, 0, tiled=True)]
    all_to_all x1, blocking collectives: 20.2 us -> 18.5 us  [local(): got = lax.all_to_all(ret, ('y', 'w'), 0, 0, tiled=True)]
    ppermute x3, waiting for transfers between devices: 0.01 us -> 1.44 us  [local(): lax.ppermute(stats, ('y', 'w'), [(i, i ^ m) for i in range(8)])]
    ppermute x2, waiting for transfers between devices: 0.01 us -> 1.33 us  [local(): lax.ppermute(grad_attn, ('p', 'c'), [(i, i ^ m) for i in range(4)])]
    pallas_call x10 -> x11, Pallas kernels: 25.4 us -> 26.4 us  [call(): pl.pallas_call(kernel, out_shape=[jax.ShapeDtypeStruct(shape, dtype) for...]
  transfers between devices with their start and end apart: 8 -> 13, of which waited for: 2 -> 7; matrix products, arithmetic and copies ran while one was open for 0% -> 0% of each run, Pallas kernels for 13% -> 17%
where the time goes in v6:
time: 117 us
  blocking collectives  40.1 us (34%)
  Pallas kernels  31.9 us (27%)
  starting transfers between devices  21.8 us (19%)
  waiting for transfers between devices  17.1 us (15%)
  local copies, waits for them, and re-layouts  5.83 us (5%)
    pallas_call x11, Pallas kernels, call(): pl.pallas_call(kernel, out_shape=[jax.ShapeDtypeStruct(shape, dtype) for...  26.4 us
    all_to_all x1, blocking collectives, local(): lax.all_to_all(rows.reshape(128, CAP, D + EXT), ('c', 'y', 'p', 'w', 'row...  21.5 us
    all_to_all x1, blocking collectives, local(): got = lax.all_to_all(ret, ('y', 'w'), 0, 0, tiled=True)  18.5 us
    all_to_all x1, waiting for transfers between devices, local(): own = lax.all_to_all(send, ('y', 'w'), 0, 0, tiled=True)  7.4 us
    all_to_all x1, starting transfers between devices, local(): own = lax.all_to_all(send, ('y', 'w'), 0, 0, tiled=True)  5.96 us
    ppermute x1, waiting for transfers between devices, local(): vk_p = lax.ppermute(vk, 'p', swap)  5.61 us
    unnamed x28, local copies, waits for them, and re-layouts  5.45 us
    pallas_call x1, Pallas kernels, project(): pl.pallas_call(project_kernel, out_shape=jax.ShapeDtypeStruct((8 * BLK, 4...  3.88 us
  transfers between devices with their start and end apart: 13, of which 7 were waited for; matrix products, arithmetic and copies ran while one was open for 0% of the time, Pallas kernels for 17%

profile of v6, /device:TPU:1, one launch (start us, length us, event | category | flops | bytes accessed | tf_op | source)
XLA Modules:
  0.0 117.1 jit_solution(6701292109635123281)
XLA Ops:
  0.0 3.9 %shard_map.64 = bf16[1024,512]{1,0:T(8,128)(2,1)} custom-call(bf16[256,512]{1,0:T(8,128)(2,1)} %bitcast.24, bf16[256,512]{1,0:T(8,128)(2,1)} %bitcast.21, bf16[512,2048]{1,0:T(8,128)(2,1)} %w_inner.3, bf16[512,512]{1,0:T(8,128)(2,1)} %w_outer.1), custom_call_target="tpu_custom_call" | custom-call | tf_op jit(solution)/shard_map/pallas_call | solution.py:366
  3.9 6.0 %all-to-all-start = ((bf16[8,128,512]{2,1,0:T(8,128)(2,1)}), bf16[8,128,512]{2,1,0:T(8,128)(2,1)S(1)}, u32[]{:S(2)}, u32[]{:S(2)}) async-start(bf16[8,128,512]{2,1,0:T(8,128)(2,1)} %bitcast.27), calls=%async_computation | async-start | bytes 2097152 | tf_op jit(solution)/shard_map/all_to_all | solution.py:389
  9.9 0.0 copy-start.6
  9.9 1.0 copy-done.6
  10.9 0.9 copy-done.9
  11.9 1.6 %shard_map.65 = (f32[256,2048]{1,0:T(8,128)S(1)}, f32[256,512]{1,0:T(8,128)S(1)}, f32[256,128]{1,0:T(8,128)S(1)}, bf16[512,256]{1,0:T(8,128)(2,1)S(1)}, bf16[256,128]{1,0:T(8,128)(2,1)S(1)}) custom-call(bf16[256,512]{1,0:T(8,128)(2,1)S(1)} %bitcast.25, bf16[256,512]{1,0:T(8,128)(2,1)S(1)} %bitcast.22, bf16[512,2048]{1,0:T(8,128)(2,1)S(1)} %copy-done, ...), custom_call_target="tpu_custom_call" | custom-call | flops 2000000000 | bytes 1048576 | tf_op jit(solution)/shard_map/pallas_call | solution.py:353
  13.5 0.0 copy-start.1
  13.5 1.3 %copy-done.1 = f32[256,2048]{1,0:T(8,128)} copy-done((f32[256,2048]{1,0:T(8,128)}, f32[256,2048]{1,0:T(8,128)S(1)}, u32[]{:S(2)}) %copy-start.1) | copy-done | bytes 2097176
  14.8 0.8 copy-done.4
  15.6 0.7 copy-done.7
  16.3 0.6 copy-done.10
  16.9 7.4 %all-to-all-done = bf16[8,128,512]{2,1,0:T(8,128)(2,1)S(1)} async-done(((bf16[8,128,512]{2,1,0:T(8,128)(2,1)}), bf16[8,128,512]{2,1,0:T(8,128)(2,1)S(1)}, u32[]{:S(2)}, u32[]{:S(2)}) %all-to-all-start) | async-done | bytes 1048608 | tf_op jit(solution)/shard_map/all_to_all | solution.py:389
  24.4 2.2 %collective-permute-start.1 = (bf16[1024,256]{1,0:T(8,128)(2,1)S(1)}, bf16[1024,256]{1,0:T(8,128)(2,1)S(1)}, u32[]{:S(2)}, u32[]{:S(2)}) collective-permute-start(bf16[1024,256]{1,0:T(8,128)(2,1)S(1)} %slice.6), channel_id=1, source_target_pairs={{0,4},{4,0},{1,5},{5,1},{2,6},{6,2},{3,7},{7,3},{8,12},{12,8},{9,1... | collective-permute-start | bytes 1572872 | tf_op jit(solution)/shard_map/ppermute | solution.py:407
  26.6 2.5 %collective-permute-start = (bf16[1024,256]{1,0:T(8,128)(2,1)S(1)}, bf16[1024,256]{1,0:T(8,128)(2,1)S(1)}, u32[]{:S(2)}, u32[]{:S(2)}) collective-permute-start(bf16[1024,256]{1,0:T(8,128)(2,1)S(1)} %slice.6), channel_id=1, source_target_pairs={{0,16},{16,0},{1,17},{17,1},{2,18},{18,2},{3,19},{19,3},{4,20},{20... | collective-permute-start | bytes 1572872 | tf_op jit(solution)/shard_map/ppermute | solution.py:406
  29.1 0.4 collective-permute-start.2
  29.6 1.2 %collective-permute-done.2.refs_1_ = bf16[1024,128]{1,0:T(8,128)(2,1)S(1)} collective-permute-done((bf16[1024,128]{1,0:T(8,128)(2,1)S(1)}, bf16[1024,128]{1,0:T(8,128)(2,1)S(1)}, u32[]{:S(2)}, u32[]{:S(2)}) %collective-permute-start.2) | collective-permute-done | bytes 262176 | tf_op jit(solution)/shard_map/ppermute | solution.py:408
  30.8 2.4 %shard_map.67 = (f32[2560,256]{1,0:T(8,128)S(1)}, bf16[2560,256]{1,0:T(8,128)(2,1)S(1)}, f32[2560,256]{1,0:T(8,128)S(1)}, bf16[2560,256]{1,0:T(8,128)(2,1)S(1)}) custom-call(bf16[1024,512]{1,0:T(8,128)(2,1)S(1)} %bitcast.9, bf16[1024,128]{1,0:T(8,128)(2,1)S(1)} %slice.7.refs_0_, bf16[1024,128]{1,0:T(8,128)(2,1)S(1)} %collective-permute-done.2.refs_1_), custom_call_target="tpu_custom_call" | custom-call | flops 1000000000 | bytes 1048576 | tf_op jit(solution)/shard_map/pallas_call | solution.py:353
  33.1 2.9 %shard_map.66 = (f32[1024,128]{1,0:T(8,128)S(1)}, f32[2560,256]{1,0:T(8,128)S(1)}, f32[2560,256]{1,0:T(8,128)S(1)}) custom-call(s32[2]{0:T(128)S(1)} %copy-done.12, bf16[1024,512]{1,0:T(8,128)(2,1)S(1)} %bitcast.10, bf16[1024,512]{1,0:T(8,128)(2,1)S(1)} %bitcast.11, bf16[1024,256]{1,0:T(8,128)(2,1)S(1)} %collective-permute-done.1.refs_1_), custom_call_target="tpu_custom_call" | custom-call | flops 1000000000 | bytes 1048576 | tf_op jit(solution)/shard_map/pallas_call | solution.py:353
  36.0 5.6 %collective-permute-done.refs_0_.refs_2_ = bf16[1024,256]{1,0:T(8,128)(2,1)S(1)} collective-permute-done((bf16[1024,256]{1,0:T(8,128)(2,1)S(1)}, bf16[1024,256]{1,0:T(8,128)(2,1)S(1)}, u32[]{:S(2)}, u32[]{:S(2)}) %collective-permute-start) | collective-permute-done | bytes 524320 | tf_op jit(solution)/shard_map/ppermute | solution.py:406
  41.6 0.9 collective-permute-start.4
  42.5 2.5 %collective-permute-start.3 = (bf16[1024,128]{1,0:T(8,128)(2,1)S(1)}, bf16[1024,128]{1,0:T(8,128)(2,1)S(1)}, u32[]{:S(2)}, u32[]{:S(2)}) collective-permute-start(bf16[1024,128]{1,0:T(8,128)(2,1)S(1)} %slice.7.refs_0_), channel_id=1, source_target_pairs={{0,16},{16,0},{1,17},{17,1},{2,18},{18,2},{3,19},{19,3},{4,20},{20... | collective-permute-start | bytes 786440 | tf_op jit(solution)/shard_map/ppermute | solution.py:431
  44.9 1.8 %shard_map.68 = (f32[1024,128]{1,0:T(8,128)S(1)}, f32[2560,256]{1,0:T(8,128)S(1)}) custom-call(s32[2]{0:T(128)S(1)} %copy-done.12, bf16[1024,512]{1,0:T(8,128)(2,1)S(1)} %bitcast.12, bf16[1024,256]{1,0:T(8,128)(2,1)S(1)} %collective-permute-done.refs_0_.refs_2_, f32[1024,128]{1,0:T(8,128)S(1)} %get-tuple-element.60.refs_1_), custom_call_target="tpu_custom_call" | custom-call | flops 500000000 | bytes 1048576 | tf_op jit(solution)/shard_map/pallas_call | solution.py:353
  46.8 0.0 collective-permute-done.4.refs_0_.refs_3_
  46.8 2.3 %shard_map.69 = (f32[1024,128]{1,0:T(8,128)S(1)}, f32[2560,256]{1,0:T(8,128)S(1)}, f32[8,1024]{1,0:T(8,128)S(1)}) custom-call(s32[2]{0:T(128)S(1)} %copy-done.12, bf16[1024,512]{1,0:T(8,128)(2,1)S(1)} %bitcast.13, bf16[1024,256]{1,0:T(8,128)(2,1)S(1)} %collective-permute-done.4.refs_0_.refs_3_, f32[1024,128]{1,0:T(8,128)S(1)} %get-tuple-element.61.refs_1_), custom_call_target="tpu_custom_call" | custom-call | flops 500000000 | bytes 1048576 | tf_op jit(solution)/shard_map/pallas_call | solution.py:353
  49.1 0.0 collective-permute-start.7
  49.1 1.2 collective-permute-start.6
  50.3 1.5 %collective-permute-start.5 = (f32[8,1024]{1,0:T(8,128)S(1)}, f32[8,1024]{1,0:T(8,128)S(1)}, u32[]{:S(2)}, u32[]{:S(2)}) collective-permute-start(f32[8,1024]{1,0:T(8,128)S(1)} %get-tuple-element.62.s0), channel_id=1, source_target_pairs={{0,8},{8,0},{32,40},{40,32},{64,72},{72,64},{96,104},{104,96},{1,9... | collective-permute-start | bytes 98312 | tf_op jit(solution)/shard_map/ppermute | solution.py:435
  51.8 0.2 collective-permute-done.3.refs_0_
  51.9 0.9 collective-permute-done.7.s3
  52.8 0.0 collective-permute-done.6.s2
  52.8 0.6 collective-permute-done.5.s1
  53.4 1.4 %shard_map.70 = (bf16[1024,128]{1,0:T(8,128)(2,1)S(1)}, bf16[1024,128]{1,0:T(8,128)(2,1)S(1)}) custom-call(s32[2]{0:T(128)S(1)} %copy-done.12, f32[1024,128]{1,0:T(8,128)S(1)} %get-tuple-element.64.attn_out, bf16[1024,512]{1,0:T(8,128)(2,1)S(1)} %bitcast.14, f32[8,1024]{1,0:T(8,128)S(1)} %get-tuple-element.62.s0, f32[8,1024]{1,0:T(8,128)S(1)} %collective-permute-done.5.s1, ...), custom_call_target="tpu_custom_call" | custom-call | flops 10000000 | bytes 1048576 | tf_op jit(solution)/shard_map/pallas_call | solution.py:353
  54.8 1.7 %collective-permute-start.11 = (bf16[1024,128]{1,0:T(8,128)(2,1)S(1)}, bf16[1024,128]{1,0:T(8,128)(2,1)S(1)}, u32[]{:S(2)}, u32[]{:S(2)}) collective-permute-start(bf16[1024,128]{1,0:T(8,128)(2,1)S(1)} %get-tuple-element.69.grad_attn.refs_6_), channel_id=1, source_target_pairs={{0,4},{4,0},{16,20},{20,16},{1,5},{5,1},{17,21},{21,17},{2,6},{6,2... | collective-permute-start | bytes 786440 | tf_op jit(solution)/shard_map/ppermute | solution.py:446
  56.5 1.7 %collective-permute-start.9 = (bf16[1024,128]{1,0:T(8,128)(2,1)S(1)}, bf16[1024,128]{1,0:T(8,128)(2,1)S(1)}, u32[]{:S(2)}, u32[]{:S(2)}) collective-permute-start(bf16[1024,128]{1,0:T(8,128)(2,1)S(1)} %get-tuple-element.69.grad_attn.refs_6_), channel_id=1, source_target_pairs={{0,16},{4,20},{16,0},{20,4},{1,17},{5,21},{17,1},{21,5},{2,18},{6,... | collective-permute-start | bytes 786440 | tf_op jit(solution)/shard_map/ppermute | solution.py:446
  58.3 0.4 collective-permute-start.8
  58.6 3.6 %shard_map.71.refs_11_ = bf16[1024,128]{1,0:T(8,128)(2,1)S(1)} custom-call(s32[2]{0:T(128)S(1)} %copy-done.12, bf16[1024,128]{1,0:T(8,128)(2,1)S(1)} %get-tuple-element.69.grad_attn.refs_6_, bf16[1024,512]{1,0:T(8,128)(2,1)S(1)} %bitcast.15, bf16[1024,256]{1,0:T(8,128)(2,1)S(1)} %collective-permute-done.1.refs_1_, ...), custom_call_target="tpu_custom_call" | custom-call | flops 4000000000 | bytes 1048576 | tf_op jit(solution)/shard_map/pallas_call | solution.py:353
  62.2 2.4 %shard_map.72 = (f32[2560,256]{1,0:T(8,128)S(1)}, bf16[2560,256]{1,0:T(8,128)(2,1)S(1)}, f32[2560,256]{1,0:T(8,128)S(1)}, bf16[2560,256]{1,0:T(8,128)(2,1)S(1)}) custom-call(bf16[1024,512]{1,0:T(8,128)(2,1)S(1)} %bitcast.16, bf16[1024,128]{1,0:T(8,128)(2,1)S(1)} %collective-permute-done.3.refs_0_, bf16[1024,128]{1,0:T(8,128)(2,1)S(1)} %collective-permute-done.8.refs_1_), custom_call_target="tpu_custom_call" | custom-call | flops 1000000000 | bytes 1048576 | tf_op jit(solution)/shard_map/pallas_call | solution.py:353
  64.6 1.3 %collective-permute-done.9.refs_6_ = bf16[1024,128]{1,0:T(8,128)(2,1)S(1)} collective-permute-done((bf16[1024,128]{1,0:T(8,128)(2,1)S(1)}, bf16[1024,128]{1,0:T(8,128)(2,1)S(1)}, u32[]{:S(2)}, u32[]{:S(2)}) %collective-permute-start.9) | collective-permute-done | bytes 262176 | tf_op jit(solution)/shard_map/ppermute | solution.py:446
  65.9 0.9 collective-permute-start.10
  66.8 3.0 %shard_map.73 = (f32[1024,128]{1,0:T(8,128)S(1)}, f32[1024,128]{1,0:T(8,128)S(1)}) custom-call(s32[2]{0:T(128)S(1)} %copy-done.12, bf16[1024,512]{1,0:T(8,128)(2,1)S(1)} %bitcast.17, bf16[1024,128]{1,0:T(8,128)(2,1)S(1)} %slice.7.refs_0_, bf16[1024,128]{1,0:T(8,128)(2,1)S(1)} %collective-permute-done.2.refs_1_, f32[2560,256]{1,0:T(8,128)S(1)} %get-tuple-element.84.refs_2_, ...), custom_call_target="tpu_custom_call" | custom-call | flops 3000000000 | bytes 1048576 | tf_op jit(solution)/shard_map/pallas_call | solution.py:353
  69.8 3.0 %shard_map.74 = bf16[1024,512]{1,0:T(8,128)(2,1)S(1)} custom-call(s32[2]{0:T(128)S(1)} %copy-done.12, bf16[1024,512]{1,0:T(8,128)(2,1)S(1)} %bitcast.18, bf16[1024,128]{1,0:T(8,128)(2,1)S(1)} %collective-permute-done.3.refs_0_, bf16[1024,128]{1,0:T(8,128)(2,1)S(1)} %collective-permute-done.8.refs_1_, f32[2560,256]{1,0:T(8,128)S(1)} %get-tuple-element.79.refs_2_, ...), custom_call_target="tpu_custom_call" | custom-call | flops 3000000000 | bytes 1048576 | tf_op jit(solution)/shard_map/pallas_call | solution.py:353
  72.9 0.0 copy-start.2
  72.9 18.5 %all_to_all.28 = bf16[8,128,512]{2,1,0:T(8,128)(2,1)S(1)} all-to-all(bf16[8,128,512]{2,1,0:T(8,128)(2,1)S(1)} %bitcast.19), channel_id=1, replica_groups=mesh['y'=4,'p'=2,'w'=2,'c'=2,'row'=4] {'y','w'}, dimensions={0} | all-to-all | bytes 2097152 | tf_op jit(solution)/shard_map/all_to_all | solution.py:484
  91.4 2.0 %shard_map.75 = bf16[512,640]{1,0:T(8,128)(2,1)S(1)} custom-call(s32[2]{0:T(128)S(1)} %copy-done.12, bf16[1024,512]{1,0:T(8,128)(2,1)S(1)} %bitcast.20, f32[256,2048]{1,0:T(8,128)S(1)} %copy-done.2, f32[256,512]{1,0:T(8,128)S(1)} %copy-done.5, f32[256,128]{1,0:T(8,128)S(1)} %get-tuple-element.94.inverse, bf16[256,512]{1,0:T(8,128)(2,1)S(1)} %bitcast.23, ...), custom_call_target="tpu_custom_call" | custom-call | flops 1000000000 | bytes 1048576 | tf_op jit(solution)/shard_map/pallas_call | solution.py:353
  93.5 0.2 reshape.22
  93.6 21.5 %all_to_all.29 = bf16[128,4,640]{2,1,0:T(4,128)(2,1)S(1)} all-to-all(bf16[128,4,640]{2,1,0:T(4,128)(2,1)S(1)} %reshape.22), channel_id=1, replica_groups=mesh['y'=4,'p'=2,'w'=2,'c'=2,'row'=4] {'c','y','p','w','row'}, dimensions={0} | all-to-all | bytes 1310720 | tf_op jit(solution)/shard_map/all_to_all | solution.py:492
  115.1 0.1 reshape.23.got
  115.3 1.7 %shard_map.76 = f32[1024,512]{1,0:T(8,128)} custom-call(bf16[512,640]{1,0:T(8,128)(2,1)S(1)} %reshape.23.got), custom_call_target="tpu_custom_call" | custom-call | tf_op jit(solution)/shard_map/pallas_call | solution.py:495
  (25 shorter events, 0.1 us)
Async XLA Ops:
  0.0 9.9 %copy-start = (bf16[512,2048]{1,0:T(8,128)(2,1)S(1)}, bf16[512,2048]{1,0:T(8,128)(2,1)}, u32[]{:S(2)}) copy-start(bf16[512,2048]{1,0:T(8,128)(2,1)} %w_inner.3) | copy-start | bytes 6291460
  0.0 9.9 %copy-start.3 = (bf16[2,128,512]{2,1,0:T(8,128)(2,1)S(1)}, bf16[2,128,512]{2,1,0:T(8,128)(2,1)}, u32[]{:S(2)}) copy-start(bf16[2,128,512]{2,1,0:T(8,128)(2,1)} %param.7) | copy-start | bytes 786436
  0.0 9.9 %copy-start.13 = (s32[2,128]{1,0:T(2,128)S(1)}, s32[2,128]{1,0:T(2,128)}, u32[]{:S(2)}) copy-start(s32[2,128]{1,0:T(2,128)} %param.11) | copy-start | bytes 3076
  3.9 20.5 %all-to-all-start = ((bf16[8,128,512]{2,1,0:T(8,128)(2,1)}), bf16[8,128,512]{2,1,0:T(8,128)(2,1)S(1)}, u32[]{:S(2)}, u32[]{:S(2)}) async-start(bf16[8,128,512]{2,1,0:T(8,128)(2,1)} %bitcast.27), calls=%async_computation | async-start | bytes 2097152 | tf_op jit(solution)/shard_map/all_to_all | solution.py:389
  9.9 1.0 copy-start.6
  10.9 0.9 copy-start.9
  13.5 1.3 %copy-start.1 = (f32[256,2048]{1,0:T(8,128)}, f32[256,2048]{1,0:T(8,128)S(1)}, u32[]{:S(2)}) copy-start(f32[256,2048]{1,0:T(8,128)S(1)} %get-tuple-element.92.slope) | copy-start | bytes 6291460
  14.8 0.8 copy-start.4
  15.6 0.7 copy-start.7
  16.3 0.6 copy-start.10
  24.4 8.8 %copy-start.12 = (s32[2]{0:T(128)S(1)}, s32[2]{0:T(128)}, u32[]{:S(2)}) copy-start(s32[2]{0:T(128)} %lengths.15) | copy-start | bytes 28
  24.4 8.7 %collective-permute-start.1 = (bf16[1024,256]{1,0:T(8,128)(2,1)S(1)}, bf16[1024,256]{1,0:T(8,128)(2,1)S(1)}, u32[]{:S(2)}, u32[]{:S(2)}) collective-permute-start(bf16[1024,256]{1,0:T(8,128)(2,1)S(1)} %slice.6), channel_id=1, source_target_pairs={{0,4},{4,0},{1,5},{5,1},{2,6},{6,2},{3,7},{7,3},{8,12},{12,8},{9,1... | collective-permute-start | bytes 1572872 | tf_op jit(solution)/shard_map/ppermute | solution.py:407
  26.6 15.0 %collective-permute-start = (bf16[1024,256]{1,0:T(8,128)(2,1)S(1)}, bf16[1024,256]{1,0:T(8,128)(2,1)S(1)}, u32[]{:S(2)}, u32[]{:S(2)}) collective-permute-start(bf16[1024,256]{1,0:T(8,128)(2,1)S(1)} %slice.6), channel_id=1, source_target_pairs={{0,16},{16,0},{1,17},{17,1},{2,18},{18,2},{3,19},{19,3},{4,20},{20... | collective-permute-start | bytes 1572872 | tf_op jit(solution)/shard_map/ppermute | solution.py:406
  29.1 1.6 %collective-permute-start.2 = (bf16[1024,128]{1,0:T(8,128)(2,1)S(1)}, bf16[1024,128]{1,0:T(8,128)(2,1)S(1)}, u32[]{:S(2)}, u32[]{:S(2)}) collective-permute-start(bf16[1024,128]{1,0:T(8,128)(2,1)S(1)} %slice.7.refs_0_), channel_id=1, source_target_pairs={{0,4},{4,0},{1,5},{5,1},{2,6},{6,2},{3,7},{7,3},{8,12},{12,8},{9,1... | collective-permute-start | bytes 786440 | tf_op jit(solution)/shard_map/ppermute | solution.py:408
  41.6 5.2 %collective-permute-start.4 = (bf16[1024,256]{1,0:T(8,128)(2,1)S(1)}, bf16[1024,256]{1,0:T(8,128)(2,1)S(1)}, u32[]{:S(2)}, u32[]{:S(2)}) collective-permute-start(bf16[1024,256]{1,0:T(8,128)(2,1)S(1)} %collective-permute-done.refs_0_.refs_2_), channel_id=1, source_target_pairs={{0,4},{4,0},{1,5},{5,1},{2,6},{6,2},{3,7},{7,3},{8,12},{12,8},{9,1... | collective-permute-start | bytes 1572872 | tf_op jit(solution)/shard_map/ppermute | solution.py:430
  42.5 9.4 %collective-permute-start.3 = (bf16[1024,128]{1,0:T(8,128)(2,1)S(1)}, bf16[1024,128]{1,0:T(8,128)(2,1)S(1)}, u32[]{:S(2)}, u32[]{:S(2)}) collective-permute-start(bf16[1024,128]{1,0:T(8,128)(2,1)S(1)} %slice.7.refs_0_), channel_id=1, source_target_pairs={{0,16},{16,0},{1,17},{17,1},{2,18},{18,2},{3,19},{19,3},{4,20},{20... | collective-permute-start | bytes 786440 | tf_op jit(solution)/shard_map/ppermute | solution.py:431
  49.1 3.7 %collective-permute-start.7 = (f32[8,1024]{1,0:T(8,128)S(1)}, f32[8,1024]{1,0:T(8,128)S(1)}, u32[]{:S(2)}, u32[]{:S(2)}) collective-permute-start(f32[8,1024]{1,0:T(8,128)S(1)} %get-tuple-element.62.s0), channel_id=1, source_target_pairs={{0,40},{8,32},{32,8},{40,0},{64,104},{72,96},{96,72},{104,64},{1,4... | collective-permute-start | bytes 98312 | tf_op jit(solution)/shard_map/ppermute | solution.py:435
  49.1 3.7 %collective-permute-start.6 = (f32[8,1024]{1,0:T(8,128)S(1)}, f32[8,1024]{1,0:T(8,128)S(1)}, u32[]{:S(2)}, u32[]{:S(2)}) collective-permute-start(f32[8,1024]{1,0:T(8,128)S(1)} %get-tuple-element.62.s0), channel_id=1, source_target_pairs={{0,32},{8,40},{32,0},{40,8},{64,96},{72,104},{96,64},{104,72},{1,3... | collective-permute-start | bytes 98312 | tf_op jit(solution)/shard_map/ppermute | solution.py:435
  50.3 3.1 %collective-permute-start.5 = (f32[8,1024]{1,0:T(8,128)S(1)}, f32[8,1024]{1,0:T(8,128)S(1)}, u32[]{:S(2)}, u32[]{:S(2)}) collective-permute-start(f32[8,1024]{1,0:T(8,128)S(1)} %get-tuple-element.62.s0), channel_id=1, source_target_pairs={{0,8},{8,0},{32,40},{40,32},{64,72},{72,64},{96,104},{104,96},{1,9... | collective-permute-start | bytes 98312 | tf_op jit(solution)/shard_map/ppermute | solution.py:435
  54.8 12.0 %collective-permute-start.11 = (bf16[1024,128]{1,0:T(8,128)(2,1)S(1)}, bf16[1024,128]{1,0:T(8,128)(2,1)S(1)}, u32[]{:S(2)}, u32[]{:S(2)}) collective-permute-start(bf16[1024,128]{1,0:T(8,128)(2,1)S(1)} %get-tuple-element.69.grad_attn.refs_6_), channel_id=1, source_target_pairs={{0,4},{4,0},{16,20},{20,16},{1,5},{5,1},{17,21},{21,17},{2,6},{6,2... | collective-permute-start | bytes 786440 | tf_op jit(solution)/shard_map/ppermute | solution.py:446
  56.5 9.4 %collective-permute-start.9 = (bf16[1024,128]{1,0:T(8,128)(2,1)S(1)}, bf16[1024,128]{1,0:T(8,128)(2,1)S(1)}, u32[]{:S(2)}, u32[]{:S(2)}) collective-permute-start(bf16[1024,128]{1,0:T(8,128)(2,1)S(1)} %get-tuple-element.69.grad_attn.refs_6_), channel_id=1, source_target_pairs={{0,16},{4,20},{16,0},{20,4},{1,17},{5,21},{17,1},{21,5},{2,18},{6,... | collective-permute-start | bytes 786440 | tf_op jit(solution)/shard_map/ppermute | solution.py:446
  58.3 3.9 %collective-permute-start.8 = (bf16[1024,128]{1,0:T(8,128)(2,1)S(1)}, bf16[1024,128]{1,0:T(8,128)(2,1)S(1)}, u32[]{:S(2)}, u32[]{:S(2)}) collective-permute-start(bf16[1024,128]{1,0:T(8,128)(2,1)S(1)} %collective-permute-done.3.refs_0_), channel_id=1, source_target_pairs={{0,4},{4,0},{1,5},{5,1},{2,6},{6,2},{3,7},{7,3},{8,12},{12,8},{9,1... | collective-permute-start | bytes 786440 | tf_op jit(solution)/shard_map/ppermute | solution.py:438
  65.9 3.9 %collective-permute-start.10 = (bf16[1024,128]{1,0:T(8,128)(2,1)S(1)}, bf16[1024,128]{1,0:T(8,128)(2,1)S(1)}, u32[]{:S(2)}, u32[]{:S(2)}) collective-permute-start(bf16[1024,128]{1,0:T(8,128)(2,1)S(1)} %collective-permute-done.9.refs_6_), channel_id=1, source_target_pairs={{0,4},{4,0},{1,5},{5,1},{2,6},{6,2},{3,7},{7,3},{8,12},{12,8},{9,1... | collective-permute-start | bytes 786440 | tf_op jit(solution)/shard_map/ppermute | solution.py:458
  69.8 21.6 %copy-start.5 = (f32[256,512]{1,0:T(8,128)S(1)}, f32[256,512]{1,0:T(8,128)}, u32[]{:S(2)}) copy-start(f32[256,512]{1,0:T(8,128)} %copy-done.4) | copy-start | bytes 1572868
  69.8 21.6 %copy-start.8 = (bf16[512,256]{1,0:T(8,128)(2,1)S(1)}, bf16[512,256]{1,0:T(8,128)(2,1)}, u32[]{:S(2)}) copy-start(bf16[512,256]{1,0:T(8,128)(2,1)} %copy-done.7) | copy-start | bytes 786436
  69.8 21.6 %copy-start.11 = (bf16[256,128]{1,0:T(8,128)(2,1)S(1)}, bf16[256,128]{1,0:T(8,128)(2,1)}, u32[]{:S(2)}) copy-start(bf16[256,128]{1,0:T(8,128)(2,1)} %copy-done.10) | copy-start | bytes 196612
  72.9 18.6 %copy-start.2 = (f32[256,2048]{1,0:T(8,128)S(1)}, f32[256,2048]{1,0:T(8,128)}, u32[]{:S(2)}) copy-start(f32[256,2048]{1,0:T(8,128)} %copy-done.1) | copy-start | bytes 6291460

commit v7 on v6

--- a/solution.py
+++ b/solution.py
@@ -442,9 +442,7 @@
         (valid_lengths, attn_out, own, stats, *others),
         flops=10**7,
     )
-    grad_p, grad_c = [
-        lax.ppermute(grad_attn, ("p", "c"), [(i, i ^ m) for i in range(4)]) for m in (2, 1)
-    ]
+    grad_p = lax.ppermute(grad_attn, "p", swap)
     own_late, grad_attn = lax.optimization_barrier((own, grad_attn))
     scores_two = key_scores((2, 3), own_late, (q_p, q_pc))
     (grad_q,) = call(
@@ -454,6 +452,8 @@
         scratch=[rows_f32],
         flops=4 * 10**9,
     )
+    grad_late, grad_q = lax.optimization_barrier((grad_attn, grad_q))
+    grad_c = lax.ppermute(grad_late, "c", swap)
     grad_p, grad_q, scores_two = lax.optimization_barrier((grad_p, grad_q, scores_two))
     grad_pc = lax.ppermute(grad_p, "c", swap)
     grad_k, grad_v = call(

time: 117 us -> 117 us (level)
  waiting for transfers between devices: 17.1 us -> 15.8 us
    ppermute x2, starting transfers between devices: 3.49 us -> 1.87 us  [the longest x1 1.78 us: local(): grad_p = lax.ppermute(grad_attn, 'p', swap)]
    ppermute x1, starting transfers between devices: 0.36 us -> 1.98 us  [local(): q_pc = lax.ppermute(q_p, 'c', swap)]
    ppermute x2, waiting for transfers between devices: 1.33 us -> 0.01 us  [the longest x1 0.01 us: local(): grad_p = lax.ppermute(grad_attn, 'p', swap)]
  transfers between devices with their start and end apart: 13 -> 13, of which waited for: 7 -> 6; matrix products, arithmetic and copies ran while one was open for 0% -> 0% of each run, Pallas kernels for 17% -> 17%
where the time goes in v7:
time: 117 us; the launch traced here: 116 us
  blocking collectives  40.6 us (35%)
  Pallas kernels  31.9 us (27%)
  starting transfers between devices  21.7 us (19%)
  waiting for transfers between devices  15.8 us (14%)
  local copies, waits for them, and re-layouts  5.83 us (5%)
    pallas_call x11, Pallas kernels, call(): pl.pallas_call(kernel, out_shape=[jax.ShapeDtypeStruct(shape, dtype) for...  26.4 us
    all_to_all x1, blocking collectives, local(): lax.all_to_all(rows.reshape(128, CAP, D + EXT), ('c', 'y', 'p', 'w', 'row...  22.3 us
    all_to_all x1, blocking collectives, local(): got = lax.all_to_all(ret, ('y', 'w'), 0, 0, tiled=True)  18.3 us
    all_to_all x1, waiting for transfers between devices, local(): own = lax.all_to_all(send, ('y', 'w'), 0, 0, tiled=True)  7.4 us
    all_to_all x1, starting transfers between devices, local(): own = lax.all_to_all(send, ('y', 'w'), 0, 0, tiled=True)  5.96 us
    ppermute x1, waiting for transfers between devices, local(): vk_p = lax.ppermute(vk, 'p', swap)  5.61 us
    unnamed x28, local copies, waits for them, and re-layouts  5.45 us
    pallas_call x1, Pallas kernels, project(): pl.pallas_call(project_kernel, out_shape=jax.ShapeDtypeStruct((8 * BLK, 4...  3.88 us
  transfers between devices with their start and end apart: 13, of which 6 were waited for; matrix products, arithmetic and copies ran while one was open for 0% of the time, Pallas kernels for 17%

profile of v7, /device:TPU:1, one launch (start us, length us, event | category | flops | bytes accessed | tf_op | source)
XLA Modules:
  0.0 116.3 jit_solution(9943880724812344294)
XLA Ops:
  0.0 3.9 %shard_map.64 = bf16[1024,512]{1,0:T(8,128)(2,1)} custom-call(bf16[256,512]{1,0:T(8,128)(2,1)} %bitcast.24, bf16[256,512]{1,0:T(8,128)(2,1)} %bitcast.21, bf16[512,2048]{1,0:T(8,128)(2,1)} %w_inner.3, bf16[512,512]{1,0:T(8,128)(2,1)} %w_outer.1), custom_call_target="tpu_custom_call" | custom-call | tf_op jit(solution)/shard_map/pallas_call | solution.py:366
  3.9 6.0 %all-to-all-start = ((bf16[8,128,512]{2,1,0:T(8,128)(2,1)}), bf16[8,128,512]{2,1,0:T(8,128)(2,1)S(1)}, u32[]{:S(2)}, u32[]{:S(2)}) async-start(bf16[8,128,512]{2,1,0:T(8,128)(2,1)} %bitcast.27), calls=%async_computation | async-start | bytes 2097152 | tf_op jit(solution)/shard_map/all_to_all | solution.py:389
  9.9 0.0 copy-start.6
  9.9 1.0 copy-done.6
  10.9 0.9 copy-done.9
  11.9 1.6 %shard_map.65 = (f32[256,2048]{1,0:T(8,128)S(1)}, f32[256,512]{1,0:T(8,128)S(1)}, f32[256,128]{1,0:T(8,128)S(1)}, bf16[512,256]{1,0:T(8,128)(2,1)S(1)}, bf16[256,128]{1,0:T(8,128)(2,1)S(1)}) custom-call(bf16[256,512]{1,0:T(8,128)(2,1)S(1)} %bitcast.25, bf16[256,512]{1,0:T(8,128)(2,1)S(1)} %bitcast.22, bf16[512,2048]{1,0:T(8,128)(2,1)S(1)} %copy-done, ...), custom_call_target="tpu_custom_call" | custom-call | flops 2000000000 | bytes 1048576 | tf_op jit(solution)/shard_map/pallas_call | solution.py:353
  13.5 0.0 copy-start.1
  13.5 1.3 %copy-done.1 = f32[256,2048]{1,0:T(8,128)} copy-done((f32[256,2048]{1,0:T(8,128)}, f32[256,2048]{1,0:T(8,128)S(1)}, u32[]{:S(2)}) %copy-start.1) | copy-done | bytes 2097176
  14.8 0.8 copy-done.4
  15.6 0.7 copy-done.7
  16.3 0.6 copy-done.10
  16.9 7.4 %all-to-all-done = bf16[8,128,512]{2,1,0:T(8,128)(2,1)S(1)} async-done(((bf16[8,128,512]{2,1,0:T(8,128)(2,1)}), bf16[8,128,512]{2,1,0:T(8,128)(2,1)S(1)}, u32[]{:S(2)}, u32[]{:S(2)}) %all-to-all-start) | async-done | bytes 1048608 | tf_op jit(solution)/shard_map/all_to_all | solution.py:389
  24.4 2.2 %collective-permute-start.1 = (bf16[1024,256]{1,0:T(8,128)(2,1)S(1)}, bf16[1024,256]{1,0:T(8,128)(2,1)S(1)}, u32[]{:S(2)}, u32[]{:S(2)}) collective-permute-start(bf16[1024,256]{1,0:T(8,128)(2,1)S(1)} %slice.6), channel_id=1, source_target_pairs={{0,4},{4,0},{1,5},{5,1},{2,6},{6,2},{3,7},{7,3},{8,12},{12,8},{9,1... | collective-permute-start | bytes 1572872 | tf_op jit(solution)/shard_map/ppermute | solution.py:407
  26.6 2.5 %collective-permute-start = (bf16[1024,256]{1,0:T(8,128)(2,1)S(1)}, bf16[1024,256]{1,0:T(8,128)(2,1)S(1)}, u32[]{:S(2)}, u32[]{:S(2)}) collective-permute-start(bf16[1024,256]{1,0:T(8,128)(2,1)S(1)} %slice.6), channel_id=1, source_target_pairs={{0,16},{16,0},{1,17},{17,1},{2,18},{18,2},{3,19},{19,3},{4,20},{20... | collective-permute-start | bytes 1572872 | tf_op jit(solution)/shard_map/ppermute | solution.py:406
  29.1 0.4 collective-permute-start.2
  29.6 1.2 %collective-permute-done.2.refs_1_ = bf16[1024,128]{1,0:T(8,128)(2,1)S(1)} collective-permute-done((bf16[1024,128]{1,0:T(8,128)(2,1)S(1)}, bf16[1024,128]{1,0:T(8,128)(2,1)S(1)}, u32[]{:S(2)}, u32[]{:S(2)}) %collective-permute-start.2) | collective-permute-done | bytes 262176 | tf_op jit(solution)/shard_map/ppermute | solution.py:408
  30.8 2.4 %shard_map.67 = (f32[2560,256]{1,0:T(8,128)S(1)}, bf16[2560,256]{1,0:T(8,128)(2,1)S(1)}, f32[2560,256]{1,0:T(8,128)S(1)}, bf16[2560,256]{1,0:T(8,128)(2,1)S(1)}) custom-call(bf16[1024,512]{1,0:T(8,128)(2,1)S(1)} %bitcast.9, bf16[1024,128]{1,0:T(8,128)(2,1)S(1)} %slice.7.refs_0_, bf16[1024,128]{1,0:T(8,128)(2,1)S(1)} %collective-permute-done.2.refs_1_), custom_call_target="tpu_custom_call" | custom-call | flops 1000000000 | bytes 1048576 | tf_op jit(solution)/shard_map/pallas_call | solution.py:353
  33.1 0.0 collective-permute-done.1.refs_1_
  33.1 2.9 %shard_map.66 = (f32[1024,128]{1,0:T(8,128)S(1)}, f32[2560,256]{1,0:T(8,128)S(1)}, f32[2560,256]{1,0:T(8,128)S(1)}) custom-call(s32[2]{0:T(128)S(1)} %copy-done.12, bf16[1024,512]{1,0:T(8,128)(2,1)S(1)} %bitcast.10, bf16[1024,512]{1,0:T(8,128)(2,1)S(1)} %bitcast.11, bf16[1024,256]{1,0:T(8,128)(2,1)S(1)} %collective-permute-done.1.refs_1_), custom_call_target="tpu_custom_call" | custom-call | flops 1000000000 | bytes 1048576 | tf_op jit(solution)/shard_map/pallas_call | solution.py:353
  36.0 5.6 %collective-permute-done.refs_0_.refs_2_ = bf16[1024,256]{1,0:T(8,128)(2,1)S(1)} collective-permute-done((bf16[1024,256]{1,0:T(8,128)(2,1)S(1)}, bf16[1024,256]{1,0:T(8,128)(2,1)S(1)}, u32[]{:S(2)}, u32[]{:S(2)}) %collective-permute-start) | collective-permute-done | bytes 524320 | tf_op jit(solution)/shard_map/ppermute | solution.py:406
  41.6 0.9 collective-permute-start.4
  42.5 2.5 %collective-permute-start.3 = (bf16[1024,128]{1,0:T(8,128)(2,1)S(1)}, bf16[1024,128]{1,0:T(8,128)(2,1)S(1)}, u32[]{:S(2)}, u32[]{:S(2)}) collective-permute-start(bf16[1024,128]{1,0:T(8,128)(2,1)S(1)} %slice.7.refs_0_), channel_id=1, source_target_pairs={{0,16},{16,0},{1,17},{17,1},{2,18},{18,2},{3,19},{19,3},{4,20},{20... | collective-permute-start | bytes 786440 | tf_op jit(solution)/shard_map/ppermute | solution.py:431
  44.9 1.8 %shard_map.68 = (f32[1024,128]{1,0:T(8,128)S(1)}, f32[2560,256]{1,0:T(8,128)S(1)}) custom-call(s32[2]{0:T(128)S(1)} %copy-done.12, bf16[1024,512]{1,0:T(8,128)(2,1)S(1)} %bitcast.12, bf16[1024,256]{1,0:T(8,128)(2,1)S(1)} %collective-permute-done.refs_0_.refs_2_, f32[1024,128]{1,0:T(8,128)S(1)} %get-tuple-element.62.refs_1_), custom_call_target="tpu_custom_call" | custom-call | flops 500000000 | bytes 1048576 | tf_op jit(solution)/shard_map/pallas_call | solution.py:353
  46.8 0.0 collective-permute-done.4.refs_0_.refs_3_
  46.8 2.3 %shard_map.69 = (f32[1024,128]{1,0:T(8,128)S(1)}, f32[2560,256]{1,0:T(8,128)S(1)}, f32[8,1024]{1,0:T(8,128)S(1)}) custom-call(s32[2]{0:T(128)S(1)} %copy-done.12, bf16[1024,512]{1,0:T(8,128)(2,1)S(1)} %bitcast.13, bf16[1024,256]{1,0:T(8,128)(2,1)S(1)} %collective-permute-done.4.refs_0_.refs_3_, f32[1024,128]{1,0:T(8,128)S(1)} %get-tuple-element.63.refs_1_), custom_call_target="tpu_custom_call" | custom-call | flops 500000000 | bytes 1048576 | tf_op jit(solution)/shard_map/pallas_call | solution.py:353
  49.1 1.2 collective-permute-start.6
  50.3 1.5 %collective-permute-start.5 = (f32[8,1024]{1,0:T(8,128)S(1)}, f32[8,1024]{1,0:T(8,128)S(1)}, u32[]{:S(2)}, u32[]{:S(2)}) collective-permute-start(f32[8,1024]{1,0:T(8,128)S(1)} %get-tuple-element.64.s0), channel_id=1, source_target_pairs={{0,8},{8,0},{32,40},{40,32},{64,72},{72,64},{96,104},{104,96},{1,9... | collective-permute-start | bytes 98312 | tf_op jit(solution)/shard_map/ppermute | solution.py:435
  51.8 0.2 collective-permute-done.3.refs_0_
  51.9 0.9 collective-permute-done.7.s3
  52.8 0.0 collective-permute-done.6.s2
  52.8 0.6 collective-permute-done.5.s1
  53.4 1.4 %shard_map.70 = (bf16[1024,128]{1,0:T(8,128)(2,1)S(1)}, bf16[1024,128]{1,0:T(8,128)(2,1)S(1)}) custom-call(s32[2]{0:T(128)S(1)} %copy-done.12, f32[1024,128]{1,0:T(8,128)S(1)} %get-tuple-element.66.attn_out, bf16[1024,512]{1,0:T(8,128)(2,1)S(1)} %bitcast.14, f32[8,1024]{1,0:T(8,128)S(1)} %get-tuple-element.64.s0, f32[8,1024]{1,0:T(8,128)S(1)} %collective-permute-done.5.s1, ...), custom_call_target="tpu_custom_call" | custom-call | flops 10000000 | bytes 1048576 | tf_op jit(solution)/shard_map/pallas_call | solution.py:353
  54.8 1.8 %collective-permute-start.9 = (bf16[1024,128]{1,0:T(8,128)(2,1)S(1)}, bf16[1024,128]{1,0:T(8,128)(2,1)S(1)}, u32[]{:S(2)}, u32[]{:S(2)}) collective-permute-start(bf16[1024,128]{1,0:T(8,128)(2,1)S(1)} %get-tuple-element.91.grad_attn.refs_6_), channel_id=1, source_target_pairs={{0,16},{16,0},{1,17},{17,1},{2,18},{18,2},{3,19},{19,3},{4,20},{20... | collective-permute-start | bytes 786440 | tf_op jit(solution)/shard_map/ppermute | solution.py:445
  56.6 2.0 %collective-permute-start.8 = (bf16[1024,128]{1,0:T(8,128)(2,1)S(1)}, bf16[1024,128]{1,0:T(8,128)(2,1)S(1)}, u32[]{:S(2)}, u32[]{:S(2)}) collective-permute-start(bf16[1024,128]{1,0:T(8,128)(2,1)S(1)} %collective-permute-done.3.refs_0_), channel_id=1, source_target_pairs={{0,4},{4,0},{1,5},{5,1},{2,6},{6,2},{3,7},{7,3},{8,12},{12,8},{9,1... | collective-permute-start | bytes 786440 | tf_op jit(solution)/shard_map/ppermute | solution.py:438
  58.5 3.6 %shard_map.71.refs_11_ = bf16[1024,128]{1,0:T(8,128)(2,1)S(1)} custom-call(s32[2]{0:T(128)S(1)} %copy-done.12, bf16[1024,128]{1,0:T(8,128)(2,1)S(1)} %get-tuple-element.91.grad_attn.refs_6_, bf16[1024,512]{1,0:T(8,128)(2,1)S(1)} %bitcast.15, bf16[1024,256]{1,0:T(8,128)(2,1)S(1)} %collective-permute-done.1.refs_1_, ...), custom_call_target="tpu_custom_call" | custom-call | flops 4000000000 | bytes 1048576 | tf_op jit(solution)/shard_map/pallas_call | solution.py:353
  62.1 0.1 collective-permute-start.11
  62.2 0.0 collective-permute-done.8.refs_1_
  62.2 2.4 %shard_map.72 = (f32[2560,256]{1,0:T(8,128)S(1)}, bf16[2560,256]{1,0:T(8,128)(2,1)S(1)}, f32[2560,256]{1,0:T(8,128)S(1)}, bf16[2560,256]{1,0:T(8,128)(2,1)S(1)}) custom-call(bf16[1024,512]{1,0:T(8,128)(2,1)S(1)} %bitcast.16, bf16[1024,128]{1,0:T(8,128)(2,1)S(1)} %collective-permute-done.3.refs_0_, bf16[1024,128]{1,0:T(8,128)(2,1)S(1)} %collective-permute-done.8.refs_1_), custom_call_target="tpu_custom_call" | custom-call | flops 1000000000 | bytes 1048576 | tf_op jit(solution)/shard_map/pallas_call | solution.py:353
  64.6 0.8 collective-permute-start.10
  65.4 3.0 %shard_map.73 = (f32[1024,128]{1,0:T(8,128)S(1)}, f32[1024,128]{1,0:T(8,128)S(1)}) custom-call(s32[2]{0:T(128)S(1)} %copy-done.12, bf16[1024,512]{1,0:T(8,128)(2,1)S(1)} %bitcast.17, bf16[1024,128]{1,0:T(8,128)(2,1)S(1)} %slice.7.refs_0_, bf16[1024,128]{1,0:T(8,128)(2,1)S(1)} %collective-permute-done.2.refs_1_, f32[2560,256]{1,0:T(8,128)S(1)} %get-tuple-element.87.refs_2_, ...), custom_call_target="tpu_custom_call" | custom-call | flops 3000000000 | bytes 1048576 | tf_op jit(solution)/shard_map/pallas_call | solution.py:353
  68.4 3.0 %shard_map.74 = bf16[1024,512]{1,0:T(8,128)(2,1)S(1)} custom-call(s32[2]{0:T(128)S(1)} %copy-done.12, bf16[1024,512]{1,0:T(8,128)(2,1)S(1)} %bitcast.18, bf16[1024,128]{1,0:T(8,128)(2,1)S(1)} %collective-permute-done.3.refs_0_, bf16[1024,128]{1,0:T(8,128)(2,1)S(1)} %collective-permute-done.8.refs_1_, f32[2560,256]{1,0:T(8,128)S(1)} %get-tuple-element.82.refs_2_, ...), custom_call_target="tpu_custom_call" | custom-call | flops 3000000000 | bytes 1048576 | tf_op jit(solution)/shard_map/pallas_call | solution.py:353
  71.5 0.0 copy-start.2
  71.5 18.3 %all_to_all.28 = bf16[8,128,512]{2,1,0:T(8,128)(2,1)S(1)} all-to-all(bf16[8,128,512]{2,1,0:T(8,128)(2,1)S(1)} %bitcast.19), channel_id=1, replica_groups=mesh['y'=4,'p'=2,'w'=2,'c'=2,'row'=4] {'y','w'}, dimensions={0} | all-to-all | bytes 2097152 | tf_op jit(solution)/shard_map/all_to_all | solution.py:484
  89.8 2.0 %shard_map.75 = bf16[512,640]{1,0:T(8,128)(2,1)S(1)} custom-call(s32[2]{0:T(128)S(1)} %copy-done.12, bf16[1024,512]{1,0:T(8,128)(2,1)S(1)} %bitcast.20, f32[256,2048]{1,0:T(8,128)S(1)} %copy-done.2, f32[256,512]{1,0:T(8,128)S(1)} %copy-done.5, f32[256,128]{1,0:T(8,128)S(1)} %get-tuple-element.98.inverse, bf16[256,512]{1,0:T(8,128)(2,1)S(1)} %bitcast.23, ...), custom_call_target="tpu_custom_call" | custom-call | flops 1000000000 | bytes 1048576 | tf_op jit(solution)/shard_map/pallas_call | solution.py:353
  91.8 0.2 reshape.22
  91.9 22.3 %all_to_all.29 = bf16[128,4,640]{2,1,0:T(4,128)(2,1)S(1)} all-to-all(bf16[128,4,640]{2,1,0:T(4,128)(2,1)S(1)} %reshape.22), channel_id=1, replica_groups=mesh['y'=4,'p'=2,'w'=2,'c'=2,'row'=4] {'c','y','p','w','row'}, dimensions={0} | all-to-all | bytes 1310720 | tf_op jit(solution)/shard_map/all_to_all | solution.py:492
  114.3 0.1 reshape.23.got
  114.4 1.7 %shard_map.76 = f32[1024,512]{1,0:T(8,128)} custom-call(bf16[512,640]{1,0:T(8,128)(2,1)S(1)} %reshape.23.got), custom_call_target="tpu_custom_call" | custom-call | tf_op jit(solution)/shard_map/pallas_call | solution.py:495
  (25 shorter events, 0.1 us)
Async XLA Ops:
  0.0 9.9 %copy-start = (bf16[512,2048]{1,0:T(8,128)(2,1)S(1)}, bf16[512,2048]{1,0:T(8,128)(2,1)}, u32[]{:S(2)}) copy-start(bf16[512,2048]{1,0:T(8,128)(2,1)} %w_inner.3) | copy-start | bytes 6291460
  0.0 9.9 %copy-start.3 = (bf16[2,128,512]{2,1,0:T(8,128)(2,1)S(1)}, bf16[2,128,512]{2,1,0:T(8,128)(2,1)}, u32[]{:S(2)}) copy-start(bf16[2,128,512]{2,1,0:T(8,128)(2,1)} %param.7) | copy-start | bytes 786436
  0.0 9.9 %copy-start.13 = (s32[2,128]{1,0:T(2,128)S(1)}, s32[2,128]{1,0:T(2,128)}, u32[]{:S(2)}) copy-start(s32[2,128]{1,0:T(2,128)} %param.11) | copy-start | bytes 3076
  3.9 20.5 %all-to-all-start = ((bf16[8,128,512]{2,1,0:T(8,128)(2,1)}), bf16[8,128,512]{2,1,0:T(8,128)(2,1)S(1)}, u32[]{:S(2)}, u32[]{:S(2)}) async-start(bf16[8,128,512]{2,1,0:T(8,128)(2,1)} %bitcast.27), calls=%async_computation | async-start | bytes 2097152 | tf_op jit(solution)/shard_map/all_to_all | solution.py:389
  9.9 1.0 copy-start.6
  10.9 0.9 copy-start.9
  13.5 1.3 %copy-start.1 = (f32[256,2048]{1,0:T(8,128)}, f32[256,2048]{1,0:T(8,128)S(1)}, u32[]{:S(2)}) copy-start(f32[256,2048]{1,0:T(8,128)S(1)} %get-tuple-element.96.slope) | copy-start | bytes 6291460
  14.8 0.8 copy-start.4
  15.6 0.7 copy-start.7
  16.3 0.6 copy-start.10
  24.4 8.8 %copy-start.12 = (s32[2]{0:T(128)S(1)}, s32[2]{0:T(128)}, u32[]{:S(2)}) copy-start(s32[2]{0:T(128)} %lengths.15) | copy-start | bytes 28
  24.4 8.7 %collective-permute-start.1 = (bf16[1024,256]{1,0:T(8,128)(2,1)S(1)}, bf16[1024,256]{1,0:T(8,128)(2,1)S(1)}, u32[]{:S(2)}, u32[]{:S(2)}) collective-permute-start(bf16[1024,256]{1,0:T(8,128)(2,1)S(1)} %slice.6), channel_id=1, source_target_pairs={{0,4},{4,0},{1,5},{5,1},{2,6},{6,2},{3,7},{7,3},{8,12},{12,8},{9,1... | collective-permute-start | bytes 1572872 | tf_op jit(solution)/shard_map/ppermute | solution.py:407
  26.6 15.0 %collective-permute-start = (bf16[1024,256]{1,0:T(8,128)(2,1)S(1)}, bf16[1024,256]{1,0:T(8,128)(2,1)S(1)}, u32[]{:S(2)}, u32[]{:S(2)}) collective-permute-start(bf16[1024,256]{1,0:T(8,128)(2,1)S(1)} %slice.6), channel_id=1, source_target_pairs={{0,16},{16,0},{1,17},{17,1},{2,18},{18,2},{3,19},{19,3},{4,20},{20... | collective-permute-start | bytes 1572872 | tf_op jit(solution)/shard_map/ppermute | solution.py:406
  29.1 1.6 %collective-permute-start.2 = (bf16[1024,128]{1,0:T(8,128)(2,1)S(1)}, bf16[1024,128]{1,0:T(8,128)(2,1)S(1)}, u32[]{:S(2)}, u32[]{:S(2)}) collective-permute-start(bf16[1024,128]{1,0:T(8,128)(2,1)S(1)} %slice.7.refs_0_), channel_id=1, source_target_pairs={{0,4},{4,0},{1,5},{5,1},{2,6},{6,2},{3,7},{7,3},{8,12},{12,8},{9,1... | collective-permute-start | bytes 786440 | tf_op jit(solution)/shard_map/ppermute | solution.py:408
  41.6 5.2 %collective-permute-start.4 = (bf16[1024,256]{1,0:T(8,128)(2,1)S(1)}, bf16[1024,256]{1,0:T(8,128)(2,1)S(1)}, u32[]{:S(2)}, u32[]{:S(2)}) collective-permute-start(bf16[1024,256]{1,0:T(8,128)(2,1)S(1)} %collective-permute-done.refs_0_.refs_2_), channel_id=1, source_target_pairs={{0,4},{4,0},{1,5},{5,1},{2,6},{6,2},{3,7},{7,3},{8,12},{12,8},{9,1... | collective-permute-start | bytes 1572872 | tf_op jit(solution)/shard_map/ppermute | solution.py:430
  42.5 9.4 %collective-permute-start.3 = (bf16[1024,128]{1,0:T(8,128)(2,1)S(1)}, bf16[1024,128]{1,0:T(8,128)(2,1)S(1)}, u32[]{:S(2)}, u32[]{:S(2)}) collective-permute-start(bf16[1024,128]{1,0:T(8,128)(2,1)S(1)} %slice.7.refs_0_), channel_id=1, source_target_pairs={{0,16},{16,0},{1,17},{17,1},{2,18},{18,2},{3,19},{19,3},{4,20},{20... | collective-permute-start | bytes 786440 | tf_op jit(solution)/shard_map/ppermute | solution.py:431
  49.1 3.7 %collective-permute-start.7 = (f32[8,1024]{1,0:T(8,128)S(1)}, f32[8,1024]{1,0:T(8,128)S(1)}, u32[]{:S(2)}, u32[]{:S(2)}) collective-permute-start(f32[8,1024]{1,0:T(8,128)S(1)} %get-tuple-element.64.s0), channel_id=1, source_target_pairs={{0,40},{8,32},{32,8},{40,0},{64,104},{72,96},{96,72},{104,64},{1,4... | collective-permute-start | bytes 98312 | tf_op jit(solution)/shard_map/ppermute | solution.py:435
  49.1 3.7 %collective-permute-start.6 = (f32[8,1024]{1,0:T(8,128)S(1)}, f32[8,1024]{1,0:T(8,128)S(1)}, u32[]{:S(2)}, u32[]{:S(2)}) collective-permute-start(f32[8,1024]{1,0:T(8,128)S(1)} %get-tuple-element.64.s0), channel_id=1, source_target_pairs={{0,32},{8,40},{32,0},{40,8},{64,96},{72,104},{96,64},{104,72},{1,3... | collective-permute-start | bytes 98312 | tf_op jit(solution)/shard_map/ppermute | solution.py:435
  50.3 3.1 %collective-permute-start.5 = (f32[8,1024]{1,0:T(8,128)S(1)}, f32[8,1024]{1,0:T(8,128)S(1)}, u32[]{:S(2)}, u32[]{:S(2)}) collective-permute-start(f32[8,1024]{1,0:T(8,128)S(1)} %get-tuple-element.64.s0), channel_id=1, source_target_pairs={{0,8},{8,0},{32,40},{40,32},{64,72},{72,64},{96,104},{104,96},{1,9... | collective-permute-start | bytes 98312 | tf_op jit(solution)/shard_map/ppermute | solution.py:435
  54.8 9.8 %collective-permute-start.9 = (bf16[1024,128]{1,0:T(8,128)(2,1)S(1)}, bf16[1024,128]{1,0:T(8,128)(2,1)S(1)}, u32[]{:S(2)}, u32[]{:S(2)}) collective-permute-start(bf16[1024,128]{1,0:T(8,128)(2,1)S(1)} %get-tuple-element.91.grad_attn.refs_6_), channel_id=1, source_target_pairs={{0,16},{16,0},{1,17},{17,1},{2,18},{18,2},{3,19},{19,3},{4,20},{20... | collective-permute-start | bytes 786440 | tf_op jit(solution)/shard_map/ppermute | solution.py:445
  56.6 5.6 %collective-permute-start.8 = (bf16[1024,128]{1,0:T(8,128)(2,1)S(1)}, bf16[1024,128]{1,0:T(8,128)(2,1)S(1)}, u32[]{:S(2)}, u32[]{:S(2)}) collective-permute-start(bf16[1024,128]{1,0:T(8,128)(2,1)S(1)} %collective-permute-done.3.refs_0_), channel_id=1, source_target_pairs={{0,4},{4,0},{1,5},{5,1},{2,6},{6,2},{3,7},{7,3},{8,12},{12,8},{9,1... | collective-permute-start | bytes 786440 | tf_op jit(solution)/shard_map/ppermute | solution.py:438
  62.1 3.3 %collective-permute-start.11 = (bf16[1024,128]{1,0:T(8,128)(2,1)S(1)}, bf16[1024,128]{1,0:T(8,128)(2,1)S(1)}, u32[]{:S(2)}, u32[]{:S(2)}) collective-permute-start(bf16[1024,128]{1,0:T(8,128)(2,1)S(1)} %get-tuple-element.91.grad_attn.refs_6_), channel_id=1, source_target_pairs={{0,4},{4,0},{1,5},{5,1},{2,6},{6,2},{3,7},{7,3},{8,12},{12,8},{9,1... | collective-permute-start | bytes 786440 | tf_op jit(solution)/shard_map/ppermute | solution.py:456
  64.6 3.8 %collective-permute-start.10 = (bf16[1024,128]{1,0:T(8,128)(2,1)S(1)}, bf16[1024,128]{1,0:T(8,128)(2,1)S(1)}, u32[]{:S(2)}, u32[]{:S(2)}) collective-permute-start(bf16[1024,128]{1,0:T(8,128)(2,1)S(1)} %collective-permute-done.9.refs_6_), channel_id=1, source_target_pairs={{0,4},{4,0},{1,5},{5,1},{2,6},{6,2},{3,7},{7,3},{8,12},{12,8},{9,1... | collective-permute-start | bytes 786440 | tf_op jit(solution)/shard_map/ppermute | solution.py:458
  68.4 21.4 %copy-start.5 = (f32[256,512]{1,0:T(8,128)S(1)}, f32[256,512]{1,0:T(8,128)}, u32[]{:S(2)}) copy-start(f32[256,512]{1,0:T(8,128)} %copy-done.4) | copy-start | bytes 1572868
  68.4 21.4 %copy-start.8 = (bf16[512,256]{1,0:T(8,128)(2,1)S(1)}, bf16[512,256]{1,0:T(8,128)(2,1)}, u32[]{:S(2)}) copy-start(bf16[512,256]{1,0:T(8,128)(2,1)} %copy-done.7) | copy-start | bytes 786436
  68.4 21.3 %copy-start.11 = (bf16[256,128]{1,0:T(8,128)(2,1)S(1)}, bf16[256,128]{1,0:T(8,128)(2,1)}, u32[]{:S(2)}) copy-start(bf16[256,128]{1,0:T(8,128)(2,1)} %copy-done.10) | copy-start | bytes 196612
  71.5 18.3 %copy-start.2 = (f32[256,2048]{1,0:T(8,128)S(1)}, f32[256,2048]{1,0:T(8,128)}, u32[]{:S(2)}) copy-start(f32[256,2048]{1,0:T(8,128)} %copy-done.1) | copy-start | bytes 6291460

commit v8 on v7

--- a/solution.py
+++ b/solution.py
@@ -101,8 +101,7 @@
     )
     same = jnp.where((owner_col == owner_row) & earlier, 1, 0)
     rank = jnp.sum(same, axis=0, keepdims=True)
-    dest = (owner_row // 4 % 2) * 64 + owner_row // 8 * 4 + owner_row % 4
-    slot = dest * CAP + rank
+    slot = owner_row * CAP + rank
     slots = hot.shape[0]
     hot[...] = jnp.where(
         lax.broadcasted_iota(jnp.int32, (slots, count), 0) == slot, 1.0, 0.0
@@ -490,7 +489,7 @@
         flops=10**9,
     )
     got = lax.all_to_all(
-        rows.reshape(128, CAP, D + EXT), ("c", "y", "p", "w", "row"), 0, 0, tiled=True
+        rows.reshape(128, CAP, D + EXT), ("y", "p", "w", "c", "row"), 0, 0, tiled=True
     ).reshape(128 * CAP, D + EXT)
     return pl.pallas_call(
         table_kernel,

time: 117 us -> 118 us (level)
  no operation moved by 1% of the time
where the time goes in v8:
time: 118 us; the launch traced here: 117 us
  blocking collectives  41.7 us (35%)
  Pallas kernels  31.9 us (27%)
  starting transfers between devices  21.7 us (18%)
  waiting for transfers between devices  15.8 us (13%)
  local copies, waits for them, and re-layouts  5.83 us (5%)
    pallas_call x11, Pallas kernels, call(): pl.pallas_call(kernel, out_shape=[jax.ShapeDtypeStruct(shape, dtype) for...  26.3 us
    all_to_all x1, blocking collectives, local(): lax.all_to_all(rows.reshape(128, CAP, D + EXT), ('y', 'p', 'w', 'c', 'row...  23.4 us
    all_to_all x1, blocking collectives, local(): got = lax.all_to_all(ret, ('y', 'w'), 0, 0, tiled=True)  18.3 us
    all_to_all x1, waiting for transfers between devices, local(): own = lax.all_to_all(send, ('y', 'w'), 0, 0, tiled=True)  7.41 us
    all_to_all x1, starting transfers between devices, local(): own = lax.all_to_all(send, ('y', 'w'), 0, 0, tiled=True)  5.96 us
    ppermute x1, waiting for transfers between devices, local(): vk_p = lax.ppermute(vk, 'p', swap)  5.61 us
    unnamed x28, local copies, waits for them, and re-layouts  5.45 us
    pallas_call x1, Pallas kernels, project(): pl.pallas_call(project_kernel, out_shape=jax.ShapeDtypeStruct((8 * BLK, 4...  3.88 us
  transfers between devices with their start and end apart: 13, of which 6 were waited for; matrix products, arithmetic and copies ran while one was open for 0% of the time, Pallas kernels for 17%

profile of v8, /device:TPU:1, one launch (start us, length us, event | category | flops | bytes accessed | tf_op | source)
XLA Modules:
  0.0 117.4 jit_solution(14854368593597871949)
XLA Ops:
  0.0 3.9 %shard_map.64 = bf16[1024,512]{1,0:T(8,128)(2,1)} custom-call(bf16[256,512]{1,0:T(8,128)(2,1)} %bitcast.24, bf16[256,512]{1,0:T(8,128)(2,1)} %bitcast.21, bf16[512,2048]{1,0:T(8,128)(2,1)} %w_inner.3, bf16[512,512]{1,0:T(8,128)(2,1)} %w_outer.1), custom_call_target="tpu_custom_call" | custom-call | tf_op jit(solution)/shard_map/pallas_call | solution.py:365
  3.9 6.0 %all-to-all-start = ((bf16[8,128,512]{2,1,0:T(8,128)(2,1)}), bf16[8,128,512]{2,1,0:T(8,128)(2,1)S(1)}, u32[]{:S(2)}, u32[]{:S(2)}) async-start(bf16[8,128,512]{2,1,0:T(8,128)(2,1)} %bitcast.27), calls=%async_computation | async-start | bytes 2097152 | tf_op jit(solution)/shard_map/all_to_all | solution.py:388
  9.9 0.0 copy-start.6
  9.9 1.0 copy-done.6
  10.9 0.9 copy-done.9
  11.9 1.6 %shard_map.65 = (f32[256,2048]{1,0:T(8,128)S(1)}, f32[256,512]{1,0:T(8,128)S(1)}, f32[256,128]{1,0:T(8,128)S(1)}, bf16[512,256]{1,0:T(8,128)(2,1)S(1)}, bf16[256,128]{1,0:T(8,128)(2,1)S(1)}) custom-call(bf16[256,512]{1,0:T(8,128)(2,1)S(1)} %bitcast.25, bf16[256,512]{1,0:T(8,128)(2,1)S(1)} %bitcast.22, bf16[512,2048]{1,0:T(8,128)(2,1)S(1)} %copy-done, ...), custom_call_target="tpu_custom_call" | custom-call | flops 2000000000 | bytes 1048576 | tf_op jit(solution)/shard_map/pallas_call | solution.py:352
  13.5 0.0 copy-start.1
  13.5 1.3 %copy-done.1 = f32[256,2048]{1,0:T(8,128)} copy-done((f32[256,2048]{1,0:T(8,128)}, f32[256,2048]{1,0:T(8,128)S(1)}, u32[]{:S(2)}) %copy-start.1) | copy-done | bytes 2097176
  14.8 0.8 copy-done.4
  15.6 0.7 copy-done.7
  16.3 0.6 copy-done.10
  16.9 7.4 %all-to-all-done = bf16[8,128,512]{2,1,0:T(8,128)(2,1)S(1)} async-done(((bf16[8,128,512]{2,1,0:T(8,128)(2,1)}), bf16[8,128,512]{2,1,0:T(8,128)(2,1)S(1)}, u32[]{:S(2)}, u32[]{:S(2)}) %all-to-all-start) | async-done | bytes 1048608 | tf_op jit(solution)/shard_map/all_to_all | solution.py:388
  24.4 2.2 %collective-permute-start.1 = (bf16[1024,256]{1,0:T(8,128)(2,1)S(1)}, bf16[1024,256]{1,0:T(8,128)(2,1)S(1)}, u32[]{:S(2)}, u32[]{:S(2)}) collective-permute-start(bf16[1024,256]{1,0:T(8,128)(2,1)S(1)} %slice.6), channel_id=1, source_target_pairs={{0,4},{4,0},{1,5},{5,1},{2,6},{6,2},{3,7},{7,3},{8,12},{12,8},{9,1... | collective-permute-start | bytes 1572872 | tf_op jit(solution)/shard_map/ppermute | solution.py:406
  26.6 2.5 %collective-permute-start = (bf16[1024,256]{1,0:T(8,128)(2,1)S(1)}, bf16[1024,256]{1,0:T(8,128)(2,1)S(1)}, u32[]{:S(2)}, u32[]{:S(2)}) collective-permute-start(bf16[1024,256]{1,0:T(8,128)(2,1)S(1)} %slice.6), channel_id=1, source_target_pairs={{0,16},{16,0},{1,17},{17,1},{2,18},{18,2},{3,19},{19,3},{4,20},{20... | collective-permute-start | bytes 1572872 | tf_op jit(solution)/shard_map/ppermute | solution.py:405
  29.1 0.4 collective-permute-start.2
  29.6 1.2 %collective-permute-done.2.refs_1_ = bf16[1024,128]{1,0:T(8,128)(2,1)S(1)} collective-permute-done((bf16[1024,128]{1,0:T(8,128)(2,1)S(1)}, bf16[1024,128]{1,0:T(8,128)(2,1)S(1)}, u32[]{:S(2)}, u32[]{:S(2)}) %collective-permute-start.2) | collective-permute-done | bytes 262176 | tf_op jit(solution)/shard_map/ppermute | solution.py:407
  30.8 2.4 %shard_map.67 = (f32[2560,256]{1,0:T(8,128)S(1)}, bf16[2560,256]{1,0:T(8,128)(2,1)S(1)}, f32[2560,256]{1,0:T(8,128)S(1)}, bf16[2560,256]{1,0:T(8,128)(2,1)S(1)}) custom-call(bf16[1024,512]{1,0:T(8,128)(2,1)S(1)} %bitcast.9, bf16[1024,128]{1,0:T(8,128)(2,1)S(1)} %slice.7.refs_0_, bf16[1024,128]{1,0:T(8,128)(2,1)S(1)} %collective-permute-done.2.refs_1_), custom_call_target="tpu_custom_call" | custom-call | flops 1000000000 | bytes 1048576 | tf_op jit(solution)/shard_map/pallas_call | solution.py:352
  33.1 2.9 %shard_map.66 = (f32[1024,128]{1,0:T(8,128)S(1)}, f32[2560,256]{1,0:T(8,128)S(1)}, f32[2560,256]{1,0:T(8,128)S(1)}) custom-call(s32[2]{0:T(128)S(1)} %copy-done.12, bf16[1024,512]{1,0:T(8,128)(2,1)S(1)} %bitcast.10, bf16[1024,512]{1,0:T(8,128)(2,1)S(1)} %bitcast.11, bf16[1024,256]{1,0:T(8,128)(2,1)S(1)} %collective-permute-done.1.refs_1_), custom_call_target="tpu_custom_call" | custom-call | flops 1000000000 | bytes 1048576 | tf_op jit(solution)/shard_map/pallas_call | solution.py:352
  36.0 5.6 %collective-permute-done.refs_0_.refs_2_ = bf16[1024,256]{1,0:T(8,128)(2,1)S(1)} collective-permute-done((bf16[1024,256]{1,0:T(8,128)(2,1)S(1)}, bf16[1024,256]{1,0:T(8,128)(2,1)S(1)}, u32[]{:S(2)}, u32[]{:S(2)}) %collective-permute-start) | collective-permute-done | bytes 524320 | tf_op jit(solution)/shard_map/ppermute | solution.py:405
  41.6 0.9 collective-permute-start.4
  42.5 2.5 %collective-permute-start.3 = (bf16[1024,128]{1,0:T(8,128)(2,1)S(1)}, bf16[1024,128]{1,0:T(8,128)(2,1)S(1)}, u32[]{:S(2)}, u32[]{:S(2)}) collective-permute-start(bf16[1024,128]{1,0:T(8,128)(2,1)S(1)} %slice.7.refs_0_), channel_id=1, source_target_pairs={{0,16},{16,0},{1,17},{17,1},{2,18},{18,2},{3,19},{19,3},{4,20},{20... | collective-permute-start | bytes 786440 | tf_op jit(solution)/shard_map/ppermute | solution.py:430
  44.9 1.8 %shard_map.68 = (f32[1024,128]{1,0:T(8,128)S(1)}, f32[2560,256]{1,0:T(8,128)S(1)}) custom-call(s32[2]{0:T(128)S(1)} %copy-done.12, bf16[1024,512]{1,0:T(8,128)(2,1)S(1)} %bitcast.12, bf16[1024,256]{1,0:T(8,128)(2,1)S(1)} %collective-permute-done.refs_0_.refs_2_, f32[1024,128]{1,0:T(8,128)S(1)} %get-tuple-element.62.refs_1_), custom_call_target="tpu_custom_call" | custom-call | flops 500000000 | bytes 1048576 | tf_op jit(solution)/shard_map/pallas_call | solution.py:352
  46.8 0.0 collective-permute-done.4.refs_0_.refs_3_
  46.8 2.3 %shard_map.69 = (f32[1024,128]{1,0:T(8,128)S(1)}, f32[2560,256]{1,0:T(8,128)S(1)}, f32[8,1024]{1,0:T(8,128)S(1)}) custom-call(s32[2]{0:T(128)S(1)} %copy-done.12, bf16[1024,512]{1,0:T(8,128)(2,1)S(1)} %bitcast.13, bf16[1024,256]{1,0:T(8,128)(2,1)S(1)} %collective-permute-done.4.refs_0_.refs_3_, f32[1024,128]{1,0:T(8,128)S(1)} %get-tuple-element.63.refs_1_), custom_call_target="tpu_custom_call" | custom-call | flops 500000000 | bytes 1048576 | tf_op jit(solution)/shard_map/pallas_call | solution.py:352
  49.1 0.0 collective-permute-start.7
  49.1 1.2 collective-permute-start.6
  50.3 1.5 %collective-permute-start.5 = (f32[8,1024]{1,0:T(8,128)S(1)}, f32[8,1024]{1,0:T(8,128)S(1)}, u32[]{:S(2)}, u32[]{:S(2)}) collective-permute-start(f32[8,1024]{1,0:T(8,128)S(1)} %get-tuple-element.64.s0), channel_id=1, source_target_pairs={{0,8},{8,0},{32,40},{40,32},{64,72},{72,64},{96,104},{104,96},{1,9... | collective-permute-start | bytes 98312 | tf_op jit(solution)/shard_map/ppermute | solution.py:434
  51.8 0.2 collective-permute-done.3.refs_0_
  51.9 0.9 collective-permute-done.7.s3
  52.8 0.0 collective-permute-done.6.s2
  52.8 0.6 collective-permute-done.5.s1
  53.4 1.4 %shard_map.70 = (bf16[1024,128]{1,0:T(8,128)(2,1)S(1)}, bf16[1024,128]{1,0:T(8,128)(2,1)S(1)}) custom-call(s32[2]{0:T(128)S(1)} %copy-done.12, f32[1024,128]{1,0:T(8,128)S(1)} %get-tuple-element.66.attn_out, bf16[1024,512]{1,0:T(8,128)(2,1)S(1)} %bitcast.14, f32[8,1024]{1,0:T(8,128)S(1)} %get-tuple-element.64.s0, f32[8,1024]{1,0:T(8,128)S(1)} %collective-permute-done.5.s1, ...), custom_call_target="tpu_custom_call" | custom-call | flops 10000000 | bytes 1048576 | tf_op jit(solution)/shard_map/pallas_call | solution.py:352
  54.8 1.8 %collective-permute-start.9 = (bf16[1024,128]{1,0:T(8,128)(2,1)S(1)}, bf16[1024,128]{1,0:T(8,128)(2,1)S(1)}, u32[]{:S(2)}, u32[]{:S(2)}) collective-permute-start(bf16[1024,128]{1,0:T(8,128)(2,1)S(1)} %get-tuple-element.91.grad_attn.refs_6_), channel_id=1, source_target_pairs={{0,16},{16,0},{1,17},{17,1},{2,18},{18,2},{3,19},{19,3},{4,20},{20... | collective-permute-start | bytes 786440 | tf_op jit(solution)/shard_map/ppermute | solution.py:444
  56.6 2.0 %collective-permute-start.8 = (bf16[1024,128]{1,0:T(8,128)(2,1)S(1)}, bf16[1024,128]{1,0:T(8,128)(2,1)S(1)}, u32[]{:S(2)}, u32[]{:S(2)}) collective-permute-start(bf16[1024,128]{1,0:T(8,128)(2,1)S(1)} %collective-permute-done.3.refs_0_), channel_id=1, source_target_pairs={{0,4},{4,0},{1,5},{5,1},{2,6},{6,2},{3,7},{7,3},{8,12},{12,8},{9,1... | collective-permute-start | bytes 786440 | tf_op jit(solution)/shard_map/ppermute | solution.py:437
  58.5 3.6 %shard_map.71.refs_11_ = bf16[1024,128]{1,0:T(8,128)(2,1)S(1)} custom-call(s32[2]{0:T(128)S(1)} %copy-done.12, bf16[1024,128]{1,0:T(8,128)(2,1)S(1)} %get-tuple-element.91.grad_attn.refs_6_, bf16[1024,512]{1,0:T(8,128)(2,1)S(1)} %bitcast.15, bf16[1024,256]{1,0:T(8,128)(2,1)S(1)} %collective-permute-done.1.refs_1_, ...), custom_call_target="tpu_custom_call" | custom-call | flops 4000000000 | bytes 1048576 | tf_op jit(solution)/shard_map/pallas_call | solution.py:352
  62.1 0.1 collective-permute-start.11
  62.2 2.4 %shard_map.72 = (f32[2560,256]{1,0:T(8,128)S(1)}, bf16[2560,256]{1,0:T(8,128)(2,1)S(1)}, f32[2560,256]{1,0:T(8,128)S(1)}, bf16[2560,256]{1,0:T(8,128)(2,1)S(1)}) custom-call(bf16[1024,512]{1,0:T(8,128)(2,1)S(1)} %bitcast.16, bf16[1024,128]{1,0:T(8,128)(2,1)S(1)} %collective-permute-done.3.refs_0_, bf16[1024,128]{1,0:T(8,128)(2,1)S(1)} %collective-permute-done.8.refs_1_), custom_call_target="tpu_custom_call" | custom-call | flops 1000000000 | bytes 1048576 | tf_op jit(solution)/shard_map/pallas_call | solution.py:352
  64.6 0.0 collective-permute-done.9.refs_6_
  64.6 0.8 collective-permute-start.10
  65.4 3.0 %shard_map.73 = (f32[1024,128]{1,0:T(8,128)S(1)}, f32[1024,128]{1,0:T(8,128)S(1)}) custom-call(s32[2]{0:T(128)S(1)} %copy-done.12, bf16[1024,512]{1,0:T(8,128)(2,1)S(1)} %bitcast.17, bf16[1024,128]{1,0:T(8,128)(2,1)S(1)} %slice.7.refs_0_, bf16[1024,128]{1,0:T(8,128)(2,1)S(1)} %collective-permute-done.2.refs_1_, f32[2560,256]{1,0:T(8,128)S(1)} %get-tuple-element.87.refs_2_, ...), custom_call_target="tpu_custom_call" | custom-call | flops 3000000000 | bytes 1048576 | tf_op jit(solution)/shard_map/pallas_call | solution.py:352
  68.4 3.0 %shard_map.74 = bf16[1024,512]{1,0:T(8,128)(2,1)S(1)} custom-call(s32[2]{0:T(128)S(1)} %copy-done.12, bf16[1024,512]{1,0:T(8,128)(2,1)S(1)} %bitcast.18, bf16[1024,128]{1,0:T(8,128)(2,1)S(1)} %collective-permute-done.3.refs_0_, bf16[1024,128]{1,0:T(8,128)(2,1)S(1)} %collective-permute-done.8.refs_1_, f32[2560,256]{1,0:T(8,128)S(1)} %get-tuple-element.82.refs_2_, ...), custom_call_target="tpu_custom_call" | custom-call | flops 3000000000 | bytes 1048576 | tf_op jit(solution)/shard_map/pallas_call | solution.py:352
  71.5 0.0 copy-start.2
  71.5 18.3 %all_to_all.28 = bf16[8,128,512]{2,1,0:T(8,128)(2,1)S(1)} all-to-all(bf16[8,128,512]{2,1,0:T(8,128)(2,1)S(1)} %bitcast.19), channel_id=1, replica_groups=mesh['y'=4,'p'=2,'w'=2,'c'=2,'row'=4] {'y','w'}, dimensions={0} | all-to-all | bytes 2097152 | tf_op jit(solution)/shard_map/all_to_all | solution.py:483
  89.8 2.0 %shard_map.75 = bf16[512,640]{1,0:T(8,128)(2,1)S(1)} custom-call(s32[2]{0:T(128)S(1)} %copy-done.12, bf16[1024,512]{1,0:T(8,128)(2,1)S(1)} %bitcast.20, f32[256,2048]{1,0:T(8,128)S(1)} %copy-done.2, f32[256,512]{1,0:T(8,128)S(1)} %copy-done.5, f32[256,128]{1,0:T(8,128)S(1)} %get-tuple-element.98.inverse, bf16[256,512]{1,0:T(8,128)(2,1)S(1)} %bitcast.23, ...), custom_call_target="tpu_custom_call" | custom-call | flops 1000000000 | bytes 1048576 | tf_op jit(solution)/shard_map/pallas_call | solution.py:352
  91.8 0.2 reshape.22
  91.9 23.4 %all_to_all.29 = bf16[128,4,640]{2,1,0:T(4,128)(2,1)S(1)} all-to-all(bf16[128,4,640]{2,1,0:T(4,128)(2,1)S(1)} %reshape.22), channel_id=1, replica_groups=mesh['y'=4,'p'=2,'w'=2,'c'=2,'row'=4] {'y','p','w','c','row'}, dimensions={0} | all-to-all | bytes 1310720 | tf_op jit(solution)/shard_map/all_to_all | solution.py:491
  115.4 0.1 reshape.23.got
  115.5 1.7 %shard_map.76 = f32[1024,512]{1,0:T(8,128)} custom-call(bf16[512,640]{1,0:T(8,128)(2,1)S(1)} %reshape.23.got), custom_call_target="tpu_custom_call" | custom-call | tf_op jit(solution)/shard_map/pallas_call | solution.py:494
  (25 shorter events, 0.1 us)
Async XLA Ops:
  0.0 9.9 %copy-start = (bf16[512,2048]{1,0:T(8,128)(2,1)S(1)}, bf16[512,2048]{1,0:T(8,128)(2,1)}, u32[]{:S(2)}) copy-start(bf16[512,2048]{1,0:T(8,128)(2,1)} %w_inner.3) | copy-start | bytes 6291460
  0.0 9.9 %copy-start.3 = (bf16[2,128,512]{2,1,0:T(8,128)(2,1)S(1)}, bf16[2,128,512]{2,1,0:T(8,128)(2,1)}, u32[]{:S(2)}) copy-start(bf16[2,128,512]{2,1,0:T(8,128)(2,1)} %param.7) | copy-start | bytes 786436
  0.0 9.9 %copy-start.13 = (s32[2,128]{1,0:T(2,128)S(1)}, s32[2,128]{1,0:T(2,128)}, u32[]{:S(2)}) copy-start(s32[2,128]{1,0:T(2,128)} %param.11) | copy-start | bytes 3076
  3.9 20.5 %all-to-all-start = ((bf16[8,128,512]{2,1,0:T(8,128)(2,1)}), bf16[8,128,512]{2,1,0:T(8,128)(2,1)S(1)}, u32[]{:S(2)}, u32[]{:S(2)}) async-start(bf16[8,128,512]{2,1,0:T(8,128)(2,1)} %bitcast.27), calls=%async_computation | async-start | bytes 2097152 | tf_op jit(solution)/shard_map/all_to_all | solution.py:388
  9.9 1.0 copy-start.6
  10.9 0.9 copy-start.9
  13.5 1.3 %copy-start.1 = (f32[256,2048]{1,0:T(8,128)}, f32[256,2048]{1,0:T(8,128)S(1)}, u32[]{:S(2)}) copy-start(f32[256,2048]{1,0:T(8,128)S(1)} %get-tuple-element.96.slope) | copy-start | bytes 6291460
  14.8 0.8 copy-start.4
  15.6 0.7 copy-start.7
  16.3 0.6 copy-start.10
  24.4 8.8 %copy-start.12 = (s32[2]{0:T(128)S(1)}, s32[2]{0:T(128)}, u32[]{:S(2)}) copy-start(s32[2]{0:T(128)} %lengths.15) | copy-start | bytes 28
  24.4 8.7 %collective-permute-start.1 = (bf16[1024,256]{1,0:T(8,128)(2,1)S(1)}, bf16[1024,256]{1,0:T(8,128)(2,1)S(1)}, u32[]{:S(2)}, u32[]{:S(2)}) collective-permute-start(bf16[1024,256]{1,0:T(8,128)(2,1)S(1)} %slice.6), channel_id=1, source_target_pairs={{0,4},{4,0},{1,5},{5,1},{2,6},{6,2},{3,7},{7,3},{8,12},{12,8},{9,1... | collective-permute-start | bytes 1572872 | tf_op jit(solution)/shard_map/ppermute | solution.py:406
  26.6 15.0 %collective-permute-start = (bf16[1024,256]{1,0:T(8,128)(2,1)S(1)}, bf16[1024,256]{1,0:T(8,128)(2,1)S(1)}, u32[]{:S(2)}, u32[]{:S(2)}) collective-permute-start(bf16[1024,256]{1,0:T(8,128)(2,1)S(1)} %slice.6), channel_id=1, source_target_pairs={{0,16},{16,0},{1,17},{17,1},{2,18},{18,2},{3,19},{19,3},{4,20},{20... | collective-permute-start | bytes 1572872 | tf_op jit(solution)/shard_map/ppermute | solution.py:405
  29.1 1.6 %collective-permute-start.2 = (bf16[1024,128]{1,0:T(8,128)(2,1)S(1)}, bf16[1024,128]{1,0:T(8,128)(2,1)S(1)}, u32[]{:S(2)}, u32[]{:S(2)}) collective-permute-start(bf16[1024,128]{1,0:T(8,128)(2,1)S(1)} %slice.7.refs_0_), channel_id=1, source_target_pairs={{0,4},{4,0},{1,5},{5,1},{2,6},{6,2},{3,7},{7,3},{8,12},{12,8},{9,1... | collective-permute-start | bytes 786440 | tf_op jit(solution)/shard_map/ppermute | solution.py:407
  41.6 5.2 %collective-permute-start.4 = (bf16[1024,256]{1,0:T(8,128)(2,1)S(1)}, bf16[1024,256]{1,0:T(8,128)(2,1)S(1)}, u32[]{:S(2)}, u32[]{:S(2)}) collective-permute-start(bf16[1024,256]{1,0:T(8,128)(2,1)S(1)} %collective-permute-done.refs_0_.refs_2_), channel_id=1, source_target_pairs={{0,4},{4,0},{1,5},{5,1},{2,6},{6,2},{3,7},{7,3},{8,12},{12,8},{9,1... | collective-permute-start | bytes 1572872 | tf_op jit(solution)/shard_map/ppermute | solution.py:429
  42.5 9.4 %collective-permute-start.3 = (bf16[1024,128]{1,0:T(8,128)(2,1)S(1)}, bf16[1024,128]{1,0:T(8,128)(2,1)S(1)}, u32[]{:S(2)}, u32[]{:S(2)}) collective-permute-start(bf16[1024,128]{1,0:T(8,128)(2,1)S(1)} %slice.7.refs_0_), channel_id=1, source_target_pairs={{0,16},{16,0},{1,17},{17,1},{2,18},{18,2},{3,19},{19,3},{4,20},{20... | collective-permute-start | bytes 786440 | tf_op jit(solution)/shard_map/ppermute | solution.py:430
  49.1 3.7 %collective-permute-start.7 = (f32[8,1024]{1,0:T(8,128)S(1)}, f32[8,1024]{1,0:T(8,128)S(1)}, u32[]{:S(2)}, u32[]{:S(2)}) collective-permute-start(f32[8,1024]{1,0:T(8,128)S(1)} %get-tuple-element.64.s0), channel_id=1, source_target_pairs={{0,40},{8,32},{32,8},{40,0},{64,104},{72,96},{96,72},{104,64},{1,4... | collective-permute-start | bytes 98312 | tf_op jit(solution)/shard_map/ppermute | solution.py:434
  49.1 3.7 %collective-permute-start.6 = (f32[8,1024]{1,0:T(8,128)S(1)}, f32[8,1024]{1,0:T(8,128)S(1)}, u32[]{:S(2)}, u32[]{:S(2)}) collective-permute-start(f32[8,1024]{1,0:T(8,128)S(1)} %get-tuple-element.64.s0), channel_id=1, source_target_pairs={{0,32},{8,40},{32,0},{40,8},{64,96},{72,104},{96,64},{104,72},{1,3... | collective-permute-start | bytes 98312 | tf_op jit(solution)/shard_map/ppermute | solution.py:434
  50.3 3.1 %collective-permute-start.5 = (f32[8,1024]{1,0:T(8,128)S(1)}, f32[8,1024]{1,0:T(8,128)S(1)}, u32[]{:S(2)}, u32[]{:S(2)}) collective-permute-start(f32[8,1024]{1,0:T(8,128)S(1)} %get-tuple-element.64.s0), channel_id=1, source_target_pairs={{0,8},{8,0},{32,40},{40,32},{64,72},{72,64},{96,104},{104,96},{1,9... | collective-permute-start | bytes 98312 | tf_op jit(solution)/shard_map/ppermute | solution.py:434
  54.8 9.8 %collective-permute-start.9 = (bf16[1024,128]{1,0:T(8,128)(2,1)S(1)}, bf16[1024,128]{1,0:T(8,128)(2,1)S(1)}, u32[]{:S(2)}, u32[]{:S(2)}) collective-permute-start(bf16[1024,128]{1,0:T(8,128)(2,1)S(1)} %get-tuple-element.91.grad_attn.refs_6_), channel_id=1, source_target_pairs={{0,16},{16,0},{1,17},{17,1},{2,18},{18,2},{3,19},{19,3},{4,20},{20... | collective-permute-start | bytes 786440 | tf_op jit(solution)/shard_map/ppermute | solution.py:444
  56.6 5.6 %collective-permute-start.8 = (bf16[1024,128]{1,0:T(8,128)(2,1)S(1)}, bf16[1024,128]{1,0:T(8,128)(2,1)S(1)}, u32[]{:S(2)}, u32[]{:S(2)}) collective-permute-start(bf16[1024,128]{1,0:T(8,128)(2,1)S(1)} %collective-permute-done.3.refs_0_), channel_id=1, source_target_pairs={{0,4},{4,0},{1,5},{5,1},{2,6},{6,2},{3,7},{7,3},{8,12},{12,8},{9,1... | collective-permute-start | bytes 786440 | tf_op jit(solution)/shard_map/ppermute | solution.py:437
  62.1 3.3 %collective-permute-start.11 = (bf16[1024,128]{1,0:T(8,128)(2,1)S(1)}, bf16[1024,128]{1,0:T(8,128)(2,1)S(1)}, u32[]{:S(2)}, u32[]{:S(2)}) collective-permute-start(bf16[1024,128]{1,0:T(8,128)(2,1)S(1)} %get-tuple-element.91.grad_attn.refs_6_), channel_id=1, source_target_pairs={{0,4},{4,0},{1,5},{5,1},{2,6},{6,2},{3,7},{7,3},{8,12},{12,8},{9,1... | collective-permute-start | bytes 786440 | tf_op jit(solution)/shard_map/ppermute | solution.py:455
  64.6 3.8 %collective-permute-start.10 = (bf16[1024,128]{1,0:T(8,128)(2,1)S(1)}, bf16[1024,128]{1,0:T(8,128)(2,1)S(1)}, u32[]{:S(2)}, u32[]{:S(2)}) collective-permute-start(bf16[1024,128]{1,0:T(8,128)(2,1)S(1)} %collective-permute-done.9.refs_6_), channel_id=1, source_target_pairs={{0,4},{4,0},{1,5},{5,1},{2,6},{6,2},{3,7},{7,3},{8,12},{12,8},{9,1... | collective-permute-start | bytes 786440 | tf_op jit(solution)/shard_map/ppermute | solution.py:457
  68.4 21.4 %copy-start.5 = (f32[256,512]{1,0:T(8,128)S(1)}, f32[256,512]{1,0:T(8,128)}, u32[]{:S(2)}) copy-start(f32[256,512]{1,0:T(8,128)} %copy-done.4) | copy-start | bytes 1572868
  68.4 21.4 %copy-start.8 = (bf16[512,256]{1,0:T(8,128)(2,1)S(1)}, bf16[512,256]{1,0:T(8,128)(2,1)}, u32[]{:S(2)}) copy-start(bf16[512,256]{1,0:T(8,128)(2,1)} %copy-done.7) | copy-start | bytes 786436
  68.4 21.3 %copy-start.11 = (bf16[256,128]{1,0:T(8,128)(2,1)S(1)}, bf16[256,128]{1,0:T(8,128)(2,1)}, u32[]{:S(2)}) copy-start(bf16[256,128]{1,0:T(8,128)(2,1)} %copy-done.10) | copy-start | bytes 196612
  71.5 18.3 %copy-start.2 = (f32[256,2048]{1,0:T(8,128)S(1)}, f32[256,2048]{1,0:T(8,128)}, u32[]{:S(2)}) copy-start(f32[256,2048]{1,0:T(8,128)} %copy-done.1) | copy-start | bytes 6291460

commit v9 on v7

--- a/solution.py
+++ b/solution.py
@@ -426,10 +426,11 @@
 
     attn_out, slope_o, slope_c = forward((0, 1), (own, vk_c), ())
     scores_one = key_scores((0, 1), own, (q, q_c))
-    vk_p, attn_out, scores_one, q_late = lax.optimization_barrier((vk_p, attn_out, scores_one, q))
+    vk_p, attn_out, scores_one = lax.optimization_barrier((vk_p, attn_out, scores_one))
     vk_pc = lax.ppermute(vk_p, "c", swap)
+    attn_out, slope_p = forward((2,), (vk_p,), (attn_out,))
+    attn_out, q_late = lax.optimization_barrier((attn_out, q))
     q_p = lax.ppermute(q_late, "p", swap)
-    attn_out, slope_p = forward((2,), (vk_p,), (attn_out,))
     attn_out, slope_pc, stats = forward((3,), (vk_pc,), (attn_out,), [((8, 1024), F32)])
     others = [
         lax.ppermute(stats, ("y", "w"), [(i, i ^ m) for i in range(8)]) for m in (1, 2, 3)

time: 117 us -> 118 us (level)
  waiting for transfers between devices: 15.8 us -> 17.1 us
    ppermute x1, waiting for transfers between devices: 0.16 us -> 2.02 us  [local(): q_p = lax.ppermute(q_late, 'p', swap)]
where the time goes in v9:
time: 118 us; the launch traced here: 117 us
  blocking collectives  40.6 us (34%)
  Pallas kernels  31.9 us (27%)
  starting transfers between devices  21.7 us (18%)
  waiting for transfers between devices  17.1 us (14%)
  local copies, waits for them, and re-layouts  5.83 us (5%)
    pallas_call x11, Pallas kernels, call(): pl.pallas_call(kernel, out_shape=[jax.ShapeDtypeStruct(shape, dtype) for...  26.4 us
    all_to_all x1, blocking collectives, local(): lax.all_to_all(rows.reshape(128, CAP, D + EXT), ('c', 'y', 'p', 'w', 'row...  22 us
    all_to_all x1, blocking collectives, local(): got = lax.all_to_all(ret, ('y', 'w'), 0, 0, tiled=True)  18.5 us
    all_to_all x1, waiting for transfers between devices, local(): own = lax.all_to_all(send, ('y', 'w'), 0, 0, tiled=True)  7.4 us
    all_to_all x1, starting transfers between devices, local(): own = lax.all_to_all(send, ('y', 'w'), 0, 0, tiled=True)  5.96 us
    ppermute x1, waiting for transfers between devices, local(): vk_p = lax.ppermute(vk, 'p', swap)  5.61 us
    unnamed x28, local copies, waits for them, and re-layouts  5.45 us
    pallas_call x1, Pallas kernels, project(): pl.pallas_call(project_kernel, out_shape=jax.ShapeDtypeStruct((8 * BLK, 4...  3.88 us
  transfers between devices with their start and end apart: 13, of which 6 were waited for; matrix products, arithmetic and copies ran while one was open for 0% of the time, Pallas kernels for 17%

profile of v9, /device:TPU:1, one launch (start us, length us, event | category | flops | bytes accessed | tf_op | source)
XLA Modules:
  0.0 117.5 jit_solution(2408862315032783321)
XLA Ops:
  0.0 3.9 %shard_map.64 = bf16[1024,512]{1,0:T(8,128)(2,1)} custom-call(bf16[256,512]{1,0:T(8,128)(2,1)} %bitcast.24, bf16[256,512]{1,0:T(8,128)(2,1)} %bitcast.21, bf16[512,2048]{1,0:T(8,128)(2,1)} %w_inner.3, bf16[512,512]{1,0:T(8,128)(2,1)} %w_outer.1), custom_call_target="tpu_custom_call" | custom-call | tf_op jit(solution)/shard_map/pallas_call | solution.py:366
  3.9 6.0 %all-to-all-start = ((bf16[8,128,512]{2,1,0:T(8,128)(2,1)}), bf16[8,128,512]{2,1,0:T(8,128)(2,1)S(1)}, u32[]{:S(2)}, u32[]{:S(2)}) async-start(bf16[8,128,512]{2,1,0:T(8,128)(2,1)} %bitcast.27), calls=%async_computation | async-start | bytes 2097152 | tf_op jit(solution)/shard_map/all_to_all | solution.py:389
  9.9 0.0 copy-start.6
  9.9 1.0 copy-done.6
  10.9 0.9 copy-done.9
  11.9 1.6 %shard_map.65 = (f32[256,2048]{1,0:T(8,128)S(1)}, f32[256,512]{1,0:T(8,128)S(1)}, f32[256,128]{1,0:T(8,128)S(1)}, bf16[512,256]{1,0:T(8,128)(2,1)S(1)}, bf16[256,128]{1,0:T(8,128)(2,1)S(1)}) custom-call(bf16[256,512]{1,0:T(8,128)(2,1)S(1)} %bitcast.25, bf16[256,512]{1,0:T(8,128)(2,1)S(1)} %bitcast.22, bf16[512,2048]{1,0:T(8,128)(2,1)S(1)} %copy-done, ...), custom_call_target="tpu_custom_call" | custom-call | flops 2000000000 | bytes 1048576 | tf_op jit(solution)/shard_map/pallas_call | solution.py:353
  13.5 0.0 copy-start.1
  13.5 1.3 %copy-done.1 = f32[256,2048]{1,0:T(8,128)} copy-done((f32[256,2048]{1,0:T(8,128)}, f32[256,2048]{1,0:T(8,128)S(1)}, u32[]{:S(2)}) %copy-start.1) | copy-done | bytes 2097176
  14.8 0.8 copy-done.4
  15.6 0.7 copy-done.7
  16.3 0.6 copy-done.10
  16.9 7.4 %all-to-all-done = bf16[8,128,512]{2,1,0:T(8,128)(2,1)S(1)} async-done(((bf16[8,128,512]{2,1,0:T(8,128)(2,1)}), bf16[8,128,512]{2,1,0:T(8,128)(2,1)S(1)}, u32[]{:S(2)}, u32[]{:S(2)}) %all-to-all-start) | async-done | bytes 1048608 | tf_op jit(solution)/shard_map/all_to_all | solution.py:389
  24.4 2.2 %collective-permute-start.1 = (bf16[1024,256]{1,0:T(8,128)(2,1)S(1)}, bf16[1024,256]{1,0:T(8,128)(2,1)S(1)}, u32[]{:S(2)}, u32[]{:S(2)}) collective-permute-start(bf16[1024,256]{1,0:T(8,128)(2,1)S(1)} %slice.6), channel_id=1, source_target_pairs={{0,4},{4,0},{1,5},{5,1},{2,6},{6,2},{3,7},{7,3},{8,12},{12,8},{9,1... | collective-permute-start | bytes 1572872 | tf_op jit(solution)/shard_map/ppermute | solution.py:407
  26.6 2.5 %collective-permute-start = (bf16[1024,256]{1,0:T(8,128)(2,1)S(1)}, bf16[1024,256]{1,0:T(8,128)(2,1)S(1)}, u32[]{:S(2)}, u32[]{:S(2)}) collective-permute-start(bf16[1024,256]{1,0:T(8,128)(2,1)S(1)} %slice.6), channel_id=1, source_target_pairs={{0,16},{16,0},{1,17},{17,1},{2,18},{18,2},{3,19},{19,3},{4,20},{20... | collective-permute-start | bytes 1572872 | tf_op jit(solution)/shard_map/ppermute | solution.py:406
  29.1 0.4 collective-permute-start.2
  29.6 1.2 %collective-permute-done.2.refs_1_ = bf16[1024,128]{1,0:T(8,128)(2,1)S(1)} collective-permute-done((bf16[1024,128]{1,0:T(8,128)(2,1)S(1)}, bf16[1024,128]{1,0:T(8,128)(2,1)S(1)}, u32[]{:S(2)}, u32[]{:S(2)}) %collective-permute-start.2) | collective-permute-done | bytes 262176 | tf_op jit(solution)/shard_map/ppermute | solution.py:408
  30.8 2.4 %shard_map.67 = (f32[2560,256]{1,0:T(8,128)S(1)}, bf16[2560,256]{1,0:T(8,128)(2,1)S(1)}, f32[2560,256]{1,0:T(8,128)S(1)}, bf16[2560,256]{1,0:T(8,128)(2,1)S(1)}) custom-call(bf16[1024,512]{1,0:T(8,128)(2,1)S(1)} %bitcast.9, bf16[1024,128]{1,0:T(8,128)(2,1)S(1)} %slice.7.refs_0_, bf16[1024,128]{1,0:T(8,128)(2,1)S(1)} %collective-permute-done.2.refs_1_), custom_call_target="tpu_custom_call" | custom-call | flops 1000000000 | bytes 1048576 | tf_op jit(solution)/shard_map/pallas_call | solution.py:353
  33.1 2.9 %shard_map.66 = (f32[1024,128]{1,0:T(8,128)S(1)}, f32[2560,256]{1,0:T(8,128)S(1)}, f32[2560,256]{1,0:T(8,128)S(1)}) custom-call(s32[2]{0:T(128)S(1)} %copy-done.12, bf16[1024,512]{1,0:T(8,128)(2,1)S(1)} %bitcast.10, bf16[1024,512]{1,0:T(8,128)(2,1)S(1)} %bitcast.11, bf16[1024,256]{1,0:T(8,128)(2,1)S(1)} %collective-permute-done.1.refs_1_), custom_call_target="tpu_custom_call" | custom-call | flops 1000000000 | bytes 1048576 | tf_op jit(solution)/shard_map/pallas_call | solution.py:353
  36.0 5.6 %collective-permute-done.refs_0_.refs_2_ = bf16[1024,256]{1,0:T(8,128)(2,1)S(1)} collective-permute-done((bf16[1024,256]{1,0:T(8,128)(2,1)S(1)}, bf16[1024,256]{1,0:T(8,128)(2,1)S(1)}, u32[]{:S(2)}, u32[]{:S(2)}) %collective-permute-start) | collective-permute-done | bytes 524320 | tf_op jit(solution)/shard_map/ppermute | solution.py:406
  41.6 0.9 collective-permute-start.4
  42.5 1.8 %shard_map.68 = (f32[1024,128]{1,0:T(8,128)S(1)}, f32[2560,256]{1,0:T(8,128)S(1)}) custom-call(s32[2]{0:T(128)S(1)} %copy-done.12, bf16[1024,512]{1,0:T(8,128)(2,1)S(1)} %bitcast.12, bf16[1024,256]{1,0:T(8,128)(2,1)S(1)} %collective-permute-done.refs_0_.refs_2_, f32[1024,128]{1,0:T(8,128)S(1)} %get-tuple-element.62.refs_1_), custom_call_target="tpu_custom_call" | custom-call | flops 500000000 | bytes 1048576 | tf_op jit(solution)/shard_map/pallas_call | solution.py:353
  44.3 2.7 %collective-permute-start.3 = (bf16[1024,128]{1,0:T(8,128)(2,1)S(1)}, bf16[1024,128]{1,0:T(8,128)(2,1)S(1)}, u32[]{:S(2)}, u32[]{:S(2)}) collective-permute-start(bf16[1024,128]{1,0:T(8,128)(2,1)S(1)} %slice.7.refs_0_), channel_id=1, source_target_pairs={{0,16},{16,0},{1,17},{17,1},{2,18},{18,2},{3,19},{19,3},{4,20},{20... | collective-permute-start | bytes 786440 | tf_op jit(solution)/shard_map/ppermute | solution.py:433
  47.1 0.0 collective-permute-done.4.refs_0_.refs_3_
  47.1 2.3 %shard_map.69 = (f32[1024,128]{1,0:T(8,128)S(1)}, f32[2560,256]{1,0:T(8,128)S(1)}, f32[8,1024]{1,0:T(8,128)S(1)}) custom-call(s32[2]{0:T(128)S(1)} %copy-done.12, bf16[1024,512]{1,0:T(8,128)(2,1)S(1)} %bitcast.13, bf16[1024,256]{1,0:T(8,128)(2,1)S(1)} %collective-permute-done.4.refs_0_.refs_3_, f32[1024,128]{1,0:T(8,128)S(1)} %get-tuple-element.65.refs_1_), custom_call_target="tpu_custom_call" | custom-call | flops 500000000 | bytes 1048576 | tf_op jit(solution)/shard_map/pallas_call | solution.py:353
  49.4 0.0 collective-permute-start.7
  49.4 1.2 collective-permute-start.6
  50.5 1.5 %collective-permute-start.5 = (f32[8,1024]{1,0:T(8,128)S(1)}, f32[8,1024]{1,0:T(8,128)S(1)}, u32[]{:S(2)}, u32[]{:S(2)}) collective-permute-start(f32[8,1024]{1,0:T(8,128)S(1)} %get-tuple-element.66.s0), channel_id=1, source_target_pairs={{0,8},{8,0},{32,40},{40,32},{64,72},{72,64},{96,104},{104,96},{1,9... | collective-permute-start | bytes 98312 | tf_op jit(solution)/shard_map/ppermute | solution.py:436
  52.0 2.0 %collective-permute-done.3.refs_0_ = bf16[1024,128]{1,0:T(8,128)(2,1)S(1)} collective-permute-done((bf16[1024,128]{1,0:T(8,128)(2,1)S(1)}, bf16[1024,128]{1,0:T(8,128)(2,1)S(1)}, u32[]{:S(2)}, u32[]{:S(2)}) %collective-permute-start.3) | collective-permute-done | bytes 262176 | tf_op jit(solution)/shard_map/ppermute | solution.py:433
  54.0 0.2 collective-permute-done.7.s3
  54.2 0.0 collective-permute-done.6.s2
  54.2 0.7 collective-permute-done.5.s1
  54.9 1.4 %shard_map.70 = (bf16[1024,128]{1,0:T(8,128)(2,1)S(1)}, bf16[1024,128]{1,0:T(8,128)(2,1)S(1)}) custom-call(s32[2]{0:T(128)S(1)} %copy-done.12, f32[1024,128]{1,0:T(8,128)S(1)} %get-tuple-element.68.attn_out, bf16[1024,512]{1,0:T(8,128)(2,1)S(1)} %bitcast.14, f32[8,1024]{1,0:T(8,128)S(1)} %get-tuple-element.66.s0, f32[8,1024]{1,0:T(8,128)S(1)} %collective-permute-done.5.s1, ...), custom_call_target="tpu_custom_call" | custom-call | flops 10000000 | bytes 1048576 | tf_op jit(solution)/shard_map/pallas_call | solution.py:353
  56.3 1.8 %collective-permute-start.9 = (bf16[1024,128]{1,0:T(8,128)(2,1)S(1)}, bf16[1024,128]{1,0:T(8,128)(2,1)S(1)}, u32[]{:S(2)}, u32[]{:S(2)}) collective-permute-start(bf16[1024,128]{1,0:T(8,128)(2,1)S(1)} %get-tuple-element.93.grad_attn.refs_6_), channel_id=1, source_target_pairs={{0,16},{16,0},{1,17},{17,1},{2,18},{18,2},{3,19},{19,3},{4,20},{20... | collective-permute-start | bytes 786440 | tf_op jit(solution)/shard_map/ppermute | solution.py:446
  58.1 1.3 %collective-permute-start.8 = (bf16[1024,128]{1,0:T(8,128)(2,1)S(1)}, bf16[1024,128]{1,0:T(8,128)(2,1)S(1)}, u32[]{:S(2)}, u32[]{:S(2)}) collective-permute-start(bf16[1024,128]{1,0:T(8,128)(2,1)S(1)} %collective-permute-done.3.refs_0_), channel_id=1, source_target_pairs={{0,4},{4,0},{1,5},{5,1},{2,6},{6,2},{3,7},{7,3},{8,12},{12,8},{9,1... | collective-permute-start | bytes 786440 | tf_op jit(solution)/shard_map/ppermute | solution.py:439
  59.5 3.6 %shard_map.71.refs_11_ = bf16[1024,128]{1,0:T(8,128)(2,1)S(1)} custom-call(s32[2]{0:T(128)S(1)} %copy-done.12, bf16[1024,128]{1,0:T(8,128)(2,1)S(1)} %get-tuple-element.93.grad_attn.refs_6_, bf16[1024,512]{1,0:T(8,128)(2,1)S(1)} %bitcast.15, bf16[1024,256]{1,0:T(8,128)(2,1)S(1)} %collective-permute-done.1.refs_1_, ...), custom_call_target="tpu_custom_call" | custom-call | flops 4000000000 | bytes 1048576 | tf_op jit(solution)/shard_map/pallas_call | solution.py:353
  63.0 0.1 collective-permute-start.11
  63.1 2.4 %shard_map.72 = (f32[2560,256]{1,0:T(8,128)S(1)}, bf16[2560,256]{1,0:T(8,128)(2,1)S(1)}, f32[2560,256]{1,0:T(8,128)S(1)}, bf16[2560,256]{1,0:T(8,128)(2,1)S(1)}) custom-call(bf16[1024,512]{1,0:T(8,128)(2,1)S(1)} %bitcast.16, bf16[1024,128]{1,0:T(8,128)(2,1)S(1)} %collective-permute-done.3.refs_0_, bf16[1024,128]{1,0:T(8,128)(2,1)S(1)} %collective-permute-done.8.refs_1_), custom_call_target="tpu_custom_call" | custom-call | flops 1000000000 | bytes 1048576 | tf_op jit(solution)/shard_map/pallas_call | solution.py:353
  65.5 0.0 collective-permute-done.9.refs_6_
  65.5 1.1 collective-permute-start.10
  66.6 3.0 %shard_map.73 = (f32[1024,128]{1,0:T(8,128)S(1)}, f32[1024,128]{1,0:T(8,128)S(1)}) custom-call(s32[2]{0:T(128)S(1)} %copy-done.12, bf16[1024,512]{1,0:T(8,128)(2,1)S(1)} %bitcast.17, bf16[1024,128]{1,0:T(8,128)(2,1)S(1)} %slice.7.refs_0_, bf16[1024,128]{1,0:T(8,128)(2,1)S(1)} %collective-permute-done.2.refs_1_, f32[2560,256]{1,0:T(8,128)S(1)} %get-tuple-element.89.refs_2_, ...), custom_call_target="tpu_custom_call" | custom-call | flops 3000000000 | bytes 1048576 | tf_op jit(solution)/shard_map/pallas_call | solution.py:353
  69.7 3.0 %shard_map.74 = bf16[1024,512]{1,0:T(8,128)(2,1)S(1)} custom-call(s32[2]{0:T(128)S(1)} %copy-done.12, bf16[1024,512]{1,0:T(8,128)(2,1)S(1)} %bitcast.18, bf16[1024,128]{1,0:T(8,128)(2,1)S(1)} %collective-permute-done.3.refs_0_, bf16[1024,128]{1,0:T(8,128)(2,1)S(1)} %collective-permute-done.8.refs_1_, f32[2560,256]{1,0:T(8,128)S(1)} %get-tuple-element.84.refs_2_, ...), custom_call_target="tpu_custom_call" | custom-call | flops 3000000000 | bytes 1048576 | tf_op jit(solution)/shard_map/pallas_call | solution.py:353
  72.7 0.0 copy-start.2
  72.7 18.5 %all_to_all.28 = bf16[8,128,512]{2,1,0:T(8,128)(2,1)S(1)} all-to-all(bf16[8,128,512]{2,1,0:T(8,128)(2,1)S(1)} %bitcast.19), channel_id=1, replica_groups=mesh['y'=4,'p'=2,'w'=2,'c'=2,'row'=4] {'y','w'}, dimensions={0} | all-to-all | bytes 2097152 | tf_op jit(solution)/shard_map/all_to_all | solution.py:485
  91.3 2.0 %shard_map.75 = bf16[512,640]{1,0:T(8,128)(2,1)S(1)} custom-call(s32[2]{0:T(128)S(1)} %copy-done.12, bf16[1024,512]{1,0:T(8,128)(2,1)S(1)} %bitcast.20, f32[256,2048]{1,0:T(8,128)S(1)} %copy-done.2, f32[256,512]{1,0:T(8,128)S(1)} %copy-done.5, f32[256,128]{1,0:T(8,128)S(1)} %get-tuple-element.100.inverse, bf16[256,512]{1,0:T(8,128)(2,1)S(1)} %bitcast.23, ...), custom_call_target="tpu_custom_call" | custom-call | flops 1000000000 | bytes 1048576 | tf_op jit(solution)/shard_map/pallas_call | solution.py:353
  93.3 0.2 reshape.22
  93.5 22.0 %all_to_all.29 = bf16[128,4,640]{2,1,0:T(4,128)(2,1)S(1)} all-to-all(bf16[128,4,640]{2,1,0:T(4,128)(2,1)S(1)} %reshape.22), channel_id=1, replica_groups=mesh['y'=4,'p'=2,'w'=2,'c'=2,'row'=4] {'c','y','p','w','row'}, dimensions={0} | all-to-all | bytes 1310720 | tf_op jit(solution)/shard_map/all_to_all | solution.py:493
  115.5 0.1 reshape.23.got
  115.6 1.7 %shard_map.76 = f32[1024,512]{1,0:T(8,128)} custom-call(bf16[512,640]{1,0:T(8,128)(2,1)S(1)} %reshape.23.got), custom_call_target="tpu_custom_call" | custom-call | tf_op jit(solution)/shard_map/pallas_call | solution.py:496
  (25 shorter events, 0.1 us)
Async XLA Ops:
  0.0 9.9 %copy-start = (bf16[512,2048]{1,0:T(8,128)(2,1)S(1)}, bf16[512,2048]{1,0:T(8,128)(2,1)}, u32[]{:S(2)}) copy-start(bf16[512,2048]{1,0:T(8,128)(2,1)} %w_inner.3) | copy-start | bytes 6291460
  0.0 9.9 %copy-start.3 = (bf16[2,128,512]{2,1,0:T(8,128)(2,1)S(1)}, bf16[2,128,512]{2,1,0:T(8,128)(2,1)}, u32[]{:S(2)}) copy-start(bf16[2,128,512]{2,1,0:T(8,128)(2,1)} %param.7) | copy-start | bytes 786436
  0.0 9.9 %copy-start.13 = (s32[2,128]{1,0:T(2,128)S(1)}, s32[2,128]{1,0:T(2,128)}, u32[]{:S(2)}) copy-start(s32[2,128]{1,0:T(2,128)} %param.11) | copy-start | bytes 3076
  3.9 20.5 %all-to-all-start = ((bf16[8,128,512]{2,1,0:T(8,128)(2,1)}), bf16[8,128,512]{2,1,0:T(8,128)(2,1)S(1)}, u32[]{:S(2)}, u32[]{:S(2)}) async-start(bf16[8,128,512]{2,1,0:T(8,128)(2,1)} %bitcast.27), calls=%async_computation | async-start | bytes 2097152 | tf_op jit(solution)/shard_map/all_to_all | solution.py:389
  9.9 1.0 copy-start.6
  10.9 0.9 copy-start.9
  13.5 1.3 %copy-start.1 = (f32[256,2048]{1,0:T(8,128)}, f32[256,2048]{1,0:T(8,128)S(1)}, u32[]{:S(2)}) copy-start(f32[256,2048]{1,0:T(8,128)S(1)} %get-tuple-element.98.slope) | copy-start | bytes 6291460
  14.8 0.8 copy-start.4
  15.6 0.7 copy-start.7
  16.3 0.6 copy-start.10
  24.4 8.8 %copy-start.12 = (s32[2]{0:T(128)S(1)}, s32[2]{0:T(128)}, u32[]{:S(2)}) copy-start(s32[2]{0:T(128)} %lengths.15) | copy-start | bytes 28
  24.4 8.7 %collective-permute-start.1 = (bf16[1024,256]{1,0:T(8,128)(2,1)S(1)}, bf16[1024,256]{1,0:T(8,128)(2,1)S(1)}, u32[]{:S(2)}, u32[]{:S(2)}) collective-permute-start(bf16[1024,256]{1,0:T(8,128)(2,1)S(1)} %slice.6), channel_id=1, source_target_pairs={{0,4},{4,0},{1,5},{5,1},{2,6},{6,2},{3,7},{7,3},{8,12},{12,8},{9,1... | collective-permute-start | bytes 1572872 | tf_op jit(solution)/shard_map/ppermute | solution.py:407
  26.6 15.0 %collective-permute-start = (bf16[1024,256]{1,0:T(8,128)(2,1)S(1)}, bf16[1024,256]{1,0:T(8,128)(2,1)S(1)}, u32[]{:S(2)}, u32[]{:S(2)}) collective-permute-start(bf16[1024,256]{1,0:T(8,128)(2,1)S(1)} %slice.6), channel_id=1, source_target_pairs={{0,16},{16,0},{1,17},{17,1},{2,18},{18,2},{3,19},{19,3},{4,20},{20... | collective-permute-start | bytes 1572872 | tf_op jit(solution)/shard_map/ppermute | solution.py:406
  29.1 1.6 %collective-permute-start.2 = (bf16[1024,128]{1,0:T(8,128)(2,1)S(1)}, bf16[1024,128]{1,0:T(8,128)(2,1)S(1)}, u32[]{:S(2)}, u32[]{:S(2)}) collective-permute-start(bf16[1024,128]{1,0:T(8,128)(2,1)S(1)} %slice.7.refs_0_), channel_id=1, source_target_pairs={{0,4},{4,0},{1,5},{5,1},{2,6},{6,2},{3,7},{7,3},{8,12},{12,8},{9,1... | collective-permute-start | bytes 786440 | tf_op jit(solution)/shard_map/ppermute | solution.py:408
  41.6 5.4 %collective-permute-start.4 = (bf16[1024,256]{1,0:T(8,128)(2,1)S(1)}, bf16[1024,256]{1,0:T(8,128)(2,1)S(1)}, u32[]{:S(2)}, u32[]{:S(2)}) collective-permute-start(bf16[1024,256]{1,0:T(8,128)(2,1)S(1)} %collective-permute-done.refs_0_.refs_2_), channel_id=1, source_target_pairs={{0,4},{4,0},{1,5},{5,1},{2,6},{6,2},{3,7},{7,3},{8,12},{12,8},{9,1... | collective-permute-start | bytes 1572872 | tf_op jit(solution)/shard_map/ppermute | solution.py:430
  44.3 9.7 %collective-permute-start.3 = (bf16[1024,128]{1,0:T(8,128)(2,1)S(1)}, bf16[1024,128]{1,0:T(8,128)(2,1)S(1)}, u32[]{:S(2)}, u32[]{:S(2)}) collective-permute-start(bf16[1024,128]{1,0:T(8,128)(2,1)S(1)} %slice.7.refs_0_), channel_id=1, source_target_pairs={{0,16},{16,0},{1,17},{17,1},{2,18},{18,2},{3,19},{19,3},{4,20},{20... | collective-permute-start | bytes 786440 | tf_op jit(solution)/shard_map/ppermute | solution.py:433
  49.4 4.8 %collective-permute-start.7 = (f32[8,1024]{1,0:T(8,128)S(1)}, f32[8,1024]{1,0:T(8,128)S(1)}, u32[]{:S(2)}, u32[]{:S(2)}) collective-permute-start(f32[8,1024]{1,0:T(8,128)S(1)} %get-tuple-element.66.s0), channel_id=1, source_target_pairs={{0,40},{8,32},{32,8},{40,0},{64,104},{72,96},{96,72},{104,64},{1,4... | collective-permute-start | bytes 98312 | tf_op jit(solution)/shard_map/ppermute | solution.py:436
  49.4 4.8 %collective-permute-start.6 = (f32[8,1024]{1,0:T(8,128)S(1)}, f32[8,1024]{1,0:T(8,128)S(1)}, u32[]{:S(2)}, u32[]{:S(2)}) collective-permute-start(f32[8,1024]{1,0:T(8,128)S(1)} %get-tuple-element.66.s0), channel_id=1, source_target_pairs={{0,32},{8,40},{32,0},{40,8},{64,96},{72,104},{96,64},{104,72},{1,3... | collective-permute-start | bytes 98312 | tf_op jit(solution)/shard_map/ppermute | solution.py:436
  50.5 4.4 %collective-permute-start.5 = (f32[8,1024]{1,0:T(8,128)S(1)}, f32[8,1024]{1,0:T(8,128)S(1)}, u32[]{:S(2)}, u32[]{:S(2)}) collective-permute-start(f32[8,1024]{1,0:T(8,128)S(1)} %get-tuple-element.66.s0), channel_id=1, source_target_pairs={{0,8},{8,0},{32,40},{40,32},{64,72},{72,64},{96,104},{104,96},{1,9... | collective-permute-start | bytes 98312 | tf_op jit(solution)/shard_map/ppermute | solution.py:436
  56.3 9.2 %collective-permute-start.9 = (bf16[1024,128]{1,0:T(8,128)(2,1)S(1)}, bf16[1024,128]{1,0:T(8,128)(2,1)S(1)}, u32[]{:S(2)}, u32[]{:S(2)}) collective-permute-start(bf16[1024,128]{1,0:T(8,128)(2,1)S(1)} %get-tuple-element.93.grad_attn.refs_6_), channel_id=1, source_target_pairs={{0,16},{16,0},{1,17},{17,1},{2,18},{18,2},{3,19},{19,3},{4,20},{20... | collective-permute-start | bytes 786440 | tf_op jit(solution)/shard_map/ppermute | solution.py:446
  58.1 5.0 %collective-permute-start.8 = (bf16[1024,128]{1,0:T(8,128)(2,1)S(1)}, bf16[1024,128]{1,0:T(8,128)(2,1)S(1)}, u32[]{:S(2)}, u32[]{:S(2)}) collective-permute-start(bf16[1024,128]{1,0:T(8,128)(2,1)S(1)} %collective-permute-done.3.refs_0_), channel_id=1, source_target_pairs={{0,4},{4,0},{1,5},{5,1},{2,6},{6,2},{3,7},{7,3},{8,12},{12,8},{9,1... | collective-permute-start | bytes 786440 | tf_op jit(solution)/shard_map/ppermute | solution.py:439
  63.0 3.6 %collective-permute-start.11 = (bf16[1024,128]{1,0:T(8,128)(2,1)S(1)}, bf16[1024,128]{1,0:T(8,128)(2,1)S(1)}, u32[]{:S(2)}, u32[]{:S(2)}) collective-permute-start(bf16[1024,128]{1,0:T(8,128)(2,1)S(1)} %get-tuple-element.93.grad_attn.refs_6_), channel_id=1, source_target_pairs={{0,4},{4,0},{1,5},{5,1},{2,6},{6,2},{3,7},{7,3},{8,12},{12,8},{9,1... | collective-permute-start | bytes 786440 | tf_op jit(solution)/shard_map/ppermute | solution.py:457
  65.5 4.1 %collective-permute-start.10 = (bf16[1024,128]{1,0:T(8,128)(2,1)S(1)}, bf16[1024,128]{1,0:T(8,128)(2,1)S(1)}, u32[]{:S(2)}, u32[]{:S(2)}) collective-permute-start(bf16[1024,128]{1,0:T(8,128)(2,1)S(1)} %collective-permute-done.9.refs_6_), channel_id=1, source_target_pairs={{0,4},{4,0},{1,5},{5,1},{2,6},{6,2},{3,7},{7,3},{8,12},{12,8},{9,1... | collective-permute-start | bytes 786440 | tf_op jit(solution)/shard_map/ppermute | solution.py:459
  69.6 21.6 %copy-start.5 = (f32[256,512]{1,0:T(8,128)S(1)}, f32[256,512]{1,0:T(8,128)}, u32[]{:S(2)}) copy-start(f32[256,512]{1,0:T(8,128)} %copy-done.4) | copy-start | bytes 1572868
  69.6 21.6 %copy-start.8 = (bf16[512,256]{1,0:T(8,128)(2,1)S(1)}, bf16[512,256]{1,0:T(8,128)(2,1)}, u32[]{:S(2)}) copy-start(bf16[512,256]{1,0:T(8,128)(2,1)} %copy-done.7) | copy-start | bytes 786436
  69.7 21.6 %copy-start.11 = (bf16[256,128]{1,0:T(8,128)(2,1)S(1)}, bf16[256,128]{1,0:T(8,128)(2,1)}, u32[]{:S(2)}) copy-start(bf16[256,128]{1,0:T(8,128)(2,1)} %copy-done.10) | copy-start | bytes 196612
  72.7 18.6 %copy-start.2 = (f32[256,2048]{1,0:T(8,128)S(1)}, f32[256,2048]{1,0:T(8,128)}, u32[]{:S(2)}) copy-start(f32[256,2048]{1,0:T(8,128)} %copy-done.1) | copy-start | bytes 6291460
